TPU v7x, 128 devices: a whole 4x4x4 slice. The times are simulated.
128 devices in a mesh: seq: 4 (over y_hi, core), mp: 32 (over x, y_lo, z).
Axes of the slice: x: 4, y: 4 (y_hi: 2, y_lo: 2; y = y_hi * 2 + y_lo), z: 4, core: 2. Of those that a mesh axis runs over, the one named last changes fastest.
Arguments:
- queries: bfloat16 [1024, 8192], P('seq', 'mp'), may hold values from -32 to 32
- new_kv: bfloat16 [2, 1024, 512], P(None, 'seq'), may hold values from -6 to 6
- cache_kv: bfloat16 [2, 8192, 512], P(None, 'seq'), may hold values from -6 to 6
- cached_len: int32 [1], replicated, may hold values from 4096 to 8192
- image_spans: int32 [3, 2], replicated, may hold values from 0 to 1024, as said below
- residual: bfloat16 [1024, 4096], P(('seq', 'mp')), may hold values from -4 to 4
- out_proj: bfloat16 [8192, 4096], P('mp'), may hold values from -0.0625 to 0.0625
- norm_gain: float32 [4096], replicated, may hold values from 0.5 to 1.5
- routes: int32 [1024, 8], P(('seq', 'mp')), may hold values from 0 to 63, all different within a row; in each aligned block of 8 rows (0 to 7, 8 to 15, ...) at most 2 rows name the same one
- gate_weights: float32 [1024, 8], P(('seq', 'mp')), may hold values from 0.05 to 1
- w_in: bfloat16 [64, 4096, 2, 1536], P('mp', None, None, 'seq'), may hold values from -0.09375 to 0.09375
- w_out: bfloat16 [64, 1536, 4096], P('mp', 'seq'), may hold values from -0.15625 to 0.15625
Outputs:
- mixed: bfloat16 [1024, 4096], P(('seq', 'mp'))
Inputs may be any that keep to these rules, and one draw needn't show every extreme that they name: `image_spans`: each row is an image span [start, end) of tract positions; rows are in increasing order, disjoint and nonempty. `routes`: each row names 8 different experts; within the rows of one device (aligned blocks of 8 rows) no expert is named more than 2 times.
All inputs are finite; a program needn't handle non-finite values.
Results may differ from a plain program's by a relative error of at most 0.025.
Values may be sent and summed in bfloat16 or wider, within the bound.
No kernel may reach another device: no remote copies, remote signals or barrier semaphores. Data moves between devices by JAX's collectives and lax.ppermute only.
A program may use at most 128 MiB of HBM per device.

v0:
```python
import math

import jax
import jax.numpy as jnp
from jax import lax
from jax.sharding import PartitionSpec as P

HEADS = 64
KV_HEADS = 4
HEAD_DIM = 128


block_width = 512
neg_large = -1e30


def span_lookup(image_spans, positions):
    inside = (positions[:, None] >= image_spans[None, :, 0]) & (
        positions[:, None] < image_spans[None, :, 1]
    )
    labels = jnp.arange(image_spans.shape[0], dtype=jnp.int32)
    return jnp.max(jnp.where(inside, labels[None, :], -1), axis=1)


def key_facts(first_row, length, context):
    cache_dev, tract_dev, cached, image_spans, head_dim = context
    global_index = first_row + jnp.arange(length, dtype=jnp.int32)
    stride = cache_dev + tract_dev
    shard_index = global_index // stride
    within = global_index % stride
    is_cache = within < cache_dev
    cache_ok = shard_index * cache_dev + within < cached
    tract_pos = shard_index * tract_dev + within - cache_dev
    key_span = span_lookup(image_spans, tract_pos)
    return (is_cache, cache_ok, tract_pos, key_span)


def unchanged(online):
    return online


def attend_block(running, query_rows, query_pos, query_span, packed, key_info, head_dim):
    is_cache, cache_ok, tract_pos, key_span = key_info
    later_ok = (tract_pos[None, :] <= query_pos[:, None]) | (
        key_span[None, :] == query_span[:, None]
    ) & (query_span[:, None] >= 0)
    visible = jnp.where(is_cache[None, :], cache_ok[None, :], later_ok)

    def update(online):
        maxima, totals, accumulated = online
        key_part = packed[:, :head_dim]
        value_part = packed[:, head_dim:]
        scores = lax.dot_general(
            query_rows, key_part, (((1,), (1,)), ((), ())), preferred_element_type=jnp.float32
        ) * (1.0 / math.sqrt(head_dim))
        new_max = jnp.maximum(maxima, jnp.max(jnp.where(visible, scores, neg_large), axis=1))
        weights = jnp.where(visible, jnp.exp(scores - new_max[:, None]), 0.0)
        factor = jnp.exp(maxima - new_max)
        totals = totals * factor + jnp.sum(weights, axis=1)
        accumulated = accumulated * factor[:, None] + jnp.dot(
            weights.astype(jnp.bfloat16), value_part, preferred_element_type=jnp.float32
        )
        return (new_max, totals, accumulated)

    return lax.cond(jnp.any(visible), update, unchanged, running)


def fold_keys(running, query_rows, query_pos, query_span, packed, context):
    head_dim = context[4]
    length = packed.shape[0]
    block_count = length // block_width
    blocks = packed.reshape(block_count, block_width, packed.shape[1])
    offsets = block_width * jnp.arange(block_count, dtype=jnp.int32)

    def scan_step(online, block_pair):
        key_info = key_facts(block_pair[1], block_width, context)
        return (
            attend_block(
                online, query_rows, query_pos, query_span, block_pair[0], key_info, head_dim
            ),
            None,
        )

    running, _ = lax.scan(scan_step, running, (blocks, offsets))
    return running


def expert_apply(arrived, w_in, w_out):
    hidden_dev = w_in.shape[3]
    shaped_in = w_in.reshape(w_in.shape[0], w_in.shape[1], 2 * hidden_dev)
    gate_up = jnp.einsum("sjcd,jdf->sjcf", arrived, shaped_in, preferred_element_type=jnp.float32)
    inner_act = (jax.nn.silu(gate_up[..., :hidden_dev]) * gate_up[..., hidden_dev:]).astype(
        jnp.bfloat16
    )
    return jnp.einsum(
        "sjcf,jfd->sjcd", inner_act, w_out, preferred_element_type=jnp.float32
    ).astype(jnp.bfloat16)


def local(
    queries,
    new_kv,
    cache_kv,
    cached_len,
    image_spans,
    residual,
    out_proj,
    norm_gain,
    routes,
    gate_weights,
    w_in,
    w_out,
):
    seq_count = lax.axis_size("seq")
    mp_count = lax.axis_size("mp")
    seq_index = lax.axis_index("seq")
    mp_index = lax.axis_index("mp")
    head_dim = HEAD_DIM
    tract_dev = queries.shape[0]
    heads_dev = queries.shape[1] // head_dim
    cache_dev = cache_kv.shape[1]
    kv_head = mp_index * heads_dev // (HEADS // KV_HEADS)
    cached = cached_len[0]
    cache_sel = lax.dynamic_slice_in_dim(cache_kv, kv_head * head_dim, head_dim, 2)
    new_sel = lax.dynamic_slice_in_dim(new_kv, kv_head * head_dim, head_dim, 2)
    joined = jnp.concatenate([cache_sel, new_sel], axis=1)
    packed = jnp.concatenate([joined[0], joined[1]], axis=1)
    context = (cache_dev, tract_dev, cached, image_spans, head_dim)
    local_order = jnp.tile(jnp.arange(tract_dev, dtype=jnp.int32), heads_dev)
    row_total = heads_dev * tract_dev
    initial = (
        jnp.full((row_total,), neg_large, jnp.float32),
        jnp.zeros((row_total,), jnp.float32),
        jnp.zeros((row_total, head_dim), jnp.float32),
    )
    query_rows = (
        queries.reshape(tract_dev, heads_dev, head_dim)
        .transpose(1, 0, 2)
        .reshape(row_total, head_dim)
    )
    query_pos = seq_index * tract_dev + local_order
    query_span = span_lookup(image_spans, query_pos)
    maxima, totals, accumulated = fold_keys(
        initial,
        query_rows,
        query_pos,
        query_span,
        lax.all_gather(packed, "seq", axis=0, tiled=True),
        context,
    )
    attended = accumulated / totals[:, None]
    attended = (
        attended.astype(jnp.bfloat16)
        .reshape(heads_dev, tract_dev, head_dim)
        .transpose(1, 0, 2)
        .reshape(tract_dev, heads_dev * head_dim)
    )
    tok_moe = residual.shape[0]
    projected = lax.psum_scatter(
        jnp.dot(attended, out_proj, preferred_element_type=jnp.float32).astype(jnp.bfloat16),
        "mp",
        scatter_dimension=0,
        tiled=True,
    ).astype(jnp.float32)
    stream = (residual.astype(jnp.float32) + projected).astype(jnp.bfloat16)
    stream_f = lax.optimization_barrier(stream).astype(jnp.float32)
    normed = (
        stream_f
        * lax.rsqrt(jnp.mean(stream_f * stream_f, axis=1, keepdims=True) + 1e-06)
        * norm_gain
    ).astype(jnp.bfloat16)
    gate_share = gate_weights / jnp.sum(gate_weights, axis=1, keepdims=True)
    experts_dev = w_in.shape[0]
    experts_all = experts_dev * mp_count
    top_count = routes.shape[1]
    capacity = max(2, tok_moe * top_count * 3 // (2 * experts_all))
    flat_routes = routes.reshape(-1)
    onehot = (flat_routes[:, None] == jnp.arange(experts_all, dtype=jnp.int32)[None, :]).astype(
        jnp.int32
    )
    slot_rank = jnp.sum((jnp.cumsum(onehot, axis=0) - onehot) * onehot, axis=1)
    target = flat_routes * capacity + slot_rank
    placement = (
        target[:, None] == jnp.arange(experts_all * capacity, dtype=jnp.int32)[None, :]
    ).astype(jnp.float32)
    placement = placement.reshape(tok_moe, top_count, experts_all * capacity)
    selector = jnp.sum(placement, axis=1).astype(jnp.bfloat16)
    combiner = jnp.sum(placement * gate_share[:, :, None], axis=1)
    outgoing = jnp.einsum("ts,td->sd", selector, normed, preferred_element_type=jnp.float32).astype(
        jnp.bfloat16
    )
    width = outgoing.shape[1]
    shaped = outgoing.reshape(1, mp_count, experts_dev, capacity, width)
    copies = jnp.broadcast_to(shaped, (seq_count, mp_count, experts_dev, capacity, width))
    flat_copies = copies.reshape(seq_count * mp_count, experts_dev, capacity, width)
    produced = expert_apply(
        lax.all_to_all(flat_copies, ("seq", "mp"), split_axis=0, concat_axis=0, tiled=True),
        w_in,
        w_out,
    )
    returned = lax.all_to_all(produced, ("seq", "mp"), split_axis=0, concat_axis=0, tiled=True)
    returned = returned.reshape(seq_count, mp_count * experts_dev * capacity, width)
    summed = jnp.sum(returned, axis=0, dtype=jnp.float32)
    combined = jnp.dot(
        combiner, summed, precision=lax.Precision.HIGHEST, preferred_element_type=jnp.float32
    )
    return (stream_f + combined).astype(jnp.bfloat16)


def solution(mesh):
    in_specs = (
        P("seq", "mp"),
        P(None, "seq", None),
        P(None, "seq", None),
        P(),
        P(),
        P(("seq", "mp"), None),
        P("mp", None),
        P(),
        P(("seq", "mp"), None),
        P(("seq", "mp"), None),
        P("mp", None, None, "seq"),
        P("mp", "seq", None),
    )
    out_specs = P(("seq", "mp"), None)
    return jax.shard_map(local, mesh=mesh, in_specs=in_specs, out_specs=out_specs, check_vma=False)
```

profile of v0, /device:TPU:0, one launch (start us, length us, event | category | flops | bytes accessed | tf_op | source)
XLA Modules:
  0.0 516.9 jit_solution(2670055839934693706)
XLA Ops:
  6.5 1.1 constant_dynamic-slice_fusion
  7.6 1.3 constant_dynamic-slice_fusion.1
  9.0 1.2 pad_maximum_fusion
  10.5 43.9 %all-gather.2.cloned.1.call-done = bf16[9216,256]{1,0:T(8,128)(2,1)} async-done(((bf16[2304,256]{1,0:T(8,128)(2,1)}), bf16[9216,256]{1,0:T(8,128)(2,1)}) %all-gather.2.cloned.1.call-update) | async-done | bytes 4718608 | tf_op jit(solution)/shard_map/all_gather | solution.py:148
  54.4 118.0 %while.17 = (s32[]{:T(128)}, f32[512]{0:T(512)S(1)}, f32[512]{0:T(512)S(1)}, f32[512,128]{1,0:T(8,128)S(1)}, s32[18]{0:T(128)S(1)}, /*index=5*/s32[]{:T(128)}, s...) while((s32[]{:T(128)}, f32[512]{0:T(512)S(1)}, ...), condition=%wide.region_8.9_spmd.clone, body=%wide.region_1.8_spmd.clone.sunk | while | flops 138310656 | bytes 5694815 | solution.py:84
  55.7 1.3 add_compare_fusion.2
  57.8 1.3 fusion.57
  59.7 2.1 conditional.3
  63.2 1.3 add_compare_fusion.2
  65.3 1.3 fusion.57
  67.2 2.2 conditional.3
  70.7 1.3 add_compare_fusion.2
  72.8 1.3 fusion.57
  74.7 2.1 conditional.3
  78.2 1.3 add_compare_fusion.2
  80.3 1.3 fusion.57
  82.2 2.1 conditional.3
  85.7 1.3 add_compare_fusion.2
  87.8 1.3 fusion.57
  89.8 2.1 conditional.3
  93.2 1.3 add_compare_fusion.2
  95.3 1.3 fusion.57
  97.3 2.1 conditional.3
  100.7 1.3 add_compare_fusion.2
  102.8 1.3 fusion.57
  104.8 2.1 conditional.3
  108.2 1.3 add_compare_fusion.2
  110.3 1.3 fusion.57
  112.3 2.1 conditional.3
  115.7 1.3 add_compare_fusion.2
  117.8 1.3 fusion.57
  119.8 2.1 conditional.3
  123.2 1.3 add_compare_fusion.2
  125.3 1.3 fusion.57
  127.3 2.1 conditional.3
  130.8 1.3 add_compare_fusion.2
  132.8 1.3 fusion.57
  136.1 1.3 add_compare_fusion.2
  138.2 1.3 fusion.57
  141.5 1.3 add_compare_fusion.2
  143.6 1.3 fusion.57
  146.9 1.3 add_compare_fusion.2
  148.9 1.3 fusion.57
  152.2 1.3 add_compare_fusion.2
  154.3 1.3 fusion.57
  157.6 1.3 add_compare_fusion.2
  159.7 1.3 fusion.57
  163.0 1.3 add_compare_fusion.2
  165.0 1.3 fusion.57
  168.3 1.3 add_compare_fusion.2
  170.4 1.3 fusion.57
  172.7 2.1 convolution_convert_fusion
  175.7 166.3 %reduce-scatter.2.cloned.1.call-done = bf16[8,4096]{1,0:T(8,128)(2,1)} async-done(((bf16[256,4096]{1,0:T(8,128)(2,1)}), bf16[8,4096]{1,0:T(8,128)(2,1)}) %reduce-scatter.2.cloned.1.call-update) | async-done | bytes 65552 | tf_op jit(solution)/shard_map/reduce_scatter | solution.py:159
  344.2 6.2 %broadcast_in_dim.101 = bf16[4,32,2,2,4096]{4,3,2,1,0:T(2,128)(2,1)} broadcast(bf16[32,2,2,4096]{3,2,1,0:T(2,128)(2,1)S(1)} %broadcast_in_dim.100), dimensions={1,2,3,4} | broadcast | bytes 5242880 | tf_op jit(solution)/shard_map/broadcast_in_dim | solution.py:194
  350.4 6.0 %all-to-all-start = ((bf16[128,2,2,4096]{3,2,1,0:T(2,128)(2,1)}), bf16[128,2,2,4096]{3,2,1,0:T(2,128)(2,1)}, u32[]{:S(2)}, u32[]{:S(2)}) async-start(bf16[128,2,2,4096]{3,2,1,0:T(2,128)(2,1)} %bitcast.70), calls=%async_computation.1 | async-start | bytes 8388608 | tf_op jit(solution)/shard_map/all_to_all | solution.py:197
  356.4 27.7 %reshape.136 = bf16[2,4096,768,1]{2,1,0,3:T(8,128)(2,1)} reshape(bf16[2,4096,2,384]{3,2,1,0:T(2,128)(2,1)} %param.26) | data formatting | bytes 25165824 | tf_op jit(solution)/shard_map/reshape | solution.py:90
  384.1 24.9 %all-to-all-done = bf16[128,2,2,4096]{3,2,1,0:T(2,128)(2,1)} async-done(((bf16[128,2,2,4096]{3,2,1,0:T(2,128)(2,1)}), bf16[128,2,2,4096]{3,2,1,0:T(2,128)(2,1)}, u32[]{:S(2)}, u32[]{:S(2)}) %all-to-all-start) | async-done | bytes 4194336 | tf_op jit(solution)/shard_map/all_to_all | solution.py:197
  409.0 12.0 %fusion.28 = f32[128,2,2,768]{3,0,2,1:T(8,128)S(1)} fusion(bf16[2,4096,768,1]{2,1,0,3:T(8,128)(2,1)} %reshape.136, bf16[128,2,2,4096]{3,2,1,0:T(2,128)(2,1)} %all-to-all-done), kind=kOutput, calls=%fused_computation.45 | convolution fusion | flops 3221225472 | bytes 18350080 | tf_op jit(solution)/shard_map/sjcd,jdf->sjcf/dot_general | solution.py:91
  421.0 7.1 %fusion.23 = bf16[128,2,2,4096]{3,0,2,1:T(8,128)(2,1)} fusion(bf16[2,384,4096]{2,1,0:T(8,128)(2,1)} %param.27, f32[128,2,2,768]{3,0,2,1:T(8,128)S(1)} %fusion.28), kind=kOutput, calls=%fused_computation.39 | convolution fusion | flops 1613889536 | bytes 12058624 | tf_op jit(solution)/shard_map/sjcf,jfd->sjcd/dot_general | solution.py:95
  428.0 6.6 %copy.29 = bf16[128,2,2,4096]{3,2,1,0:T(2,128)(2,1)S(1)} copy(bf16[128,2,2,4096]{3,0,2,1:T(8,128)(2,1)} %fusion.23) | data formatting | bytes 8388608 | tf_op jit(solution)/shard_map/convert_element_type | solution.py:97
  434.6 58.9 %all_to_all.10 = bf16[128,2,2,4096]{3,2,1,0:T(2,128)(2,1)} all-to-all(bf16[128,2,2,4096]{3,2,1,0:T(2,128)(2,1)S(1)} %copy.29), channel_id=1, replica_groups=mesh['seq'=4,'mp'=32] {'seq','mp'}, dimensions={0} | all-to-all | bytes 8388608 | tf_op jit(solution)/shard_map/all_to_all | solution.py:201
  493.5 7.6 %reshape.135 = f32[4,128,4096]{2,1,0:T(8,128)} reshape(bf16[128,2,2,4096]{3,2,1,0:T(2,128)(2,1)} %all_to_all.10) | data formatting | bytes 12582912 | tf_op jit(solution)/shard_map/convert_element_type | solution.py:203
  501.1 5.7 %reduce_sum.72 = f32[128,4096]{1,0:T(8,128)} reduce(f32[4,128,4096]{2,1,0:T(8,128)} %reshape.135, f32[]{:T(128)} %constant.125.clone.1), dimensions={0}, to_apply=%region_16.17 | reduce | flops 1572864 | bytes 10485764 | tf_op jit(solution)/shard_map/reduce_sum | solution.py:203
  506.8 3.3 fusion.26
  (250 shorter events, 61.7 us)
Async XLA Ops:
  6.5 166.1 %copy-start = (bf16[256,4096]{1,0:T(8,128)(2,1)S(1)}, bf16[256,4096]{1,0:T(8,128)(2,1)}, u32[]{:S(2)}) copy-start(bf16[256,4096]{1,0:T(8,128)(2,1)} %param.22) | copy-start | bytes 6291460
  6.5 47.8 %all-gather.2.cloned.1.call-start = ((), (), s32[]{:S(2)}) async-start(), calls=%async_computation.3 | async-start | bytes 5898240 | tf_op jit(solution)/shard_map/all_gather | solution.py:148
  9.0 1.3 copy-start.4
  9.0 1.4 copy-start.2
  10.2 331.8 %reduce-scatter.2.cloned.1.call-start = ((), (), s32[]{:S(2)}) async-start(), calls=%async_computation.4 | async-start | bytes 2162688 | tf_op jit(solution)/shard_map/reduce_scatter | solution.py:159
  172.7 2.2 copy-start.6
  172.7 2.2 copy-start.7
  172.7 169.3 %copy-start.3 = (bf16[8,4096]{1,0:T(8,128)(2,1)S(1)}, bf16[8,4096]{1,0:T(8,128)(2,1)}, u32[]{:S(2)}) copy-start(bf16[8,4096]{1,0:T(8,128)(2,1)} %param.21) | copy-start | bytes 196612
  172.7 170.3 %copy-start.5 = (f32[4096]{0:T(1024)S(1)}, f32[4096]{0:T(1024)}, u32[]{:S(2)}) copy-start(f32[4096]{0:T(1024)} %param.23) | copy-start | bytes 49156
  350.4 58.6 %all-to-all-start = ((bf16[128,2,2,4096]{3,2,1,0:T(2,128)(2,1)}), bf16[128,2,2,4096]{3,2,1,0:T(2,128)(2,1)}, u32[]{:S(2)}, u32[]{:S(2)}) async-start(bf16[128,2,2,4096]{3,2,1,0:T(2,128)(2,1)} %bitcast.70), calls=%async_computation.1 | async-start | bytes 8388608 | tf_op jit(solution)/shard_map/all_to_all | solution.py:197
  501.1 9.0 %copy-start.1 = (bf16[256,4096]{1,0:T(8,128)(2,1)S(1)}, bf16[256,4096]{1,0:T(8,128)(2,1)}, u32[]{:S(2)}) copy-start(bf16[256,4096]{1,0:T(8,128)(2,1)} %param.22) | copy-start | bytes 6291460
Sparse Core Ops, SparseCore 0:
  10.3 43.9 all-gather.1
  174.9 166.9 reduce-scatter.1
where the time goes:
time: 526 us; the launch traced here: 517 us
  waiting for transfers between devices  235 us (45%)
  other arithmetic  83.1 us (16%)
  local copies, waits for them, and re-layouts  73.1 us (14%)
  blocking collectives  58.9 us (11%)
  matrix products  33.4 us (6%)
  loops' own time  13.7 us (3%)
  between operations  13.6 us (3%)
  starting transfers between devices  6.05 us (1%)
    reduce_scatter x1, waiting for transfers between devices, local(): lax.psum_scatter(jnp.dot(attended, out_proj, preferred_element_type=jnp.f...  166 us
    all_to_all x1, blocking collectives, local(): lax.all_to_all(produced, ('seq', 'mp'), split_axis=0, concat_axis=0, tile...  58.9 us
    all_gather x1, waiting for transfers between devices, local(): lax.all_gather(packed, 'seq', axis=0, tiled=True)  43.9 us
    reshape x1, local copies, waits for them, and re-layouts, expert_apply(): shaped_in = w_in.reshape(w_in.shape[0], w_in.shape[1], 2 * hidden_dev)  27.7 us
    all_to_all x1, waiting for transfers between devices, local(): lax.all_to_all(flat_copies, ('seq', 'mp'), split_axis=0, concat_axis=0, t...  24.9 us
    lt x18, other arithmetic, key_facts(): cache_ok = shard_index * cache_dev + within < cached  23.4 us
    reduce_or x18, other arithmetic, attend_block(): return lax.cond(jnp.any(visible), update, unchanged, running)  22.9 us
    another operation x1, loops' own time, fold_keys(): running, _ = lax.scan(scan_step, running, (blocks, offsets))  13.2 us
  transfers between devices with their start and end apart: 3, of which 3 were waited for; matrix products, arithmetic and copies ran while one was open for 6% of the time, Pallas kernels for 0%

commit v1 on v0

v1 whole, which is shorter than its diff:
```python
import math

import jax
import jax.numpy as jnp
from jax import lax
from jax.experimental import pallas as pl
from jax.experimental.pallas import tpu as pltpu
from jax.sharding import Mesh, PartitionSpec as P

HEAD_DIM = 128
SEQ = ("yh", "core")
MP = ("x", "yl", "z")
NEG = -1e30
BF = jnp.bfloat16
F32 = jnp.float32
ANY_LAST = (((1,), (1,)), ((), ()))


def attn_kernel(info, q_ref, kc_ref, vc_ref, kn_ref, vn_ref, out_ref, s_ref):
    rows = q_ref.shape[0]
    cache_rows = kc_ref.shape[1]
    chunk = kn_ref.shape[1]
    chunks = cache_rows // chunk
    coef = math.log2(math.e) / math.sqrt(HEAD_DIM)
    valid = info[1]
    key_pos = info[2] + lax.broadcasted_iota(jnp.int32, (1, chunk), 1)
    pos = info[3] + lax.broadcasted_iota(jnp.int32, (rows, 1), 0)
    limit = pos
    for a in range(3):
        start, end = info[4 + 2 * a], info[5 + 2 * a]
        limit = jnp.where((pos >= start) & (pos < end), jnp.maximum(limit, end - 1), limit)
    tract_ok = key_pos <= limit
    lane = lax.broadcasted_iota(jnp.int32, (rows, 128), 1)
    stats = jnp.zeros((rows, 128), F32)
    column = lax.broadcasted_iota(jnp.int32, (1, chunk), 1)
    for h in range(2):
        q = q_ref[:, h * HEAD_DIM : (h + 1) * HEAD_DIM]
        top = None
        for c in range(chunks + 1):
            if c < chunks:
                k = kc_ref[0, c * chunk : (c + 1) * chunk, :]
                s = lax.dot_general(q, k, ANY_LAST, preferred_element_type=F32)
                s = s + jnp.where(column < valid - c * chunk, 0.0, NEG)
            else:
                s = lax.dot_general(q, kn_ref[0], ANY_LAST, preferred_element_type=F32)
                s = jnp.where(tract_ok, s, NEG)
            s_ref[h, :, c * chunk : (c + 1) * chunk] = s
            top = s if top is None else jnp.maximum(top, s)
        m = jnp.max(top, axis=1, keepdims=True) * coef
        total = None
        acc = None
        for c in range(chunks + 1):
            p = jnp.exp2(s_ref[h, :, c * chunk : (c + 1) * chunk] * coef - m)
            total = p if total is None else total + p
            v = vc_ref[0, c * chunk : (c + 1) * chunk, :] if c < chunks else vn_ref[0]
            part = jnp.dot(p.astype(BF), v, preferred_element_type=F32)
            acc = part if acc is None else acc + part
        total = jnp.sum(total, axis=1, keepdims=True)
        out_ref[0:rows, h * HEAD_DIM : (h + 1) * HEAD_DIM] = (acc / total).astype(BF)
        level = m + jnp.log2(total)
        for part in range(3):
            piece = level.astype(BF).astype(F32)
            level = level - piece
            stats = jnp.where(lane == 3 * h + part, piece, stats)
    out_ref[rows : rows + 16, :] = stats.T[0:16, :].astype(BF)


def attend(info, q, cache_kv, new_kv):
    rows = q.shape[0]
    cache_rows, new_rows = cache_kv.shape[1], new_kv.shape[1]
    keys = cache_rows + new_rows
    return pl.pallas_call(
        attn_kernel,
        grid_spec=pltpu.PrefetchScalarGridSpec(
            num_scalar_prefetch=1,
            grid=(1,),
            in_specs=[
                pl.BlockSpec((rows, 2 * HEAD_DIM), lambda i, t: (0, 0)),
                pl.BlockSpec((1, cache_rows, HEAD_DIM), lambda i, t: (0, 0, t[0])),
                pl.BlockSpec((1, cache_rows, HEAD_DIM), lambda i, t: (1, 0, t[0])),
                pl.BlockSpec((1, new_rows, HEAD_DIM), lambda i, t: (0, 0, t[0])),
                pl.BlockSpec((1, new_rows, HEAD_DIM), lambda i, t: (1, 0, t[0])),
            ],
            out_specs=pl.BlockSpec((rows + 16, 2 * HEAD_DIM), lambda i, t: (0, 0)),
            scratch_shapes=[pltpu.VMEM((2, rows, keys), F32)],
        ),
        out_shape=jax.ShapeDtypeStruct((rows + 16, 2 * HEAD_DIM), BF),
        compiler_params=pltpu.CompilerParams(vmem_limit_bytes=32 << 20),
        cost_estimate=pl.CostEstimate(
            flops=8 * rows * keys * HEAD_DIM,
            bytes_accessed=4 * keys * HEAD_DIM,
            transcendentals=2 * rows * keys,
        ),
        name="attend",
    )(info, q, cache_kv, cache_kv, new_kv, new_kv)


def merge_kernel(a_ref, b_ref, c_ref, d_ref, out_ref):
    parts = (a_ref, b_ref, c_ref, d_ref)
    rows = out_ref.shape[0]
    pad = jnp.zeros((112, rows), F32)
    stats = [
        jnp.concatenate([p[rows : rows + 16, :].astype(F32), pad], axis=0).T for p in parts
    ]
    for h in range(2):
        cols = slice(h * HEAD_DIM, (h + 1) * HEAD_DIM)
        levels = [
            t[:, 3 * h : 3 * h + 1] + t[:, 3 * h + 1 : 3 * h + 2] + t[:, 3 * h + 2 : 3 * h + 3]
            for t in stats
        ]
        best = jnp.maximum(
            jnp.maximum(levels[0], levels[1]), jnp.maximum(levels[2], levels[3])
        )
        weights = [jnp.exp2(v - best) for v in levels]
        total = weights[0] + weights[1] + weights[2] + weights[3]
        acc = None
        for w, p in zip(weights, parts):
            term = p[0:rows, cols].astype(F32) * w
            acc = term if acc is None else acc + term
        out_ref[:, cols] = (acc / total).astype(BF)


def merge(parts):
    rows = parts[0].shape[0] - 16
    return pl.pallas_call(
        merge_kernel,
        out_shape=jax.ShapeDtypeStruct((rows, 2 * HEAD_DIM), BF),
        cost_estimate=pl.CostEstimate(flops=1 << 20, bytes_accessed=5 << 17, transcendentals=0),
        name="merge",
    )(*parts)


def project_kernel(*refs):
    out_ref = refs[8]
    acc = None
    for a, w in zip(refs[:4], refs[4:8]):
        part = jnp.dot(a[...], w[...], preferred_element_type=F32)
        acc = part if acc is None else acc + part
    out_ref[...] = acc.astype(BF)


def project(parts, weights):
    rows, depth = parts[0].shape
    width = weights[0].shape[1]
    step = 256
    return pl.pallas_call(
        project_kernel,
        grid=(width // step,),
        in_specs=[pl.BlockSpec((rows, depth), lambda i: (0, 0))] * 4
        + [pl.BlockSpec((depth, step), lambda i: (0, i))] * 4,
        out_specs=pl.BlockSpec((rows, step), lambda i: (0, i)),
        out_shape=jax.ShapeDtypeStruct((rows, width), BF),
        cost_estimate=pl.CostEstimate(
            flops=8 * rows * depth * width, bytes_accessed=8 * depth * width, transcendentals=0
        ),
        name="project",
    )(*parts, *weights)


def expert_kernel(
    own_ref, other_ref, gain_ref, win_ref, wout_ref, kept_ref, sent_ref, x_ref, hidden_ref
):
    step = pl.program_id(0)
    groups, chunks, _, chunk = own_ref.shape
    half = groups * 8
    ff = wout_ref.shape[1]
    width = chunks * chunk

    @pl.when(step == 0)
    def _():
        for side, ref in enumerate((own_ref, other_ref)):

            @pl.loop(0, groups // 2)
            def _(pair):
                normed = []
                for j in range(2):
                    v = [ref[2 * pair + j, z].astype(F32) for z in range(chunks)]
                    square = v[0] * v[0]
                    for z in range(1, chunks):
                        square = square + v[z] * v[z]
                    scale = lax.rsqrt(
                        jnp.sum(square, axis=1, keepdims=True) * (1.0 / width) + 1e-6
                    )
                    normed.append([v[z] * scale * gain_ref[z : z + 1, :] for z in range(chunks)])
                at = pl.multiple_of(side * half + pair * 16, 16)
                for e in range(2):
                    for z in range(chunks):
                        x_ref[e, z, pl.ds(at, 16), :] = jnp.concatenate(
                            [normed[j][z][8 * e : 8 * e + 8] for j in range(2)], axis=0
                        ).astype(BF)

    @pl.when(step < 2 * chunks)
    def _():
        e, z = step // chunks, step % chunks
        part = jnp.dot(x_ref[e, z], win_ref[0], preferred_element_type=F32)

        @pl.when(z == 0)
        def _():
            hidden_ref[e] = part

        @pl.when(z > 0)
        def _():
            hidden_ref[e] = hidden_ref[e] + part

    @pl.when(step >= 2 * chunks)
    def _():
        produced = []
        for e in range(2):
            gate, up = hidden_ref[e, :, :ff], hidden_ref[e, :, ff:]
            act = (gate / (1.0 + jnp.exp(-gate)) * up).astype(BF)
            produced.append(jnp.dot(act, wout_ref[e], preferred_element_type=F32))
        for side, ref in enumerate((kept_ref, sent_ref)):
            both = [
                p[side * half : (side + 1) * half].reshape(groups, 8, chunk) for p in produced
            ]
            ref[:, 0] = jnp.concatenate(both, axis=1).astype(BF)


def experts(own, other, gain, w_in, w_out):
    groups, chunks, _, chunk = own.shape
    ff = w_out.shape[1]
    last = 2 * chunks - 1
    shape = jax.ShapeDtypeStruct(own.shape, BF)
    rows = 2 * groups * 8

    def out_map(i):
        return (0, jnp.maximum(i - last - 1, 0), 0, 0)

    return pl.pallas_call(
        expert_kernel,
        grid=(3 * chunks,),
        in_specs=[
            pl.BlockSpec(own.shape, lambda i: (0, 0, 0, 0)),
            pl.BlockSpec(own.shape, lambda i: (0, 0, 0, 0)),
            pl.BlockSpec((chunks, chunk), lambda i: (0, 0)),
            pl.BlockSpec(
                (1, chunk, 2 * ff),
                lambda i: (jnp.minimum(i, last) // chunks, jnp.minimum(i, last) % chunks, 0),
            ),
            pl.BlockSpec((2, ff, chunk), lambda i: (0, 0, jnp.maximum(i - last - 1, 0))),
        ],
        out_specs=[
            pl.BlockSpec((groups, 1, 16, chunk), out_map),
            pl.BlockSpec((groups, 1, 16, chunk), out_map),
        ],
        out_shape=[shape, shape],
        scratch_shapes=[
            pltpu.VMEM((2, chunks, rows, chunk), BF),
            pltpu.VMEM((2, rows, 2 * ff), F32),
        ],
        compiler_params=pltpu.CompilerParams(vmem_limit_bytes=48 << 20),
        cost_estimate=pl.CostEstimate(
            flops=12 * rows * chunks * chunk * ff,
            bytes_accessed=12 * chunks * chunk * ff,
            transcendentals=2 * rows * ff,
        ),
        name="experts",
    )(own, other, gain.reshape(chunks, chunk), w_in, w_out)


def swap(v, axes, bit):
    count = 4 if len(axes) == 2 else 2
    return lax.ppermute(v, axes, [(i, i ^ bit) for i in range(count)])


def shift(v, d):
    return lax.ppermute(v, "z", [(i, (i + d) % 4) for i in range(4)])


def local(
    queries,
    new_kv,
    cache_kv,
    cached_len,
    image_spans,
    residual,
    out_proj,
    norm_gain,
    routes,
    gate_weights,
    w_in,
    w_out,
):
    seq = lax.axis_index(SEQ)
    z_at = lax.axis_index("z")
    tract = queries.shape[0]
    cache = cache_kv.shape[1]
    tok = residual.shape[0]
    width = residual.shape[1]
    quarter = width // 4

    query_parts = [queries] + [swap(queries, SEQ, d) for d in (1, 2, 3)]

    def column_block(z):
        return lax.dynamic_slice_in_dim(out_proj, (z % 4) * quarter, quarter, 1)

    proj_parts = [column_block(z_at)] + [shift(column_block(z_at + d), d) for d in (1, 2, 3)]

    residual_part = lax.all_to_all(
        residual.reshape(tok, 4, quarter).transpose(1, 0, 2),
        "z",
        split_axis=0,
        concat_axis=0,
        tiled=True,
    ).reshape(4 * tok, quarter)

    gate_share = gate_weights / jnp.sum(gate_weights, axis=1, keepdims=True)
    top = routes.shape[1]
    table = lax.all_gather(
        jnp.concatenate([routes.astype(F32), gate_share], axis=1), "z", axis=0, tiled=True
    )
    named = table[:, :top].astype(jnp.int32).reshape(4, tok, top)
    shares = table[:, top:]
    same = named[:, :, :, None, None] == named[:, None, None, :, :]
    earlier = (
        jnp.arange(tok)[:, None] > jnp.arange(tok)[None, :]
    )[None, :, None, :, None]
    rank = jnp.sum((same & earlier).astype(jnp.int32), axis=(3, 4))
    block = jnp.arange(4, dtype=jnp.int32)[:, None, None]
    slot = ((named // 2) * 16 + (named % 2) * 8 + block * 2 + rank).reshape(4 * tok, top)
    slots = 32 * 16
    placement = slot[:, :, None] == jnp.arange(slots, dtype=jnp.int32)[None, None, :]
    selector = jnp.sum(placement.astype(F32), axis=1).astype(BF)
    combiner = jnp.sum(jnp.where(placement, shares[:, :, None], 0.0), axis=1)
    coarse = combiner.astype(BF)
    fine = (combiner - coarse.astype(F32)).astype(BF)

    valid = jnp.clip(cached_len[0] - seq * cache, 0, cache)
    answers = []
    for d in range(4):
        info = jnp.concatenate(
            [
                jnp.stack(
                    [lax.axis_index("x"), valid, seq * tract, (seq ^ d) * tract]
                ).astype(jnp.int32),
                image_spans.reshape(-1),
            ]
        )
        part = attend(info, query_parts[d], cache_kv, new_kv)
        answers.append(swap(part, SEQ, d) if d else part)
    attended = merge(answers)

    head_parts = [attended] + [shift(attended, d) for d in (1, 2, 3)]
    partial = project(head_parts, proj_parts)
    arrived = lax.all_to_all(
        partial.reshape(8, 4 * tok, quarter), ("x", "yl"), split_axis=0, concat_axis=0, tiled=True
    )
    stream = (
        residual_part.astype(F32) + jnp.sum(arrived.astype(F32), axis=0)
    ).astype(BF)

    twice = jnp.concatenate([selector, selector], axis=1)
    outgoing = lax.dot_general(
        twice, stream, (((0,), (0,)), ((), ())), preferred_element_type=F32
    ).astype(BF)
    own = lax.all_to_all(
        outgoing.reshape(64, 16, quarter), ("yh",) + MP, split_axis=0, concat_axis=0, tiled=True
    )
    other = swap(own, ("core",), 1)
    shaped = (16, 4, 16, quarter)
    joined = w_in.reshape(w_in.shape[0], w_in.shape[1], 2 * w_in.shape[3])
    kept, sent = experts(own.reshape(shaped), other.reshape(shaped), norm_gain, joined, w_out)
    got = swap(sent, ("core",), 1)
    summed = (kept.astype(F32) + got.astype(F32)).astype(BF)
    returned = lax.all_to_all(
        summed.reshape(64, 16, quarter), ("yh",) + MP, split_axis=0, concat_axis=0, tiled=True
    ).reshape(2 * slots, quarter)

    combined = jnp.dot(
        jnp.concatenate([coarse, coarse], axis=1), returned, preferred_element_type=F32
    ) + jnp.dot(jnp.concatenate([fine, fine], axis=1), returned, preferred_element_type=F32)
    mixed = (stream.astype(F32) + combined).astype(BF)
    return (
        lax.all_to_all(
            mixed.reshape(4, tok, quarter), "z", split_axis=0, concat_axis=0, tiled=True
        )
        .transpose(1, 0, 2)
        .reshape(tok, width)
    )


def solution(mesh):
    fine = Mesh(mesh.devices.reshape(2, 2, 4, 2, 4), SEQ + MP)
    in_specs = (
        P(SEQ, MP),
        P(None, SEQ, None),
        P(None, SEQ, None),
        P(),
        P(),
        P(SEQ + MP, None),
        P(MP, None),
        P(),
        P(SEQ + MP, None),
        P(SEQ + MP, None),
        P(MP, None, None, SEQ),
        P(MP, SEQ, None),
    )
    return jax.shard_map(
        local, mesh=fine, in_specs=in_specs, out_specs=P(SEQ + MP, None), check_vma=False
    )
```

time: 526 us -> 224 us (0.43); the launches traced: 517 us -> 221 us
  waiting for transfers between devices: 235 us -> 50.4 us
  other arithmetic: 83.1 us -> 8.14 us
  Pallas kernels: 0 us -> 37.3 us
  local copies, waits for them, and re-layouts: 73.1 us -> 40.6 us
  matrix products: 33.4 us -> 1.66 us
  starting transfers between devices: 6.05 us -> 32.1 us
  loops' own time: 13.7 us -> 0 us
  between operations: 13.6 us -> 0.89 us
  blocking collectives: 58.9 us -> 49.6 us
    reduce_scatter x1 -> x0, waiting for transfers between devices: 166 us -> none  [local(): lax.psum_scatter(jnp.dot(attended, out_proj, preferred_element_type=jnp.f...]
    all_gather x1 -> x0, waiting for transfers between devices: 43.9 us -> none  [local(): lax.all_gather(packed, 'seq', axis=0, tiled=True)]
    pallas_call x0 -> x7, Pallas kernels: none -> 37.3 us  [the longest x1 18.6 us: experts(): pl.pallas_call(expert_kernel, grid=(3 * chunks,), in_specs=[pl.BlockSpec(...]
    lt x36 -> x0, other arithmetic: 35 us -> none  [the longest x18 23.4 us: key_facts(): cache_ok = shard_index * cache_dev + within < cached]
    dot_general x25 -> x3, matrix products: 33.4 us -> 1.66 us  [the longest x1 0.72 us: local(): lax.dot_general(twice, stream, (((0,), (0,)), ((), ())), preferred_elemen...]
    reduce_or x18 -> x0, other arithmetic: 22.9 us -> none  [attend_block(): return lax.cond(jnp.any(visible), update, unchanged, running)]
    all_to_all x1 -> x2, blocking collectives: 58.9 us -> 37.5 us  [the longest x1 29.2 us: local(): lax.all_to_all(outgoing.reshape(64, 16, quarter), ('yh',) + MP, split_axi...]
    ppermute x0 -> x14, starting transfers between devices: none -> 17.8 us  [the longest x6 10 us: shift(): return lax.ppermute(v, 'z', [(i, (i + d) % 4) for i in range(4)])]
  transfers between devices with their start and end apart: 3 -> 17, of which waited for: 3 -> 7; matrix products, arithmetic and copies ran while one was open for 6% -> 17% of each run, Pallas kernels for 0% -> 7%
where the time goes in v1:
time: 224 us; the launch traced here: 221 us
  waiting for transfers between devices  50.4 us (22%)
  blocking collectives  49.6 us (22%)
  local copies, waits for them, and re-layouts  40.6 us (18%)
  Pallas kernels  37.3 us (17%)
  starting transfers between devices  32.1 us (14%)
  other arithmetic  8.14 us (4%)
    all_to_all x1, waiting for transfers between devices, local(): lax.all_to_all(summed.reshape(64, 16, quarter), ('yh',) + MP, split_axis=...  29.9 us
    all_to_all x1, blocking collectives, local(): lax.all_to_all(outgoing.reshape(64, 16, quarter), ('yh',) + MP, split_axi...  29.2 us
    reshape x1, local copies, waits for them, and re-layouts, local(): joined = w_in.reshape(w_in.shape[0], w_in.shape[1], 2 * w_in.shape[3])  28.1 us
    pallas_call x1, Pallas kernels, experts(): pl.pallas_call(expert_kernel, grid=(3 * chunks,), in_specs=[pl.BlockSpec(...  18.6 us
    all_gather x1, blocking collectives, local(): lax.all_gather(jnp.concatenate([routes.astype(F32), gate_share], axis=1),...  12.1 us
    pallas_call x4, Pallas kernels, attend(): pl.pallas_call(attn_kernel, grid_spec=pltpu.PrefetchScalarGridSpec(num_sc...  11.9 us
    ppermute x6, starting transfers between devices, shift(): return lax.ppermute(v, 'z', [(i, (i + d) % 4) for i in range(4)])  10 us
    unnamed x36, local copies, waits for them, and re-layouts  9.11 us
  transfers between devices with their start and end apart: 17, of which 7 were waited for; matrix products, arithmetic and copies ran while one was open for 17% of the time, Pallas kernels for 7%

profile of v1, /device:TPU:0, one launch (start us, length us, event | category | flops | bytes accessed | tf_op | source)
XLA Modules:
  0.0 220.7 jit_solution(256916684421972111)
XLA Ops:
  0.0 3.4 %collective-permute-start.4 = (bf16[256,256]{1,0:T(8,128)(2,1)}, bf16[256,256]{1,0:T(8,128)(2,1)S(1)}, u32[]{:S(2)}, u32[]{:S(2)}) collective-permute-start(bf16[256,256]{1,0:T(8,128)(2,1)} %q_ref.1), channel_id=1, source_target_pairs={{0,96},{32,64},{64,32},{96,0},{1,97},{33,65},{65,33},{97,1},{2,98}... | collective-permute-start | bytes 393224 | tf_op jit(solution)/shard_map/ppermute | solution.py:263
  3.4 0.3 collective-permute-start.2
  3.7 2.8 %constant_dynamic-slice_fusion = (bf16[256,1024]{1,0:T(8,128)(2,1)}, bf16[256,1024]{1,0:T(8,128)(2,1)}, bf16[256,1024]{1,0:T(8,128)(2,1)}, bf16[256,1024]{1,0:T(8,128)(2,1)S(1)}) fusion(bf16[256,4096]{1,0:T(8,128)(2,1)} %param.18, s32[]{:T(128)S(6)} %select_n.57, s32[]{:T(128)S(6)} %select_n.53, s32[]{:T(128)S(6)} %select_n.51, s32[]{:T(128)S(6)} %select_n.55), kind=kLoop, calls=%fused_computation.44 | loop fusion | bytes 4194320 | tf_op jit(solution)/shard_map/dynamic_slice | solution.py:295
  6.4 4.1 %collective-permute-start.11 = (bf16[256,1024]{1,0:T(8,128)(2,1)}, bf16[256,1024]{1,0:T(8,128)(2,1)S(1)}, u32[]{:S(2)}, u32[]{:S(2)}) collective-permute-start(bf16[256,1024]{1,0:T(8,128)(2,1)} %get-tuple-element.13), channel_id=1, source_target_pairs={{0,3},{1,0},{2,1},{3,2},{4,7},{5,4},{6,5},{7,6},{8,11},{9,8},{10,9... | collective-permute-start | bytes 1572872 | tf_op jit(solution)/shard_map/ppermute | solution.py:267
  11.2 0.1 copy.15
  11.3 0.1 reshape.102
  11.4 0.1 reduce_sum.48
  11.5 0.1 concatenate.26.info
  11.6 0.0 copy-start
  11.6 2.2 copy-done
  13.8 3.0 %attend.6 = bf16[272,256]{1,0:T(8,128)(2,1)S(1)} custom-call(s32[10]{0:T(128)S(1)} %concatenate.26.info, bf16[256,256]{1,0:T(8,128)(2,1)S(1)} %collective-permute-done.2.q_ref, bf16[2,2048,512]{2,1,0:T(8,128)(2,1)S(1)} %copy-done, bf16[2,2048,512]{2,1,0:T(8,128)(2,1)S(1)} %copy-done, bf16[2,256,512]{2,1,0:T(8,128)(2,1)S(1)} %copy-done.3, ...), custom_call_target="tpu_custom_call" | custom-call | flops 603979776 | bytes 1179648 | tf_op jit(solution)/shard_map/attend/pallas_call | solution.py:72
  16.8 3.3 %collective-permute-start.3 = (bf16[272,256]{1,0:T(8,128)(2,1)S(1)}, bf16[272,256]{1,0:T(8,128)(2,1)}, u32[]{:S(2)}, u32[]{:S(2)}) collective-permute-start(bf16[272,256]{1,0:T(8,128)(2,1)S(1)} %attend.6), channel_id=1, source_target_pairs={{0,64},{32,96},{64,0},{96,32},{1,65},{33,97},{65,1},{97,33},{2,66}... | collective-permute-start | bytes 417800 | tf_op jit(solution)/shard_map/ppermute | solution.py:263
  20.1 0.1 broadcast_divide_fusion
  20.1 0.1 concatenate.27.info
  20.2 0.1 concatenate.25.info
  20.3 2.7 %collective-permute-start.10 = (bf16[256,1024]{1,0:T(8,128)(2,1)S(1)}, bf16[256,1024]{1,0:T(8,128)(2,1)S(1)}, u32[]{:S(2)}, u32[]{:S(2)}) collective-permute-start(bf16[256,1024]{1,0:T(8,128)(2,1)S(1)} %get-tuple-element.16), channel_id=1, source_target_pairs={{0,2},{1,3},{2,0},{3,1},{4,6},{5,7},{6,4},{7,5},{8,10},{9,11},{10,... | collective-permute-start | bytes 1572872 | tf_op jit(solution)/shard_map/ppermute | solution.py:267
  23.1 2.2 copy-done.1
  25.2 3.0 %attend.7 = bf16[272,256]{1,0:T(8,128)(2,1)S(1)} custom-call(s32[10]{0:T(128)S(1)} %concatenate.27.info, bf16[256,256]{1,0:T(8,128)(2,1)S(1)} %collective-permute-done.4.q_ref, bf16[2,2048,512]{2,1,0:T(8,128)(2,1)S(1)} %copy-done.1, bf16[2,2048,512]{2,1,0:T(8,128)(2,1)S(1)} %copy-done.1, bf16[2,256,512]{2,1,0:T(8,128)(2,1)S(1)} %copy-done.3, ...), custom_call_target="tpu_custom_call" | custom-call | flops 603979776 | bytes 1179648 | tf_op jit(solution)/shard_map/attend/pallas_call | solution.py:72
  28.2 0.0 copy-start.5
  28.2 0.1 collective-permute-start.5
  28.3 3.0 %attend.5 = bf16[272,256]{1,0:T(8,128)(2,1)S(1)} custom-call(s32[10]{0:T(128)S(1)} %concatenate.25.info, bf16[256,256]{1,0:T(8,128)(2,1)S(1)} %collective-permute-done.q_ref, bf16[2,2048,512]{2,1,0:T(8,128)(2,1)S(1)} %copy-done.1, bf16[2,2048,512]{2,1,0:T(8,128)(2,1)S(1)} %copy-done.1, bf16[2,256,512]{2,1,0:T(8,128)(2,1)S(1)} %copy-done.3, ...), custom_call_target="tpu_custom_call" | custom-call | flops 603979776 | bytes 1179648 | tf_op jit(solution)/shard_map/attend/pallas_call | solution.py:72
  31.3 0.6 collective-permute-start.1
  31.9 0.1 pad_maximum_fusion
  32.0 0.1 concatenate.24.info
  32.1 12.1 %all_gather.3 = f32[32,16]{1,0:T(8,128)S(1)} all-gather(f32[8,16]{1,0:T(8,128)S(1)} %pad_maximum_fusion), channel_id=1, replica_groups=mesh['yh'=2,'core'=2,'x'=4,'yl'=2,'z'=4] {'z'}, dimensions={0}, use_global_device_ids=true | all-gather | bytes 2560 | tf_op jit(solution)/shard_map/all_gather | solution.py:309
  44.2 2.2 copy-done.2
  46.4 3.0 %attend.4.a_ref = bf16[272,256]{1,0:T(8,128)(2,1)S(1)} custom-call(s32[10]{0:T(128)S(1)} %concatenate.24.info, bf16[256,256]{1,0:T(8,128)(2,1)S(1)} %copy-done.5, bf16[2,2048,512]{2,1,0:T(8,128)(2,1)S(1)} %copy-done.2, bf16[2,2048,512]{2,1,0:T(8,128)(2,1)S(1)} %copy-done.2, bf16[2,256,512]{2,1,0:T(8,128)(2,1)S(1)} %copy-done.3, ...), custom_call_target="tpu_custom_call" | custom-call | flops 603979776 | bytes 1179648 | tf_op jit(solution)/shard_map/attend/pallas_call | solution.py:72
  49.4 0.6 copy-done.4
  50.0 2.5 %merge.1.refs_0_ = bf16[256,256]{1,0:T(8,128)(2,1)} custom-call(bf16[272,256]{1,0:T(8,128)(2,1)} %copy-done.4, bf16[272,256]{1,0:T(8,128)(2,1)} %collective-permute-done.1.b_ref, bf16[272,256]{1,0:T(8,128)(2,1)} %collective-permute-done.3.c_ref, bf16[272,256]{1,0:T(8,128)(2,1)} %collective-permute-done.5.d_ref), custom_call_target="tpu_custom_call" | custom-call | flops 1048576 | bytes 655360 | tf_op jit(solution)/shard_map/merge/pallas_call | solution.py:125
  52.5 1.3 collective-permute-start.8
  53.8 0.1 fusion.23
  53.9 0.9 collective-permute-start.7
  54.8 2.9 %collective-permute-done.8.refs_3_ = bf16[256,256]{1,0:T(8,128)(2,1)S(1)} collective-permute-done((bf16[256,256]{1,0:T(8,128)(2,1)}, bf16[256,256]{1,0:T(8,128)(2,1)S(1)}, u32[]{:S(2)}, u32[]{:S(2)}) %collective-permute-start.8) | collective-permute-done | bytes 131104 | tf_op jit(solution)/shard_map/ppermute | solution.py:267
  57.7 1.0 collective-permute-start.6
  58.7 0.1 add.99
  58.8 0.1 add.100
  58.9 2.5 %collective-permute-done.7.refs_2_ = bf16[256,256]{1,0:T(8,128)(2,1)S(1)} collective-permute-done((bf16[256,256]{1,0:T(8,128)(2,1)}, bf16[256,256]{1,0:T(8,128)(2,1)S(1)}, u32[]{:S(2)}, u32[]{:S(2)}) %collective-permute-start.7) | collective-permute-done | bytes 131104 | tf_op jit(solution)/shard_map/ppermute | solution.py:267
  61.3 2.8 %collective-permute-done.6.refs_1_ = bf16[256,256]{1,0:T(8,128)(2,1)S(1)} collective-permute-done((bf16[256,256]{1,0:T(8,128)(2,1)}, bf16[256,256]{1,0:T(8,128)(2,1)S(1)}, u32[]{:S(2)}, u32[]{:S(2)}) %collective-permute-start.6) | collective-permute-done | bytes 131104 | tf_op jit(solution)/shard_map/ppermute | solution.py:267
  64.2 0.6 copy-done.12
  64.7 0.2 copy-done.7
  65.0 0.2 copy-done.8
  65.1 0.2 copy-done.9
  65.3 4.4 %project.1 = bf16[256,1024]{1,0:T(8,128)(2,1)} custom-call(bf16[256,256]{1,0:T(8,128)(2,1)} %merge.1.refs_0_, bf16[256,256]{1,0:T(8,128)(2,1)} %copy-done.12, bf16[256,256]{1,0:T(8,128)(2,1)} %copy-done.11, bf16[256,256]{1,0:T(8,128)(2,1)} %copy-done.10, bf16[256,1024]{1,0:T(8,128)(2,1)} %get-tuple-element.15.refs_4_, bf16[256,1024]{1,0:T(8,128)(2,1)} %copy-done.8, ...), custom_call_target="tpu_custom_call" | custom-call | flops 536870912 | bytes 2097152 | tf_op jit(solution)/shard_map/project/pallas_call | solution.py:146
  69.7 5.3 %all-to-all-start.1 = ((bf16[8,32,1024]{2,1,0:T(8,128)(2,1)}), bf16[8,32,1024]{2,1,0:T(8,128)(2,1)S(1)}, u32[]{:S(2)}, u32[]{:S(2)}) async-start(bf16[8,32,1024]{2,1,0:T(8,128)(2,1)} %bitcast.39), calls=%async_computation.1 | async-start | bytes 1048576 | tf_op jit(solution)/shard_map/all_to_all | solution.py:345
  75.0 5.0 %convert_reduce_fusion = s32[4,8,8]{2,1,0:T(8,128)S(1)} fusion(s32[4,8,8]{2,1,0:T(8,128)S(1)} %get-tuple-element.17, pred[8,8]{1,0:T(8,128)(4,1)S(1)} %iota_compare_fusion.1), kind=kLoop, calls=%fused_computation.6 | loop fusion | flops 65280 | bytes 2112 | tf_op jit(solution)/shard_map/reduce_sum | solution.py:318
  79.9 0.1 fusion.17
  80.0 0.4 select_reduce_fusion
  80.4 2.8 %all-to-all-done.1 = bf16[8,32,1024]{2,1,0:T(8,128)(2,1)S(1)} async-done(((bf16[8,32,1024]{2,1,0:T(8,128)(2,1)}), bf16[8,32,1024]{2,1,0:T(8,128)(2,1)S(1)}, u32[]{:S(2)}, u32[]{:S(2)}) %all-to-all-start.1) | async-done | bytes 524320 | tf_op jit(solution)/shard_map/all_to_all | solution.py:345
  83.2 3.3 %all-to-all-start = ((bf16[4,8,1024]{2,1,0:T(8,128)(2,1)}), bf16[4,8,1024]{2,1,0:T(8,128)(2,1)S(1)}, u32[]{:S(2)}, u32[]{:S(2)}) async-start(bf16[4,8,1024]{2,1,0:T(8,128)(2,1)} %bitcast.1), calls=%async_computation | async-start | bytes 131072 | tf_op jit(solution)/shard_map/all_to_all | solution.py:299
  86.5 0.1 convert_reduce_fusion.1
  86.5 5.5 %all-to-all-done = bf16[4,8,1024]{2,1,0:T(8,128)(2,1)S(1)} async-done(((bf16[4,8,1024]{2,1,0:T(8,128)(2,1)}), bf16[4,8,1024]{2,1,0:T(8,128)(2,1)S(1)}, u32[]{:S(2)}, u32[]{:S(2)}) %all-to-all-start) | async-done | bytes 65568 | tf_op jit(solution)/shard_map/all_to_all | solution.py:299
  92.0 0.7 convolution_convert_fusion
  92.8 29.2 %all_to_all.25 = bf16[64,16,1024]{2,1,0:T(8,128)(2,1)S(1)} all-to-all(bf16[64,16,1024]{2,1,0:T(8,128)(2,1)S(1)} %bitcast.38), channel_id=1, replica_groups=mesh['yh'=2,'core'=2,'x'=4,'yl'=2,'z'=4] {'yh','x','yl','z'}, dimensions={0} | all-to-all | bytes 4194304 | tf_op jit(solution)/shard_map/all_to_all | solution.py:356
  122.0 28.1 %reshape.108.win_ref = bf16[2,4096,768]{2,1,0:T(8,128)(2,1)} reshape(bf16[2,4096,2,384]{3,2,1,0:T(2,128)(2,1)} %param.22) | data formatting | bytes 25165824 | tf_op jit(solution)/shard_map/reshape | solution.py:361
  150.1 18.6 %experts.1 = (bf16[16,4,16,1024]{3,2,1,0:T(8,128)(2,1)S(1)}, bf16[16,4,16,1024]{3,2,1,0:T(8,128)(2,1)S(1)}) custom-call(bf16[16,4,16,1024]{3,2,1,0:T(8,128)(2,1)} %bitcast.36, bf16[16,4,16,1024]{3,2,1,0:T(8,128)(2,1)} %bitcast.15.other_ref, f32[4,1024]{1,0:T(4,128)S(1)} %reshape.107.gain_ref, bf16[2,4096,768]{2,1,0:T(8,128)(2,1)} %reshape.108.win_ref, ...), custom_call_target="tpu_custom_call" | custom-call | flops 4831838208 | bytes 18874368 | tf_op jit(solution)/shard_map/experts/pallas_call | solution.py:229
  168.7 0.2 collective-permute-start.13
  168.9 4.0 %collective-permute-done.13 = bf16[16,4,16,1024]{3,2,1,0:T(8,128)(2,1)S(1)} collective-permute-done((bf16[16,4,16,1024]{3,2,1,0:T(8,128)(2,1)S(1)}, bf16[16,4,16,1024]{3,2,1,0:T(8,128)(2,1)S(1)}, u32[]{:S(2)}, u32[]{:S(2)}) %collective-permute-start.13) | collective-permute-done | bytes 2097184 | tf_op jit(solution)/shard_map/ppermute | solution.py:263
  172.9 2.3 %add_convert_fusion = bf16[16,4,16,1024]{3,2,1,0:T(8,128)(2,1)} fusion(bf16[16,4,16,1024]{3,2,1,0:T(8,128)(2,1)S(1)} %collective-permute-done.13, bf16[16,4,16,1024]{3,2,1,0:T(8,128)(2,1)S(1)} %get-tuple-element.7), kind=kLoop, calls=%fused_computation | loop fusion | flops 4194304 | bytes 6291456 | tf_op jit(solution)/shard_map/convert_element_type | solution.py:364
  175.2 5.7 %all-to-all-start.3 = ((bf16[64,16,1024]{2,1,0:T(8,128)(2,1)}), bf16[64,16,1024]{2,1,0:T(8,128)(2,1)S(1)}, u32[]{:S(2)}, u32[]{:S(2)}) async-start(bf16[64,16,1024]{2,1,0:T(8,128)(2,1)} %bitcast.37), calls=%async_computation.3 | async-start | bytes 4194304 | tf_op jit(solution)/shard_map/all_to_all | solution.py:365
  180.9 29.9 %all-to-all-done.3 = bf16[64,16,1024]{2,1,0:T(8,128)(2,1)S(1)} async-done(((bf16[64,16,1024]{2,1,0:T(8,128)(2,1)}), bf16[64,16,1024]{2,1,0:T(8,128)(2,1)S(1)}, u32[]{:S(2)}, u32[]{:S(2)}) %all-to-all-start.3) | async-done | bytes 2097184 | tf_op jit(solution)/shard_map/all_to_all | solution.py:365
  210.8 0.5 fusion.10
  211.2 0.5 fusion.2
  211.7 8.4 %all_to_all.26 = bf16[4,8,1024]{2,1,0:T(8,128)(2,1)S(1)} all-to-all(bf16[4,8,1024]{2,1,0:T(8,128)(2,1)S(1)} %fusion.2), channel_id=1, replica_groups=mesh['yh'=2,'core'=2,'x'=4,'yl'=2,'z'=4] {'z'}, dimensions={0} | all-to-all | bytes 131072 | tf_op jit(solution)/shard_map/all_to_all | solution.py:374
  220.1 0.6 copy.18
  (42 shorter events, 0.1 us)
Async XLA Ops:
  0.0 28.2 %collective-permute-start = (bf16[256,256]{1,0:T(8,128)(2,1)}, bf16[256,256]{1,0:T(8,128)(2,1)S(1)}, u32[]{:S(2)}, u32[]{:S(2)}) collective-permute-start(bf16[256,256]{1,0:T(8,128)(2,1)} %q_ref.1), channel_id=1, source_target_pairs={{0,32},{32,0},{64,96},{96,64},{1,33},{33,1},{65,97},{97,65},{2,34}... | collective-permute-start | bytes 393224 | tf_op jit(solution)/shard_map/ppermute | solution.py:263
  0.0 20.3 %collective-permute-start.4 = (bf16[256,256]{1,0:T(8,128)(2,1)}, bf16[256,256]{1,0:T(8,128)(2,1)S(1)}, u32[]{:S(2)}, u32[]{:S(2)}) collective-permute-start(bf16[256,256]{1,0:T(8,128)(2,1)} %q_ref.1), channel_id=1, source_target_pairs={{0,96},{32,64},{64,32},{96,0},{1,97},{33,65},{65,33},{97,1},{2,98}... | collective-permute-start | bytes 393224 | tf_op jit(solution)/shard_map/ppermute | solution.py:263
  3.4 8.2 %collective-permute-start.2 = (bf16[256,256]{1,0:T(8,128)(2,1)}, bf16[256,256]{1,0:T(8,128)(2,1)S(1)}, u32[]{:S(2)}, u32[]{:S(2)}) collective-permute-start(bf16[256,256]{1,0:T(8,128)(2,1)} %q_ref.1), channel_id=1, source_target_pairs={{0,64},{32,96},{64,0},{96,32},{1,65},{33,97},{65,1},{97,33},{2,66}... | collective-permute-start | bytes 393224 | tf_op jit(solution)/shard_map/ppermute | solution.py:263
  3.6 7.6 %copy-start.16 = (s32[3,2]{0,1:T(2,128)S(1)}, s32[3,2]{0,1:T(2,128)}, u32[]{:S(2)}) copy-start(s32[3,2]{0,1:T(2,128)} %param.16) | copy-start | bytes 76
  3.6 7.8 %copy-start.13 = (f32[8,8]{1,0:T(8,128)S(1)}, f32[8,8]{1,0:T(8,128)}, u32[]{:S(2)}) copy-start(f32[8,8]{1,0:T(8,128)} %param.21) | copy-start | bytes 772
  3.7 8.0 %copy-start.3 = (bf16[2,256,512]{2,1,0:T(8,128)(2,1)S(1)}, bf16[2,256,512]{2,1,0:T(8,128)(2,1)}, u32[]{:S(2)}) copy-start(bf16[2,256,512]{2,1,0:T(8,128)(2,1)} %vn_ref.7) | copy-start | bytes 1572868
  6.4 57.7 %collective-permute-start.11 = (bf16[256,1024]{1,0:T(8,128)(2,1)}, bf16[256,1024]{1,0:T(8,128)(2,1)S(1)}, u32[]{:S(2)}, u32[]{:S(2)}) collective-permute-start(bf16[256,1024]{1,0:T(8,128)(2,1)} %get-tuple-element.13), channel_id=1, source_target_pairs={{0,3},{1,0},{2,1},{3,2},{4,7},{5,4},{6,5},{7,6},{8,11},{9,8},{10,9... | collective-permute-start | bytes 1572872 | tf_op jit(solution)/shard_map/ppermute | solution.py:267
  10.6 53.6 %collective-permute-start.9 = (bf16[256,1024]{1,0:T(8,128)(2,1)}, bf16[256,1024]{1,0:T(8,128)(2,1)S(1)}, u32[]{:S(2)}, u32[]{:S(2)}) collective-permute-start(bf16[256,1024]{1,0:T(8,128)(2,1)} %get-tuple-element.14), channel_id=1, source_target_pairs={{0,1},{1,2},{2,3},{3,0},{4,5},{5,6},{6,7},{7,4},{8,9},{9,10},{10,1... | collective-permute-start | bytes 1572872 | tf_op jit(solution)/shard_map/ppermute | solution.py:267
  11.6 2.2 copy-start
  13.8 6.5 %copy-start.15 = (s32[8,8]{1,0:T(8,128)S(1)}, s32[8,8]{1,0:T(8,128)}, u32[]{:S(2)}) copy-start(s32[8,8]{1,0:T(8,128)} %param.20) | copy-start | bytes 772
  16.8 14.5 %collective-permute-start.3 = (bf16[272,256]{1,0:T(8,128)(2,1)S(1)}, bf16[272,256]{1,0:T(8,128)(2,1)}, u32[]{:S(2)}, u32[]{:S(2)}) collective-permute-start(bf16[272,256]{1,0:T(8,128)(2,1)S(1)} %attend.6), channel_id=1, source_target_pairs={{0,64},{32,96},{64,0},{96,32},{1,65},{33,97},{65,1},{97,33},{2,66}... | collective-permute-start | bytes 417800 | tf_op jit(solution)/shard_map/ppermute | solution.py:263
  20.3 43.8 %collective-permute-start.10 = (bf16[256,1024]{1,0:T(8,128)(2,1)S(1)}, bf16[256,1024]{1,0:T(8,128)(2,1)S(1)}, u32[]{:S(2)}, u32[]{:S(2)}) collective-permute-start(bf16[256,1024]{1,0:T(8,128)(2,1)S(1)} %get-tuple-element.16), channel_id=1, source_target_pairs={{0,2},{1,3},{2,0},{3,1},{4,6},{5,7},{6,4},{7,5},{8,10},{9,11},{10,... | collective-permute-start | bytes 1572872 | tf_op jit(solution)/shard_map/ppermute | solution.py:267
  23.1 2.2 copy-start.1
  28.2 16.0 %copy-start.5 = (bf16[256,256]{1,0:T(8,128)(2,1)S(1)}, bf16[256,256]{1,0:T(8,128)(2,1)}, u32[]{:S(2)}) copy-start(bf16[256,256]{1,0:T(8,128)(2,1)} %q_ref.1) | copy-start | bytes 393220
  28.2 21.8 %collective-permute-start.5 = (bf16[272,256]{1,0:T(8,128)(2,1)S(1)}, bf16[272,256]{1,0:T(8,128)(2,1)}, u32[]{:S(2)}, u32[]{:S(2)}) collective-permute-start(bf16[272,256]{1,0:T(8,128)(2,1)S(1)} %attend.7), channel_id=1, source_target_pairs={{0,96},{32,64},{64,32},{96,0},{1,97},{33,65},{65,33},{97,1},{2,98}... | collective-permute-start | bytes 417800 | tf_op jit(solution)/shard_map/ppermute | solution.py:263
  31.3 18.7 %collective-permute-start.1 = (bf16[272,256]{1,0:T(8,128)(2,1)S(1)}, bf16[272,256]{1,0:T(8,128)(2,1)}, u32[]{:S(2)}, u32[]{:S(2)}) collective-permute-start(bf16[272,256]{1,0:T(8,128)(2,1)S(1)} %attend.5), channel_id=1, source_target_pairs={{0,32},{32,0},{64,96},{96,64},{1,33},{33,1},{65,97},{97,65},{2,34}... | collective-permute-start | bytes 417800 | tf_op jit(solution)/shard_map/ppermute | solution.py:263
  44.2 2.2 copy-start.2
  49.4 0.7 copy-start.4
  52.5 5.2 %collective-permute-start.8 = (bf16[256,256]{1,0:T(8,128)(2,1)}, bf16[256,256]{1,0:T(8,128)(2,1)S(1)}, u32[]{:S(2)}, u32[]{:S(2)}) collective-permute-start(bf16[256,256]{1,0:T(8,128)(2,1)} %merge.1.refs_0_), channel_id=1, source_target_pairs={{0,3},{1,0},{2,1},{3,2},{4,7},{5,4},{6,5},{7,6},{8,11},{9,8},{10,9... | collective-permute-start | bytes 393224 | tf_op jit(solution)/shard_map/ppermute | solution.py:267
  53.9 7.4 %collective-permute-start.7 = (bf16[256,256]{1,0:T(8,128)(2,1)}, bf16[256,256]{1,0:T(8,128)(2,1)S(1)}, u32[]{:S(2)}, u32[]{:S(2)}) collective-permute-start(bf16[256,256]{1,0:T(8,128)(2,1)} %merge.1.refs_0_), channel_id=1, source_target_pairs={{0,2},{1,3},{2,0},{3,1},{4,6},{5,7},{6,4},{7,5},{8,10},{9,11},{10,... | collective-permute-start | bytes 393224 | tf_op jit(solution)/shard_map/ppermute | solution.py:267
  57.7 6.4 %copy-start.10 = (bf16[256,256]{1,0:T(8,128)(2,1)}, bf16[256,256]{1,0:T(8,128)(2,1)S(1)}, u32[]{:S(2)}) copy-start(bf16[256,256]{1,0:T(8,128)(2,1)S(1)} %collective-permute-done.8.refs_3_) | copy-start | bytes 393220
  57.7 6.4 %collective-permute-start.6 = (bf16[256,256]{1,0:T(8,128)(2,1)}, bf16[256,256]{1,0:T(8,128)(2,1)S(1)}, u32[]{:S(2)}, u32[]{:S(2)}) collective-permute-start(bf16[256,256]{1,0:T(8,128)(2,1)} %merge.1.refs_0_), channel_id=1, source_target_pairs={{0,1},{1,2},{2,3},{3,0},{4,5},{5,6},{6,7},{7,4},{8,9},{9,10},{10,1... | collective-permute-start | bytes 393224 | tf_op jit(solution)/shard_map/ppermute | solution.py:267
  61.3 2.8 %copy-start.11 = (bf16[256,256]{1,0:T(8,128)(2,1)}, bf16[256,256]{1,0:T(8,128)(2,1)S(1)}, u32[]{:S(2)}) copy-start(bf16[256,256]{1,0:T(8,128)(2,1)S(1)} %collective-permute-done.7.refs_2_) | copy-start | bytes 393220
  64.1 0.6 copy-start.12
  64.1 0.8 copy-start.7
  64.1 1.0 copy-start.8
  64.1 1.2 copy-start.9
  69.7 13.5 %all-to-all-start.1 = ((bf16[8,32,1024]{2,1,0:T(8,128)(2,1)}), bf16[8,32,1024]{2,1,0:T(8,128)(2,1)S(1)}, u32[]{:S(2)}, u32[]{:S(2)}) async-start(bf16[8,32,1024]{2,1,0:T(8,128)(2,1)} %bitcast.39), calls=%async_computation.1 | async-start | bytes 1048576 | tf_op jit(solution)/shard_map/all_to_all | solution.py:345
  83.2 8.9 %all-to-all-start = ((bf16[4,8,1024]{2,1,0:T(8,128)(2,1)}), bf16[4,8,1024]{2,1,0:T(8,128)(2,1)S(1)}, u32[]{:S(2)}, u32[]{:S(2)}) async-start(bf16[4,8,1024]{2,1,0:T(8,128)(2,1)} %bitcast.1), calls=%async_computation | async-start | bytes 131072 | tf_op jit(solution)/shard_map/all_to_all | solution.py:299
  92.8 29.2 %copy-start.14 = (f32[4096]{0:T(1024)S(1)}, f32[4096]{0:T(1024)}, u32[]{:S(2)}) copy-start(f32[4096]{0:T(1024)} %param.19) | copy-start | bytes 49156
  122.0 28.1 %copy-start.6 = (bf16[64,16,1024]{2,1,0:T(8,128)(2,1)}, bf16[64,16,1024]{2,1,0:T(8,128)(2,1)S(1)}, u32[]{:S(2)}) copy-start(bf16[64,16,1024]{2,1,0:T(8,128)(2,1)S(1)} %all_to_all.25) | copy-start | bytes 6291460
  122.0 28.1 %collective-permute-start.12 = (bf16[64,16,1024]{2,1,0:T(8,128)(2,1)S(1)}, bf16[64,16,1024]{2,1,0:T(8,128)(2,1)}, u32[]{:S(2)}, u32[]{:S(2)}) collective-permute-start(bf16[64,16,1024]{2,1,0:T(8,128)(2,1)S(1)} %all_to_all.25), channel_id=1, source_target_pairs={{0,32},{32,0},{1,33},{33,1},{2,34},{34,2},{3,35},{35,3},{4,36},{36... | collective-permute-start | bytes 6291464 | tf_op jit(solution)/shard_map/ppermute | solution.py:263
  168.7 4.2 %collective-permute-start.13 = (bf16[16,4,16,1024]{3,2,1,0:T(8,128)(2,1)S(1)}, bf16[16,4,16,1024]{3,2,1,0:T(8,128)(2,1)S(1)}, u32[]{:S(2)}, u32[]{:S(2)}) collective-permute-start(bf16[16,4,16,1024]{3,2,1,0:T(8,128)(2,1)S(1)} %get-tuple-element.8), channel_id=1, source_target_pairs={{0,32},{32,0},{1,33},{33,1},{2,34},{34,2},{3,35},{35,3},{4,36},{36... | collective-permute-start | bytes 6291464 | tf_op jit(solution)/shard_map/ppermute | solution.py:263
  175.2 35.6 %all-to-all-start.3 = ((bf16[64,16,1024]{2,1,0:T(8,128)(2,1)}), bf16[64,16,1024]{2,1,0:T(8,128)(2,1)S(1)}, u32[]{:S(2)}, u32[]{:S(2)}) async-start(bf16[64,16,1024]{2,1,0:T(8,128)(2,1)} %bitcast.37), calls=%async_computation.3 | async-start | bytes 4194304 | tf_op jit(solution)/shard_map/all_to_all | solution.py:365

commit v2 on v1

v2 whole, which is shorter than its diff:
```python
import math

import jax
import jax.numpy as jnp
from jax import lax
from jax.experimental import pallas as pl
from jax.experimental.pallas import tpu as pltpu
from jax.sharding import Mesh, PartitionSpec as P

HEAD_DIM = 128
SEQ = ("yh", "core")
MP = ("x", "yl", "z")
NEG = -1e30
BF = jnp.bfloat16
F32 = jnp.float32
ANY_LAST = (((1,), (1,)), ((), ()))


def attn_kernel(info, qa_ref, qb_ref, kc_ref, vc_ref, kn_ref, vn_ref, oa_ref, ob_ref, s_ref):
    rows = qa_ref.shape[0]
    cache_rows = kc_ref.shape[1]
    chunk = kn_ref.shape[1]
    chunks = cache_rows // chunk
    coef = math.log2(math.e) / math.sqrt(HEAD_DIM)
    valid = info[1]
    key_pos = info[2] + lax.broadcasted_iota(jnp.int32, (1, chunk), 1)
    lane = lax.broadcasted_iota(jnp.int32, (rows, 128), 1)
    column = lax.broadcasted_iota(jnp.int32, (1, chunk), 1)
    for b, (q_ref, out_ref) in enumerate(((qa_ref, oa_ref), (qb_ref, ob_ref))):
        pos = info[3 + b] + lax.broadcasted_iota(jnp.int32, (rows, 1), 0)
        limit = pos
        for a in range(3):
            start, end = info[5 + 2 * a], info[6 + 2 * a]
            limit = jnp.where((pos >= start) & (pos < end), jnp.maximum(limit, end - 1), limit)
        tract_ok = key_pos <= limit
        stats = jnp.zeros((rows, 128), F32)
        for h in range(2):
            at = 2 * b + h
            q = q_ref[:, h * HEAD_DIM : (h + 1) * HEAD_DIM]
            top = None
            for c in range(chunks + 1):
                if c < chunks:
                    k = kc_ref[0, c * chunk : (c + 1) * chunk, :]
                    s = lax.dot_general(q, k, ANY_LAST, preferred_element_type=F32)
                    s = s + jnp.where(column < valid - c * chunk, 0.0, NEG)
                else:
                    s = lax.dot_general(q, kn_ref[0], ANY_LAST, preferred_element_type=F32)
                    s = jnp.where(tract_ok, s, NEG)
                s_ref[at, :, c * chunk : (c + 1) * chunk] = s
                top = s if top is None else jnp.maximum(top, s)
            m = jnp.max(top, axis=1, keepdims=True) * coef
            total = None
            acc = None
            for c in range(chunks + 1):
                p = jnp.exp2(s_ref[at, :, c * chunk : (c + 1) * chunk] * coef - m)
                total = p if total is None else total + p
                v = vc_ref[0, c * chunk : (c + 1) * chunk, :] if c < chunks else vn_ref[0]
                part = jnp.dot(p.astype(BF), v, preferred_element_type=F32)
                acc = part if acc is None else acc + part
            total = jnp.sum(total, axis=1, keepdims=True)
            out_ref[0:rows, h * HEAD_DIM : (h + 1) * HEAD_DIM] = (acc / total).astype(BF)
            level = m + jnp.log2(total)
            for part in range(3):
                piece = level.astype(BF).astype(F32)
                level = level - piece
                stats = jnp.where(lane == 3 * h + part, piece, stats)
        out_ref[rows : rows + 16, :] = stats.T[0:16, :].astype(BF)


def attend(info, qa, qb, cache_kv, new_kv):
    rows = qa.shape[0]
    cache_rows, new_rows = cache_kv.shape[1], new_kv.shape[1]
    keys = cache_rows + new_rows
    whole = pl.BlockSpec((rows, 2 * HEAD_DIM), lambda i, t: (0, 0))
    result = pl.BlockSpec((rows + 16, 2 * HEAD_DIM), lambda i, t: (0, 0))
    shape = jax.ShapeDtypeStruct((rows + 16, 2 * HEAD_DIM), BF)
    return pl.pallas_call(
        attn_kernel,
        grid_spec=pltpu.PrefetchScalarGridSpec(
            num_scalar_prefetch=1,
            grid=(1,),
            in_specs=[
                whole,
                whole,
                pl.BlockSpec((1, cache_rows, HEAD_DIM), lambda i, t: (0, 0, t[0])),
                pl.BlockSpec((1, cache_rows, HEAD_DIM), lambda i, t: (1, 0, t[0])),
                pl.BlockSpec((1, new_rows, HEAD_DIM), lambda i, t: (0, 0, t[0])),
                pl.BlockSpec((1, new_rows, HEAD_DIM), lambda i, t: (1, 0, t[0])),
            ],
            out_specs=[result, result],
            scratch_shapes=[pltpu.VMEM((4, rows, keys), F32)],
        ),
        out_shape=[shape, shape],
        compiler_params=pltpu.CompilerParams(vmem_limit_bytes=32 << 20),
        cost_estimate=pl.CostEstimate(
            flops=32 * rows * keys * HEAD_DIM,
            bytes_accessed=4 * keys * HEAD_DIM,
            transcendentals=4 * rows * keys,
        ),
        name="attend",
    )(info, qa, qb, cache_kv, cache_kv, new_kv, new_kv)


def project_kernel(a_ref, b_ref, c_ref, d_ref, w_ref, out_ref, att_ref):
    parts = (a_ref, b_ref, c_ref, d_ref)
    rows = out_ref.shape[0]

    @pl.when(pl.program_id(0) == 0)
    def _():
        pad = jnp.zeros((112, rows), F32)
        stats = [
            jnp.concatenate([p[rows : rows + 16, :].astype(F32), pad], axis=0).T for p in parts
        ]
        for h in range(2):
            cols = slice(h * HEAD_DIM, (h + 1) * HEAD_DIM)
            at = 3 * h
            levels = [
                t[:, at : at + 1] + t[:, at + 1 : at + 2] + t[:, at + 2 : at + 3] for t in stats
            ]
            best = jnp.maximum(
                jnp.maximum(levels[0], levels[1]), jnp.maximum(levels[2], levels[3])
            )
            weights = [jnp.exp2(v - best) for v in levels]
            total = weights[0] + weights[1] + weights[2] + weights[3]
            acc = None
            for w, p in zip(weights, parts):
                term = p[0:rows, cols].astype(F32) * w
                acc = term if acc is None else acc + term
            att_ref[:, cols] = (acc / total).astype(BF)

    out_ref[...] = jnp.dot(att_ref[...], w_ref[...], preferred_element_type=F32).astype(BF)


def project(parts, out_proj):
    rows, depth = parts[0].shape[0] - 16, parts[0].shape[1]
    width = out_proj.shape[1]
    step = 1024
    return pl.pallas_call(
        project_kernel,
        grid=(width // step,),
        in_specs=[pl.BlockSpec((rows + 16, depth), lambda i: (0, 0))] * 4
        + [pl.BlockSpec((depth, step), lambda i: (0, i))],
        out_specs=pl.BlockSpec((rows, step), lambda i: (0, i)),
        out_shape=jax.ShapeDtypeStruct((rows, width), BF),
        scratch_shapes=[pltpu.VMEM((rows, depth), BF)],
        cost_estimate=pl.CostEstimate(
            flops=2 * rows * depth * width, bytes_accessed=4 * depth * width, transcendentals=0
        ),
        name="project",
    )(*parts, out_proj)


def settle_kernel(arrived_ref, residual_ref, gain_ref, pick_ref, stream_ref, out_ref):
    tok, width = residual_ref.shape
    groups = arrived_ref.shape[0]
    chunk = out_ref.shape[2]
    chunks = width // chunk
    pieces = []
    square = None
    for c in range(chunks):
        cols = slice(c * chunk, (c + 1) * chunk)
        acc = arrived_ref[0, :, cols].astype(F32)
        for g in range(1, groups):
            acc = acc + arrived_ref[g, :, cols].astype(F32)
        stream = (residual_ref[:, cols].astype(F32) + acc).astype(BF)
        stream_ref[:, cols] = stream
        piece = stream.astype(F32)
        pieces.append(piece)
        term = jnp.sum(piece * piece, axis=1, keepdims=True)
        square = term if square is None else square + term
    scale = lax.rsqrt(square * (1.0 / width) + 1e-6)
    normed = [
        p * scale * gain_ref[:, c * chunk : (c + 1) * chunk] for c, p in enumerate(pieces)
    ]
    stacked = jnp.concatenate(normed, axis=0).astype(BF)
    rows = jnp.dot(pick_ref[...], stacked, preferred_element_type=F32).astype(BF)
    half = out_ref.shape[0] // 2
    rows = rows.reshape(half, 16, chunk)
    out_ref[0:half] = rows
    out_ref[half : 2 * half] = rows


def settle(arrived, residual, gain, pick):
    tok, width = residual.shape
    chunk = width // 4
    return pl.pallas_call(
        settle_kernel,
        out_shape=[
            jax.ShapeDtypeStruct((tok, width), BF),
            jax.ShapeDtypeStruct((pick.shape[0] // 8, 16, chunk), BF),
        ],
        compiler_params=pltpu.CompilerParams(vmem_limit_bytes=32 << 20),
        cost_estimate=pl.CostEstimate(
            flops=1 << 26, bytes_accessed=4 << 20, transcendentals=0
        ),
        name="settle",
    )(arrived, residual, gain.reshape(1, width), pick)


def expert_kernel(
    own_ref, other_ref, perm_ref, back_ref, win_ref, wout_ref, kept_ref, sent_ref, x_ref,
    hidden_ref, z_ref
):
    step = pl.program_id(0)
    chunk = own_ref.shape[2]
    chunks = 4
    sources = own_ref.shape[0]
    half = sources * 2
    ff = wout_ref.shape[1]
    sides = ((own_ref, kept_ref), (other_ref, sent_ref))

    @pl.when(step == 0)
    def _():
        for side, (ref, _) in enumerate(sides):
            for g in range(sources // 16):
                block = ref[16 * g : 16 * g + 16].reshape(256, chunk)
                y = jnp.dot(perm_ref[...], block, preferred_element_type=F32).astype(BF)
                at = side * half + g * 32
                for e in range(2):
                    for c in range(chunks):
                        first = (e * chunks + c) * 32
                        x_ref[e, c, at : at + 32, :] = y[first : first + 32]

    @pl.when(step < chunks)
    def _():
        for e in range(2):
            for p in range(2):
                cols = slice(p * ff, (p + 1) * ff)
                part = jnp.dot(x_ref[e, step], win_ref[e, p], preferred_element_type=F32)

                @pl.when(step == 0)
                def _():
                    hidden_ref[e, :, cols] = part

                @pl.when(step > 0)
                def _():
                    hidden_ref[e, :, cols] = hidden_ref[e, :, cols] + part

    @pl.when(step >= chunks)
    def _():
        c = step - chunks
        for e in range(2):
            gate, up = hidden_ref[e, :, :ff], hidden_ref[e, :, ff:]
            act = (gate / (1.0 + jnp.exp(-gate)) * up).astype(BF)
            z_ref[e, c] = jnp.dot(act, wout_ref[e], preferred_element_type=F32).astype(BF)

    @pl.when(step == 2 * chunks - 1)
    def _():
        for side, (_, ref) in enumerate(sides):
            for g in range(sources // 16):
                at = side * half + g * 32
                block = jnp.concatenate(
                    [z_ref[e, c, at : at + 32, :] for e in range(2) for c in range(chunks)],
                    axis=0,
                )
                y = jnp.dot(back_ref[...], block, preferred_element_type=F32).astype(BF)
                ref[16 * g : 16 * g + 16] = y.reshape(16, 16, chunk)


def experts(own, other, perm, w_in, w_out):
    sources, _, chunk = own.shape
    chunks = 4
    ff = w_out.shape[1]
    rows = 4 * sources
    shape = jax.ShapeDtypeStruct(own.shape, BF)
    whole = pl.BlockSpec(own.shape, lambda i: (0, 0, 0))
    square = pl.BlockSpec(perm.shape, lambda i: (0, 0))
    return pl.pallas_call(
        expert_kernel,
        grid=(2 * chunks,),
        in_specs=[
            whole,
            whole,
            square,
            square,
            pl.BlockSpec((2, 2, chunk, ff), lambda i: (0, 0, jnp.minimum(i, chunks - 1), 0)),
            pl.BlockSpec((2, ff, chunk), lambda i: (0, 0, jnp.maximum(i - chunks, 0))),
        ],
        out_specs=[whole, whole],
        out_shape=[shape, shape],
        scratch_shapes=[
            pltpu.VMEM((2, chunks, rows, chunk), BF),
            pltpu.VMEM((2, rows, 2 * ff), F32),
            pltpu.VMEM((2, chunks, rows, chunk), BF),
        ],
        compiler_params=pltpu.CompilerParams(vmem_limit_bytes=56 << 20),
        cost_estimate=pl.CostEstimate(
            flops=12 * rows * chunks * chunk * ff,
            bytes_accessed=12 * chunks * chunk * ff,
            transcendentals=2 * rows * ff,
        ),
        name="experts",
    )(own, other, perm, perm.T, w_in, w_out)


def combine_kernel(share_ref, returned_ref, stream_ref, out_ref):
    tok = stream_ref.shape[0]
    chunk = returned_ref.shape[1]
    both = jnp.dot(share_ref[...], returned_ref[...], preferred_element_type=F32)
    half = both.shape[0] // 2
    total = both[:half] + both[half:]
    for c in range(half // tok):
        cols = slice(c * chunk, (c + 1) * chunk)
        out_ref[:, cols] = (
            stream_ref[:, cols].astype(F32) + total[c * tok : (c + 1) * tok]
        ).astype(BF)


def combine(share, returned, stream):
    return pl.pallas_call(
        combine_kernel,
        out_shape=jax.ShapeDtypeStruct(stream.shape, BF),
        compiler_params=pltpu.CompilerParams(vmem_limit_bytes=32 << 20),
        name="combine",
    )(share, returned, stream)


def swap(v, axes, bit):
    count = 4 if len(axes) == 2 else 2
    return lax.ppermute(v, axes, [(i, i ^ bit) for i in range(count)])


def local(
    queries,
    new_kv,
    cache_kv,
    cached_len,
    image_spans,
    residual,
    out_proj,
    norm_gain,
    routes,
    gate_weights,
    w_in,
    w_out,
):
    seq = lax.axis_index(SEQ)
    tract = queries.shape[0]
    cache = cache_kv.shape[1]
    tok = residual.shape[0]
    width = residual.shape[1]
    quarter = width // 4
    spread = ("yh",) + MP

    query_parts = [queries] + [swap(queries, SEQ, d) for d in (1, 2, 3)]
    valid = jnp.clip(cached_len[0] - seq * cache, 0, cache)

    def attend_pair(d):
        info = jnp.concatenate(
            [
                jnp.stack(
                    [
                        lax.axis_index("x"),
                        valid,
                        seq * tract,
                        (seq ^ d) * tract,
                        (seq ^ (d + 1)) * tract,
                    ]
                ).astype(jnp.int32),
                image_spans.reshape(-1),
            ]
        )
        return attend(info, query_parts[d], query_parts[d + 1], cache_kv, new_kv)

    mine, beside = attend_pair(0)
    across, diagonal = attend_pair(2)
    parts = [mine, swap(beside, SEQ, 1), swap(across, SEQ, 2), swap(diagonal, SEQ, 3)]
    partial = project(parts, out_proj)
    arrived = lax.all_to_all(
        partial.reshape(32, tok, width), MP, split_axis=0, concat_axis=0, tiled=True
    )

    gate_share = gate_weights / jnp.sum(gate_weights, axis=1, keepdims=True)
    top = routes.shape[1]
    same = routes[:, :, None, None] == routes[None, None, :, :]
    earlier = jnp.arange(tok)[:, None] > jnp.arange(tok)[None, :]
    rank = jnp.sum((same & earlier[:, None, :, None]).astype(jnp.int32), axis=(2, 3))
    slot = routes * 2 + rank
    pairs = 32
    placement = slot[:, :, None] == jnp.arange(pairs * 4, dtype=jnp.int32)[None, None, :]
    chosen = jnp.sum(placement.astype(F32), axis=1)
    weighed = jnp.sum(jnp.where(placement, gate_share[:, :, None], 0.0), axis=1)
    eye = jnp.eye(4, dtype=F32)

    def spread_rows(v):
        wide = v.reshape(1, tok, pairs, 1, 4) * eye.reshape(4, 1, 1, 4, 1)
        return wide.reshape(4 * tok, pairs * 16)

    pick = spread_rows(chosen).astype(BF).T
    share = spread_rows(weighed)
    coarse = share.astype(BF)
    fine = (share - coarse.astype(F32)).astype(BF)
    share = jnp.concatenate([coarse, fine], axis=0)
    share = jnp.concatenate([share, share], axis=1)

    perm = jnp.eye(256, dtype=BF).reshape(16, 4, 2, 2, 256).transpose(2, 1, 0, 3, 4)
    perm = perm.reshape(256, 256)

    stream, outgoing = settle(arrived, residual, norm_gain, pick)

    outgoing, held = lax.optimization_barrier((outgoing, w_in))
    own = lax.all_to_all(outgoing, spread, split_axis=0, concat_axis=0, tiled=True)
    turned = held.transpose(0, 2, 1, 3)
    own, turned = lax.optimization_barrier((own, turned))
    other = swap(own, ("core",), 1)
    kept, sent = experts(own, other, perm, turned, w_out)
    got = swap(sent, ("core",), 1)
    summed = (kept.astype(F32) + got.astype(F32)).astype(BF)
    returned = lax.all_to_all(summed, spread, split_axis=0, concat_axis=0, tiled=True)
    return combine(share, returned.reshape(-1, quarter), stream)


def solution(mesh):
    fine = Mesh(mesh.devices.reshape(2, 2, 4, 2, 4), SEQ + MP)
    in_specs = (
        P(SEQ, MP),
        P(None, SEQ, None),
        P(None, SEQ, None),
        P(),
        P(),
        P(SEQ + MP, None),
        P(MP, None),
        P(),
        P(SEQ + MP, None),
        P(SEQ + MP, None),
        P(MP, None, None, SEQ),
        P(MP, SEQ, None),
    )
    return jax.shard_map(
        local, mesh=fine, in_specs=in_specs, out_specs=P(SEQ + MP, None), check_vma=False
    )
```

time: 224 us -> 185 us (0.83); the launches traced: 221 us -> 184 us
  blocking collectives: 49.6 us -> 0 us
  waiting for transfers between devices: 50.4 us -> 83.8 us
  local copies, waits for them, and re-layouts: 40.6 us -> 22.7 us
    all_to_all x2 -> x0, blocking collectives: 37.5 us -> none  [the longest x1 29.2 us: local(): lax.all_to_all(outgoing.reshape(64, 16, quarter), ('yh',) + MP, split_axi...]
    all_to_all x3, waiting for transfers between devices: 38.1 us -> 69.3 us  [the longest x1 27.6 us: local(): lax.all_to_all(summed, spread, split_axis=0, concat_axis=0, tiled=True)]
    reshape x3 -> x1, local copies, waits for them, and re-layouts: 28.2 us -> 0.08 us  [attend_pair(): image_spans.reshape(-1)]
    all_gather x1 -> x0, blocking collectives: 12.1 us -> none  [local(): lax.all_gather(jnp.concatenate([routes.astype(F32), gate_share], axis=1),...]
    optimization_barrier x0 -> x1, local copies, waits for them, and re-layouts: none -> 11.6 us  [local(): outgoing, held = lax.optimization_barrier((outgoing, w_in))]
    all_to_all x3, starting transfers between devices: 14.3 us -> 24.7 us  [the longest x1 9.28 us: local(): lax.all_to_all(partial.reshape(32, tok, width), MP, split_axis=0, concat_...]
    ppermute x8, waiting for transfers between devices: 4.06 us -> 14.4 us  [swap(): return lax.ppermute(v, axes, [(i, i ^ bit) for i in range(count)])]
    ppermute x6 -> x0, starting transfers between devices: 10 us -> none  [shift(): return lax.ppermute(v, 'z', [(i, (i + d) % 4) for i in range(4)])]
  transfers between devices with their start and end apart: 17 -> 11, of which waited for: 7 -> 7; matrix products, arithmetic and copies ran while one was open for 17% -> 11% of each run, Pallas kernels for 7% -> 5%
where the time goes in v2:
time: 185 us; the launch traced here: 184 us
  waiting for transfers between devices  83.8 us (45%)
  Pallas kernels  37.1 us (20%)
  starting transfers between devices  32 us (17%)
  local copies, waits for them, and re-layouts  22.7 us (12%)
  other arithmetic  7.74 us (4%)
    all_to_all x1, waiting for transfers between devices, local(): lax.all_to_all(summed, spread, split_axis=0, concat_axis=0, tiled=True)  27.6 us
    all_to_all x1, waiting for transfers between devices, local(): lax.all_to_all(partial.reshape(32, tok, width), MP, split_axis=0, concat_...  23.7 us
    pallas_call x1, Pallas kernels, experts(): pl.pallas_call(expert_kernel, grid=(2 * chunks,), in_specs=[whole, whole,...  20.2 us
    all_to_all x1, waiting for transfers between devices, local(): lax.all_to_all(outgoing, spread, split_axis=0, concat_axis=0, tiled=True)  18 us
    ppermute x8, waiting for transfers between devices, swap(): return lax.ppermute(v, axes, [(i, i ^ bit) for i in range(count)])  14.4 us
    optimization_barrier x1, local copies, waits for them, and re-layouts, local(): outgoing, held = lax.optimization_barrier((outgoing, w_in))  11.6 us
    pallas_call x2, Pallas kernels, attend(): pl.pallas_call(attn_kernel, grid_spec=pltpu.PrefetchScalarGridSpec(num_sc...  9.68 us
    all_to_all x1, starting transfers between devices, local(): lax.all_to_all(partial.reshape(32, tok, width), MP, split_axis=0, concat_...  9.28 us
  transfers between devices with their start and end apart: 11, of which 7 were waited for; matrix products, arithmetic and copies ran while one was open for 11% of the time, Pallas kernels for 5%

profile of v2, /device:TPU:0, one launch (start us, length us, event | category | flops | bytes accessed | tf_op | source)
XLA Modules:
  0.0 184.2 jit_solution(17476436070554427246)
XLA Ops:
  0.0 0.0 collective-permute-start
  0.0 3.4 %collective-permute-start.3 = (bf16[256,256]{1,0:T(8,128)(2,1)}, bf16[256,256]{1,0:T(8,128)(2,1)S(1)}, u32[]{:S(2)}, u32[]{:S(2)}) collective-permute-start(bf16[256,256]{1,0:T(8,128)(2,1)} %qa_ref.1), channel_id=1, source_target_pairs={{0,96},{32,64},{64,32},{96,0},{1,97},{33,65},{65,33},{97,1},{2,98}... | collective-permute-start | bytes 393224 | tf_op jit(solution)/shard_map/ppermute | solution.py:320
  3.4 0.3 collective-permute-start.2
  4.3 0.8 copy.23
  5.1 0.1 reshape.88
  5.2 0.1 concatenate.14.info
  5.2 0.1 concatenate.15.info
  5.3 0.0 collective-permute-done.qb_ref
  5.3 2.2 %copy-done = bf16[2,2048,512]{2,1,0:T(8,128)(2,1)S(1)} copy-done((bf16[2,2048,512]{2,1,0:T(8,128)(2,1)S(1)}, bf16[2,2048,512]{2,1,0:T(8,128)(2,1)}, u32[]{:S(2)}) %copy-start) | copy-done | bytes 4194328
  7.5 1.0 copy-done.2
  8.6 0.9 copy-done.6
  9.5 4.8 %attend.2 = (bf16[272,256]{1,0:T(8,128)(2,1)S(1)}, bf16[272,256]{1,0:T(8,128)(2,1)S(1)}) custom-call(s32[11]{0:T(128)S(1)} %concatenate.14.info, bf16[256,256]{1,0:T(8,128)(2,1)S(1)} %copy-done.6, bf16[256,256]{1,0:T(8,128)(2,1)S(1)} %collective-permute-done.qb_ref, bf16[2,2048,512]{2,1,0:T(8,128)(2,1)S(1)} %copy-done, bf16[2,2048,512]{2,1,0:T(8,128)(2,1)S(1)} %copy-done, ...), custom_call_target="tpu_custom_call" | custom-call | flops 2415919104 | bytes 1179648 | tf_op jit(solution)/shard_map/attend/pallas_call | solution.py:77
  14.3 0.0 copy-start.5
  14.3 0.1 collective-permute-start.1
  14.4 0.0 collective-permute-done.3.qb_ref
  14.4 0.0 collective-permute-done.2.qa_ref
  14.4 0.0 copy-done.1
  14.5 0.0 copy-done.3
  14.5 4.8 %attend.3 = (bf16[272,256]{1,0:T(8,128)(2,1)S(1)}, bf16[272,256]{1,0:T(8,128)(2,1)S(1)}) custom-call(s32[11]{0:T(128)S(1)} %concatenate.15.info, bf16[256,256]{1,0:T(8,128)(2,1)S(1)} %collective-permute-done.2.qa_ref, bf16[256,256]{1,0:T(8,128)(2,1)S(1)} %collective-permute-done.3.qb_ref, bf16[2,2048,512]{2,1,0:T(8,128)(2,1)S(1)} %copy-done.1, ...), custom_call_target="tpu_custom_call" | custom-call | flops 2415919104 | bytes 1179648 | tf_op jit(solution)/shard_map/attend/pallas_call | solution.py:77
  19.3 0.0 copy-done.5
  19.3 3.4 %collective-permute-start.4 = (bf16[272,256]{1,0:T(8,128)(2,1)S(1)}, bf16[272,256]{1,0:T(8,128)(2,1)S(1)}, u32[]{:S(2)}, u32[]{:S(2)}) collective-permute-start(bf16[272,256]{1,0:T(8,128)(2,1)S(1)} %get-tuple-element.19), channel_id=1, source_target_pairs={{0,64},{32,96},{64,0},{96,32},{1,65},{33,97},{65,1},{97,33},{2,66}... | collective-permute-start | bytes 417800 | tf_op jit(solution)/shard_map/ppermute | solution.py:320
  22.7 0.2 collective-permute-start.5
  22.8 0.0 collective-permute-done.1.b_ref
  22.9 4.1 %collective-permute-done.4.c_ref = bf16[272,256]{1,0:T(8,128)(2,1)S(1)} collective-permute-done((bf16[272,256]{1,0:T(8,128)(2,1)S(1)}, bf16[272,256]{1,0:T(8,128)(2,1)S(1)}, u32[]{:S(2)}, u32[]{:S(2)}) %collective-permute-start.4) | collective-permute-done | bytes 139296 | tf_op jit(solution)/shard_map/ppermute | solution.py:320
  27.0 2.9 %collective-permute-done.5.d_ref = bf16[272,256]{1,0:T(8,128)(2,1)S(1)} collective-permute-done((bf16[272,256]{1,0:T(8,128)(2,1)S(1)}, bf16[272,256]{1,0:T(8,128)(2,1)S(1)}, u32[]{:S(2)}, u32[]{:S(2)}) %collective-permute-start.5) | collective-permute-done | bytes 139296 | tf_op jit(solution)/shard_map/ppermute | solution.py:320
  29.9 0.0 copy-done.10
  29.9 0.0 copy-done.11
  29.9 0.6 copy-done.12
  30.5 5.3 %project.1 = bf16[256,4096]{1,0:T(8,128)(2,1)} custom-call(bf16[272,256]{1,0:T(8,128)(2,1)} %copy-done.5, bf16[272,256]{1,0:T(8,128)(2,1)} %copy-done.10, bf16[272,256]{1,0:T(8,128)(2,1)} %copy-done.11, bf16[272,256]{1,0:T(8,128)(2,1)} %copy-done.12, bf16[256,4096]{1,0:T(8,128)(2,1)} %w_ref.1), custom_call_target="tpu_custom_call" | custom-call | flops 536870912 | bytes 4194304 | tf_op jit(solution)/shard_map/project/pallas_call | solution.py:138
  35.8 9.3 %all-to-all-start = ((bf16[32,8,4096]{2,1,0:T(8,128)(2,1)}), bf16[32,8,4096]{2,1,0:T(8,128)(2,1)S(1)}, u32[]{:S(2)}, u32[]{:S(2)}) async-start(bf16[32,8,4096]{2,1,0:T(8,128)(2,1)} %bitcast.27), calls=%async_computation | async-start | bytes 4194304 | tf_op jit(solution)/shard_map/all_to_all | solution.py:369
  45.1 0.0 copy-done.14
  45.1 0.0 copy-start.7
  45.1 0.0 copy-start.8
  45.1 0.1 reduce_sum.37
  45.2 0.0 copy-done.13
  45.2 1.3 convert_reduce_fusion
  46.6 0.1 broadcast_divide_fusion
  46.6 0.1 convert_reduce_fusion.1
  46.7 0.1 copy.24
  46.8 0.1 copy.20
  46.9 1.2 multiply_convert_fusion
  48.2 1.4 convert_element_type.55
  49.6 23.7 %all-to-all-done.arrived_ref = bf16[32,8,4096]{2,1,0:T(8,128)(2,1)S(1)} async-done(((bf16[32,8,4096]{2,1,0:T(8,128)(2,1)}), bf16[32,8,4096]{2,1,0:T(8,128)(2,1)S(1)}, u32[]{:S(2)}, u32[]{:S(2)}) %all-to-all-start) | async-done | bytes 2097184 | tf_op jit(solution)/shard_map/all_to_all | solution.py:369
  73.3 0.0 copy-done.8
  73.3 0.8 settle.1
  74.1 0.0 copy-start.4
  74.1 1.3 copy-done.4
  75.4 8.7 %all-to-all-start.1 = ((bf16[64,16,1024]{2,1,0:T(8,128)(2,1)}), bf16[64,16,1024]{2,1,0:T(8,128)(2,1)S(1)}, u32[]{:S(2)}, u32[]{:S(2)}) async-start(bf16[64,16,1024]{2,1,0:T(8,128)(2,1)} %copy-done.4), calls=%async_computation.1 | async-start | bytes 4194304 | tf_op jit(solution)/shard_map/all_to_all | solution.py:402
  84.0 11.6 %copy.27 = bf16[2,4096,2,384]{3,1,2,0:T(8,128)(2,1)} copy(bf16[2,4096,2,384]{3,2,1,0:T(2,128)(2,1)} %param.22) | data formatting | bytes 25165824 | tf_op jit(solution)/shard_map/optimization_barrier | solution.py:401
  95.6 18.0 %all-to-all-done.1.own_ref = bf16[64,16,1024]{2,1,0:T(8,128)(2,1)S(1)} async-done(((bf16[64,16,1024]{2,1,0:T(8,128)(2,1)}), bf16[64,16,1024]{2,1,0:T(8,128)(2,1)S(1)}, u32[]{:S(2)}, u32[]{:S(2)}) %all-to-all-start.1) | async-done | bytes 2097184 | tf_op jit(solution)/shard_map/all_to_all | solution.py:402
  113.6 0.0 collective-permute-start.6
  113.7 0.1 iota.141
  113.8 1.0 fusion.1
  114.8 3.1 %collective-permute-done.6.other_ref = bf16[64,16,1024]{2,1,0:T(8,128)(2,1)} collective-permute-done((bf16[64,16,1024]{2,1,0:T(8,128)(2,1)S(1)}, bf16[64,16,1024]{2,1,0:T(8,128)(2,1)}, u32[]{:S(2)}, u32[]{:S(2)}) %collective-permute-start.6) | collective-permute-done | bytes 2097184 | tf_op jit(solution)/shard_map/ppermute | solution.py:320
  117.9 0.0 copy-done.9
  117.9 20.2 %experts.1 = (bf16[64,16,1024]{2,1,0:T(8,128)(2,1)}, bf16[64,16,1024]{2,1,0:T(8,128)(2,1)}) custom-call(bf16[64,16,1024]{2,1,0:T(8,128)(2,1)} %copy-done.9, bf16[64,16,1024]{2,1,0:T(8,128)(2,1)} %collective-permute-done.6.other_ref, bf16[256,256]{1,0:T(8,128)(2,1)} %get-tuple-element.36.perm_ref, bf16[256,256]{1,0:T(8,128)(2,1)} %get-tuple-element.35.back_ref, ...), custom_call_target="tpu_custom_call" | custom-call | flops 4831838208 | bytes 18874368 | tf_op jit(solution)/shard_map/experts/pallas_call | solution.py:268
  138.2 0.1 collective-permute-start.7
  138.3 4.3 %collective-permute-done.7 = bf16[64,16,1024]{2,1,0:T(8,128)(2,1)S(1)} collective-permute-done((bf16[64,16,1024]{2,1,0:T(8,128)(2,1)}, bf16[64,16,1024]{2,1,0:T(8,128)(2,1)S(1)}, u32[]{:S(2)}, u32[]{:S(2)}) %collective-permute-start.7) | collective-permute-done | bytes 2097184 | tf_op jit(solution)/shard_map/ppermute | solution.py:320
  142.5 3.9 %add_convert_fusion = bf16[64,16,1024]{2,1,0:T(8,128)(2,1)} fusion(bf16[64,16,1024]{2,1,0:T(8,128)(2,1)S(1)} %collective-permute-done.7, bf16[64,16,1024]{2,1,0:T(8,128)(2,1)} %get-tuple-element.26), kind=kLoop, calls=%fused_computation.1 | loop fusion | flops 4194304 | bytes 6291456 | tf_op jit(solution)/shard_map/convert_element_type | solution.py:408
  146.4 6.7 %all-to-all-start.2 = ((bf16[64,16,1024]{2,1,0:T(8,128)(2,1)}), bf16[64,16,1024]{2,1,0:T(8,128)(2,1)S(1)}, u32[]{:S(2)}, u32[]{:S(2)}) async-start(bf16[64,16,1024]{2,1,0:T(8,128)(2,1)} %add_convert_fusion), calls=%async_computation.2 | async-start | bytes 4194304 | tf_op jit(solution)/shard_map/all_to_all | solution.py:409
  153.2 1.2 mul.68
  154.3 1.0 copy.21
  155.4 27.6 %all-to-all-done.2 = bf16[64,16,1024]{2,1,0:T(8,128)(2,1)S(1)} async-done(((bf16[64,16,1024]{2,1,0:T(8,128)(2,1)}), bf16[64,16,1024]{2,1,0:T(8,128)(2,1)S(1)}, u32[]{:S(2)}, u32[]{:S(2)}) %all-to-all-start.2) | async-done | bytes 2097184 | tf_op jit(solution)/shard_map/all_to_all | solution.py:409
  183.1 1.1 combine.1
  (18 shorter events, 0.1 us)
Async XLA Ops:
  0.0 5.3 %collective-permute-start = (bf16[256,256]{1,0:T(8,128)(2,1)}, bf16[256,256]{1,0:T(8,128)(2,1)S(1)}, u32[]{:S(2)}, u32[]{:S(2)}) collective-permute-start(bf16[256,256]{1,0:T(8,128)(2,1)} %qa_ref.1), channel_id=1, source_target_pairs={{0,32},{32,0},{64,96},{96,64},{1,33},{33,1},{65,97},{97,65},{2,34}... | collective-permute-start | bytes 393224 | tf_op jit(solution)/shard_map/ppermute | solution.py:320
  0.0 14.4 %collective-permute-start.3 = (bf16[256,256]{1,0:T(8,128)(2,1)}, bf16[256,256]{1,0:T(8,128)(2,1)S(1)}, u32[]{:S(2)}, u32[]{:S(2)}) collective-permute-start(bf16[256,256]{1,0:T(8,128)(2,1)} %qa_ref.1), channel_id=1, source_target_pairs={{0,96},{32,64},{64,32},{96,0},{1,97},{33,65},{65,33},{97,1},{2,98}... | collective-permute-start | bytes 393224 | tf_op jit(solution)/shard_map/ppermute | solution.py:320
  3.4 11.0 %collective-permute-start.2 = (bf16[256,256]{1,0:T(8,128)(2,1)}, bf16[256,256]{1,0:T(8,128)(2,1)S(1)}, u32[]{:S(2)}, u32[]{:S(2)}) collective-permute-start(bf16[256,256]{1,0:T(8,128)(2,1)} %qa_ref.1), channel_id=1, source_target_pairs={{0,64},{32,96},{64,0},{96,32},{1,65},{33,97},{65,1},{97,33},{2,66}... | collective-permute-start | bytes 393224 | tf_op jit(solution)/shard_map/ppermute | solution.py:320
  5.3 2.2 %copy-start = (bf16[2,2048,512]{2,1,0:T(8,128)(2,1)S(1)}, bf16[2,2048,512]{2,1,0:T(8,128)(2,1)}, u32[]{:S(2)}) copy-start(bf16[2,2048,512]{2,1,0:T(8,128)(2,1)} %vc_ref.3) | copy-start | bytes 12582916
  7.5 1.0 copy-start.2
  8.6 0.9 copy-start.6
  9.5 5.0 %copy-start.1 = (bf16[2,2048,512]{2,1,0:T(8,128)(2,1)S(1)}, bf16[2,2048,512]{2,1,0:T(8,128)(2,1)}, u32[]{:S(2)}) copy-start(bf16[2,2048,512]{2,1,0:T(8,128)(2,1)} %vc_ref.3) | copy-start | bytes 12582916
  9.5 5.0 %copy-start.3 = (bf16[2,256,512]{2,1,0:T(8,128)(2,1)S(1)}, bf16[2,256,512]{2,1,0:T(8,128)(2,1)}, u32[]{:S(2)}) copy-start(bf16[2,256,512]{2,1,0:T(8,128)(2,1)} %vn_ref.3) | copy-start | bytes 1572868
  14.3 5.0 %copy-start.5 = (bf16[272,256]{1,0:T(8,128)(2,1)}, bf16[272,256]{1,0:T(8,128)(2,1)S(1)}, u32[]{:S(2)}) copy-start(bf16[272,256]{1,0:T(8,128)(2,1)S(1)} %get-tuple-element.17.a_ref) | copy-start | bytes 417796
  14.3 8.5 %collective-permute-start.1 = (bf16[272,256]{1,0:T(8,128)(2,1)S(1)}, bf16[272,256]{1,0:T(8,128)(2,1)S(1)}, u32[]{:S(2)}, u32[]{:S(2)}) collective-permute-start(bf16[272,256]{1,0:T(8,128)(2,1)S(1)} %get-tuple-element.18), channel_id=1, source_target_pairs={{0,32},{32,0},{64,96},{96,64},{1,33},{33,1},{65,97},{97,65},{2,34}... | collective-permute-start | bytes 417800 | tf_op jit(solution)/shard_map/ppermute | solution.py:320
  19.3 7.7 %collective-permute-start.4 = (bf16[272,256]{1,0:T(8,128)(2,1)S(1)}, bf16[272,256]{1,0:T(8,128)(2,1)S(1)}, u32[]{:S(2)}, u32[]{:S(2)}) collective-permute-start(bf16[272,256]{1,0:T(8,128)(2,1)S(1)} %get-tuple-element.19), channel_id=1, source_target_pairs={{0,64},{32,96},{64,0},{96,32},{1,65},{33,97},{65,1},{97,33},{2,66}... | collective-permute-start | bytes 417800 | tf_op jit(solution)/shard_map/ppermute | solution.py:320
  22.7 7.2 %collective-permute-start.5 = (bf16[272,256]{1,0:T(8,128)(2,1)S(1)}, bf16[272,256]{1,0:T(8,128)(2,1)S(1)}, u32[]{:S(2)}, u32[]{:S(2)}) collective-permute-start(bf16[272,256]{1,0:T(8,128)(2,1)S(1)} %get-tuple-element.20), channel_id=1, source_target_pairs={{0,96},{32,64},{64,32},{96,0},{1,97},{33,65},{65,33},{97,1},{2,98}... | collective-permute-start | bytes 417800 | tf_op jit(solution)/shard_map/ppermute | solution.py:320
  22.8 7.0 %copy-start.10 = (bf16[272,256]{1,0:T(8,128)(2,1)}, bf16[272,256]{1,0:T(8,128)(2,1)S(1)}, u32[]{:S(2)}) copy-start(bf16[272,256]{1,0:T(8,128)(2,1)S(1)} %collective-permute-done.1.b_ref) | copy-start | bytes 417796
  27.0 2.9 %copy-start.11 = (bf16[272,256]{1,0:T(8,128)(2,1)}, bf16[272,256]{1,0:T(8,128)(2,1)S(1)}, u32[]{:S(2)}) copy-start(bf16[272,256]{1,0:T(8,128)(2,1)S(1)} %collective-permute-done.4.c_ref) | copy-start | bytes 417796
  29.9 0.7 copy-start.12
  35.8 9.3 %copy-start.14 = (f32[8,8]{1,0:T(8,128)S(1)}, f32[8,8]{1,0:T(8,128)}, u32[]{:S(2)}) copy-start(f32[8,8]{1,0:T(8,128)} %param.21) | copy-start | bytes 772
  35.8 9.5 %copy-start.13 = (s32[8,8]{1,0:T(8,128)S(1)}, s32[8,8]{1,0:T(8,128)}, u32[]{:S(2)}) copy-start(s32[8,8]{1,0:T(8,128)} %param.20) | copy-start | bytes 772
  35.8 37.5 %all-to-all-start = ((bf16[32,8,4096]{2,1,0:T(8,128)(2,1)}), bf16[32,8,4096]{2,1,0:T(8,128)(2,1)S(1)}, u32[]{:S(2)}, u32[]{:S(2)}) async-start(bf16[32,8,4096]{2,1,0:T(8,128)(2,1)} %bitcast.27), calls=%async_computation | async-start | bytes 4194304 | tf_op jit(solution)/shard_map/all_to_all | solution.py:369
  45.1 28.2 %copy-start.7 = (bf16[8,4096]{1,0:T(8,128)(2,1)S(1)}, bf16[8,4096]{1,0:T(8,128)(2,1)}, u32[]{:S(2)}) copy-start(bf16[8,4096]{1,0:T(8,128)(2,1)} %residual_ref.1) | copy-start | bytes 196612
  45.1 28.2 %copy-start.8 = (f32[4096]{0:T(1024)S(1)}, f32[4096]{0:T(1024)}, u32[]{:S(2)}) copy-start(f32[4096]{0:T(1024)} %param.19) | copy-start | bytes 49156
  74.1 1.3 copy-start.4
  75.4 38.3 %all-to-all-start.1 = ((bf16[64,16,1024]{2,1,0:T(8,128)(2,1)}), bf16[64,16,1024]{2,1,0:T(8,128)(2,1)S(1)}, u32[]{:S(2)}, u32[]{:S(2)}) async-start(bf16[64,16,1024]{2,1,0:T(8,128)(2,1)} %copy-done.4), calls=%async_computation.1 | async-start | bytes 4194304 | tf_op jit(solution)/shard_map/all_to_all | solution.py:402
  113.6 4.3 %copy-start.9 = (bf16[64,16,1024]{2,1,0:T(8,128)(2,1)}, bf16[64,16,1024]{2,1,0:T(8,128)(2,1)S(1)}, u32[]{:S(2)}) copy-start(bf16[64,16,1024]{2,1,0:T(8,128)(2,1)S(1)} %all-to-all-done.1.own_ref) | copy-start | bytes 6291460
  113.6 4.3 %collective-permute-start.6 = (bf16[64,16,1024]{2,1,0:T(8,128)(2,1)S(1)}, bf16[64,16,1024]{2,1,0:T(8,128)(2,1)}, u32[]{:S(2)}, u32[]{:S(2)}) collective-permute-start(bf16[64,16,1024]{2,1,0:T(8,128)(2,1)S(1)} %all-to-all-done.1.own_ref), channel_id=1, source_target_pairs={{0,32},{32,0},{1,33},{33,1},{2,34},{34,2},{3,35},{35,3},{4,36},{36... | collective-permute-start | bytes 6291464 | tf_op jit(solution)/shard_map/ppermute | solution.py:320
  138.2 4.4 %collective-permute-start.7 = (bf16[64,16,1024]{2,1,0:T(8,128)(2,1)}, bf16[64,16,1024]{2,1,0:T(8,128)(2,1)S(1)}, u32[]{:S(2)}, u32[]{:S(2)}) collective-permute-start(bf16[64,16,1024]{2,1,0:T(8,128)(2,1)} %get-tuple-element.27), channel_id=1, source_target_pairs={{0,32},{32,0},{1,33},{33,1},{2,34},{34,2},{3,35},{35,3},{4,36},{36... | collective-permute-start | bytes 6291464 | tf_op jit(solution)/shard_map/ppermute | solution.py:320
  146.4 36.6 %all-to-all-start.2 = ((bf16[64,16,1024]{2,1,0:T(8,128)(2,1)}), bf16[64,16,1024]{2,1,0:T(8,128)(2,1)S(1)}, u32[]{:S(2)}, u32[]{:S(2)}) async-start(bf16[64,16,1024]{2,1,0:T(8,128)(2,1)} %add_convert_fusion), calls=%async_computation.2 | async-start | bytes 4194304 | tf_op jit(solution)/shard_map/all_to_all | solution.py:409

commit v3 on v2

v3 whole, which is shorter than its diff:
```python
import functools
import math

import jax
import jax.numpy as jnp
import numpy as np
from jax import lax
from jax.experimental import pallas as pl
from jax.experimental.pallas import tpu as pltpu
from jax.sharding import Mesh, PartitionSpec as P

HEAD_DIM = 128
SEQ = ("yh", "core")
MP = ("x", "yl", "z")
NEG = -1e30
BF = jnp.bfloat16
F32 = jnp.float32
ANY_LAST = (((1,), (1,)), ((), ()))


def attn_kernel(first, info, qa_ref, qb_ref, kc_ref, vc_ref, kn_ref, vn_ref, oa_ref, ob_ref, s_ref):
    rows = qa_ref.shape[0]
    cache_rows = kc_ref.shape[1]
    chunk = kn_ref.shape[1]
    chunks = cache_rows // chunk
    coef = math.log2(math.e) / math.sqrt(HEAD_DIM)
    valid = info[1]
    key_pos = info[2] * rows + lax.broadcasted_iota(jnp.int32, (1, chunk), 1)
    lane = lax.broadcasted_iota(jnp.int32, (rows, 128), 1)
    column = lax.broadcasted_iota(jnp.int32, (1, chunk), 1)
    for b, (q_ref, out_ref) in enumerate(((qa_ref, oa_ref), (qb_ref, ob_ref))):
        pos = (info[2] ^ (first + b)) * rows + lax.broadcasted_iota(jnp.int32, (rows, 1), 0)
        limit = pos
        for a in range(3):
            start, end = info[3 + 2 * a], info[4 + 2 * a]
            limit = jnp.where((pos >= start) & (pos < end), jnp.maximum(limit, end - 1), limit)
        tract_ok = key_pos <= limit
        stats = jnp.zeros((rows, 128), F32)
        for h in range(2):
            at = 2 * b + h
            q = q_ref[:, h * HEAD_DIM : (h + 1) * HEAD_DIM]
            top = None
            for c in range(chunks + 1):
                if c < chunks:
                    k = kc_ref[0, c * chunk : (c + 1) * chunk, :]
                    s = lax.dot_general(q, k, ANY_LAST, preferred_element_type=F32)
                    s = s + jnp.where(column < valid - c * chunk, 0.0, NEG)
                else:
                    s = lax.dot_general(q, kn_ref[0], ANY_LAST, preferred_element_type=F32)
                    s = jnp.where(tract_ok, s, NEG)
                s_ref[at, :, c * chunk : (c + 1) * chunk] = s
                top = s if top is None else jnp.maximum(top, s)
            m = jnp.max(top, axis=1, keepdims=True) * coef
            total = None
            acc = None
            for c in range(chunks + 1):
                p = jnp.exp2(s_ref[at, :, c * chunk : (c + 1) * chunk] * coef - m)
                total = p if total is None else total + p
                v = vc_ref[0, c * chunk : (c + 1) * chunk, :] if c < chunks else vn_ref[0]
                part = jnp.dot(p.astype(BF), v, preferred_element_type=F32)
                acc = part if acc is None else acc + part
            total = jnp.sum(total, axis=1, keepdims=True)
            out_ref[0:rows, h * HEAD_DIM : (h + 1) * HEAD_DIM] = (acc / total).astype(BF)
            level = m + jnp.log2(total)
            for part in range(3):
                piece = level.astype(BF).astype(F32)
                level = level - piece
                stats = jnp.where(lane == 3 * h + part, piece, stats)
        out_ref[rows : rows + 16, :] = stats.T[0:16, :].astype(BF)


def attend(first, info, qa, qb, cache_kv, new_kv):
    rows = qa.shape[0]
    cache_rows, new_rows = cache_kv.shape[1], new_kv.shape[1]
    keys = cache_rows + new_rows
    whole = pl.BlockSpec((rows, 2 * HEAD_DIM), lambda i, t: (0, 0))
    result = pl.BlockSpec((rows + 16, 2 * HEAD_DIM), lambda i, t: (0, 0))
    shape = jax.ShapeDtypeStruct((rows + 16, 2 * HEAD_DIM), BF)
    return pl.pallas_call(
        functools.partial(attn_kernel, first),
        grid_spec=pltpu.PrefetchScalarGridSpec(
            num_scalar_prefetch=1,
            grid=(1,),
            in_specs=[
                whole,
                whole,
                pl.BlockSpec((1, cache_rows, HEAD_DIM), lambda i, t: (0, 0, t[0])),
                pl.BlockSpec((1, cache_rows, HEAD_DIM), lambda i, t: (1, 0, t[0])),
                pl.BlockSpec((1, new_rows, HEAD_DIM), lambda i, t: (0, 0, t[0])),
                pl.BlockSpec((1, new_rows, HEAD_DIM), lambda i, t: (1, 0, t[0])),
            ],
            out_specs=[result, result],
            scratch_shapes=[pltpu.VMEM((4, rows, keys), F32)],
        ),
        out_shape=[shape, shape],
        compiler_params=pltpu.CompilerParams(vmem_limit_bytes=20 << 20),
        cost_estimate=pl.CostEstimate(
            flops=32 * rows * keys * HEAD_DIM,
            bytes_accessed=4 * keys * HEAD_DIM,
            transcendentals=4 * rows * keys,
        ),
        name="attend",
    )(info, qa, qb, cache_kv, cache_kv, new_kv, new_kv)


def project_kernel(a_ref, b_ref, c_ref, d_ref, w_ref, out_ref, att_ref):
    parts = (a_ref, b_ref, c_ref, d_ref)
    rows = out_ref.shape[0]
    pad = jnp.zeros((112, rows), F32)
    stats = [
        jnp.concatenate([p[rows : rows + 16, :].astype(F32), pad], axis=0).T for p in parts
    ]
    for h in range(2):
        cols = slice(h * HEAD_DIM, (h + 1) * HEAD_DIM)
        at = 3 * h
        levels = [
            t[:, at : at + 1] + t[:, at + 1 : at + 2] + t[:, at + 2 : at + 3] for t in stats
        ]
        best = jnp.maximum(
            jnp.maximum(levels[0], levels[1]), jnp.maximum(levels[2], levels[3])
        )
        weights = [jnp.exp2(v - best) for v in levels]
        total = weights[0] + weights[1] + weights[2] + weights[3]
        acc = None
        for w, p in zip(weights, parts):
            term = p[0:rows, cols].astype(F32) * w
            acc = term if acc is None else acc + term
        att_ref[:, cols] = (acc / total).astype(BF)
    out_ref[...] = jnp.dot(att_ref[...], w_ref[...], preferred_element_type=F32).astype(BF)


def project(parts, out_proj):
    rows, depth = parts[0].shape[0] - 16, parts[0].shape[1]
    width = out_proj.shape[1]
    return pl.pallas_call(
        project_kernel,
        in_specs=[pl.BlockSpec(memory_space=pltpu.VMEM)] * 5,
        out_specs=pl.BlockSpec(memory_space=pltpu.VMEM),
        out_shape=jax.ShapeDtypeStruct((rows, width), BF),
        scratch_shapes=[pltpu.VMEM((rows, depth), BF)],
        compiler_params=pltpu.CompilerParams(vmem_limit_bytes=16 << 20),
        cost_estimate=pl.CostEstimate(
            flops=2 * rows * depth * width, bytes_accessed=4 * depth * width, transcendentals=0
        ),
        name="project",
    )(*parts, out_proj)


def settle_kernel(arrived_ref, residual_ref, gain_ref, pick_ref, stream_ref, out_ref):
    tok, width = residual_ref.shape
    groups = arrived_ref.shape[0]
    chunk = out_ref.shape[2]
    chunks = width // chunk
    pieces = []
    square = None
    for c in range(chunks):
        cols = slice(c * chunk, (c + 1) * chunk)
        acc = arrived_ref[0, :, cols].astype(F32)
        for g in range(1, groups):
            acc = acc + arrived_ref[g, :, cols].astype(F32)
        stream = (residual_ref[:, cols].astype(F32) + acc).astype(BF)
        stream_ref[:, cols] = stream
        piece = stream.astype(F32)
        pieces.append(piece)
        term = jnp.sum(piece * piece, axis=1, keepdims=True)
        square = term if square is None else square + term
    scale = lax.rsqrt(square * (1.0 / width) + 1e-6)
    normed = [
        p * scale * gain_ref[:, c * chunk : (c + 1) * chunk] for c, p in enumerate(pieces)
    ]
    stacked = jnp.concatenate(normed, axis=0).astype(BF)
    rows = jnp.dot(pick_ref[...], stacked, preferred_element_type=F32).astype(BF)
    half = out_ref.shape[0] // 2
    rows = rows.reshape(half, 16, chunk)
    out_ref[0:half] = rows
    out_ref[half : 2 * half] = rows


def settle(arrived, residual, gain, pick):
    tok, width = residual.shape
    chunk = width // 4
    return pl.pallas_call(
        settle_kernel,
        out_shape=[
            jax.ShapeDtypeStruct((tok, width), BF),
            jax.ShapeDtypeStruct((pick.shape[0] // 8, 16, chunk), BF),
        ],
        compiler_params=pltpu.CompilerParams(vmem_limit_bytes=20 << 20),
        cost_estimate=pl.CostEstimate(
            flops=1 << 26, bytes_accessed=4 << 20, transcendentals=0
        ),
        name="settle",
    )(arrived, residual, gain.reshape(1, width), pick)


def expert_kernel(rows_ref, perm_ref, back_ref, win_ref, wout_ref, out_ref, x_ref, z_ref):
    chunk = rows_ref.shape[2]
    chunks = 4
    sources = rows_ref.shape[0]
    ff = wout_ref.shape[1]
    pieces = [(e, c) for e in range(2) for c in range(chunks)]
    for g in range(sources // 16):
        block = rows_ref[16 * g : 16 * g + 16].reshape(256, chunk)
        y = jnp.dot(perm_ref[...], block, preferred_element_type=F32).astype(BF)
        for i, (e, c) in enumerate(pieces):
            x_ref[e, g * 32 : g * 32 + 32, c * chunk : (c + 1) * chunk] = y[32 * i : 32 * i + 32]
    for e in range(2):
        both = jnp.concatenate([win_ref[e, 0], win_ref[e, 1]], axis=1)
        hidden = jnp.dot(x_ref[e], both, preferred_element_type=F32)
        gate, up = hidden[:, :ff], hidden[:, ff:]
        act = (gate / (1.0 + jnp.exp(-gate)) * up).astype(BF)
        z_ref[e] = jnp.dot(act, wout_ref[e], preferred_element_type=F32).astype(BF)
    for g in range(sources // 16):
        block = jnp.concatenate(
            [z_ref[e, g * 32 : g * 32 + 32, c * chunk : (c + 1) * chunk] for e, c in pieces],
            axis=0,
        )
        y = jnp.dot(back_ref[...], block, preferred_element_type=F32).astype(BF)
        out_ref[16 * g : 16 * g + 16] = y.reshape(16, 16, chunk)


def experts(rows, perm, back, w_in, w_out):
    sources, _, chunk = rows.shape
    width = 4 * chunk
    ff = w_out.shape[1]
    count = 2 * sources
    return pl.pallas_call(
        expert_kernel,
        in_specs=[pl.BlockSpec(memory_space=pltpu.VMEM)] * 5,
        out_specs=pl.BlockSpec(memory_space=pltpu.VMEM),
        out_shape=jax.ShapeDtypeStruct(rows.shape, BF),
        scratch_shapes=[
            pltpu.VMEM((2, count, width), BF),
            pltpu.VMEM((2, count, width), BF),
        ],
        compiler_params=pltpu.CompilerParams(vmem_limit_bytes=16 << 20),
        cost_estimate=pl.CostEstimate(
            flops=12 * count * width * ff,
            bytes_accessed=12 * width * ff,
            transcendentals=2 * count * ff,
        ),
        name="experts",
    )(rows, perm, back, w_in, w_out)


def combine_kernel(share_ref, returned_ref, stream_ref, out_ref):
    tok = stream_ref.shape[0]
    chunk = returned_ref.shape[1]
    both = jnp.dot(share_ref[...], returned_ref[...], preferred_element_type=F32)
    half = both.shape[0] // 2
    total = both[:half] + both[half:]
    for c in range(half // tok):
        cols = slice(c * chunk, (c + 1) * chunk)
        out_ref[:, cols] = (
            stream_ref[:, cols].astype(F32) + total[c * tok : (c + 1) * tok]
        ).astype(BF)


def combine(share, returned, stream):
    return pl.pallas_call(
        combine_kernel,
        out_shape=jax.ShapeDtypeStruct(stream.shape, BF),
        compiler_params=pltpu.CompilerParams(vmem_limit_bytes=20 << 20),
        name="combine",
    )(share, returned, stream)


def swap(v, axes, bit):
    count = 4 if len(axes) == 2 else 2
    return lax.ppermute(v, axes, [(i, i ^ bit) for i in range(count)])


def local(
    queries,
    new_kv,
    cache_kv,
    cached_len,
    image_spans,
    residual,
    out_proj,
    norm_gain,
    routes,
    gate_weights,
    w_in,
    w_out,
):
    seq = lax.axis_index(SEQ)
    tract = queries.shape[0]
    cache = cache_kv.shape[1]
    tok = residual.shape[0]
    width = residual.shape[1]
    quarter = width // 4
    spread = ("yh",) + MP

    query_parts = [queries] + [swap(queries, SEQ, d) for d in (1, 2, 3)]
    valid = jnp.clip(cached_len[0] - seq * cache, 0, cache)

    place = jnp.stack([lax.axis_index("x"), valid, seq]).astype(jnp.int32)
    info = jnp.concatenate([place, image_spans.reshape(-1)])

    def attend_pair(d):
        return attend(d, info, query_parts[d], query_parts[d + 1], cache_kv, new_kv)

    mine, beside = attend_pair(0)
    across, diagonal = attend_pair(2)
    parts = [mine, swap(beside, SEQ, 1), swap(across, SEQ, 2), swap(diagonal, SEQ, 3)]
    partial = project(parts, out_proj)
    partial, routes, gate_weights, w_in = lax.optimization_barrier(
        (partial, routes, gate_weights, w_in)
    )
    arrived = lax.all_to_all(
        partial.reshape(32, tok, width), MP, split_axis=0, concat_axis=0, tiled=True
    )
    turned = w_in.transpose(0, 2, 1, 3)

    gate_share = gate_weights / jnp.sum(gate_weights, axis=1, keepdims=True)
    top = routes.shape[1]
    same = routes[:, :, None, None] == routes[None, None, :, :]
    earlier = jnp.arange(tok)[:, None] > jnp.arange(tok)[None, :]
    rank = jnp.sum((same & earlier[:, None, :, None]).astype(jnp.int32), axis=(2, 3))
    slot = routes * 2 + rank
    pairs = 32
    placement = slot[:, :, None] == jnp.arange(pairs * 4, dtype=jnp.int32)[None, None, :]
    chosen = jnp.sum(placement.astype(F32), axis=1)
    weighed = jnp.sum(jnp.where(placement, gate_share[:, :, None], 0.0), axis=1)
    eye = jnp.eye(4, dtype=F32)

    def spread_rows(v):
        wide = v.reshape(1, tok, pairs, 1, 4) * eye.reshape(4, 1, 1, 4, 1)
        return wide.reshape(4 * tok, pairs * 16)

    pick = spread_rows(chosen).astype(BF).T
    share = spread_rows(weighed)
    coarse = share.astype(BF)
    fine = (share - coarse.astype(F32)).astype(BF)
    share = jnp.concatenate([coarse, fine], axis=0)
    share = jnp.concatenate([share, share], axis=1)

    perm = np.eye(256).reshape(16, 4, 2, 2, 256).transpose(2, 1, 0, 3, 4).reshape(256, 256)
    perm, back = jnp.asarray(perm, BF), jnp.asarray(perm.T, BF)

    arrived, pick, share, turned = lax.optimization_barrier((arrived, pick, share, turned))
    stream, outgoing = settle(arrived, residual, norm_gain, pick)

    own = lax.all_to_all(outgoing, spread, split_axis=0, concat_axis=0, tiled=True)
    other = swap(own, ("core",), 1)
    kept = experts(own, perm, back, turned, w_out)
    kept, other = lax.optimization_barrier((kept, other))
    sent = experts(other, perm, back, turned, w_out)
    got = swap(sent, ("core",), 1)
    summed = (kept.astype(F32) + got.astype(F32)).astype(BF)
    returned = lax.all_to_all(summed, spread, split_axis=0, concat_axis=0, tiled=True)
    return combine(share, returned.reshape(-1, quarter), stream)


def solution(mesh):
    fine = Mesh(mesh.devices.reshape(2, 2, 4, 2, 4), SEQ + MP)
    in_specs = (
        P(SEQ, MP),
        P(None, SEQ, None),
        P(None, SEQ, None),
        P(),
        P(),
        P(SEQ + MP, None),
        P(MP, None),
        P(),
        P(SEQ + MP, None),
        P(SEQ + MP, None),
        P(MP, None, None, SEQ),
        P(MP, SEQ, None),
    )
    return jax.shard_map(
        local, mesh=fine, in_specs=in_specs, out_specs=P(SEQ + MP, None), check_vma=False
    )
```

time: 185 us -> 168 us (0.908)
  blocking collectives: 0 us -> 74.6 us
  waiting for transfers between devices: 83.8 us -> 21.7 us
  starting transfers between devices: 32 us -> 16.6 us
  Pallas kernels: 37.1 us -> 24.1 us
  other arithmetic: 7.74 us -> 4.06 us
  local copies, waits for them, and re-layouts: 22.7 us -> 25.2 us
    all_to_all x0 -> x2, blocking collectives: none -> 74.6 us  [the longest x1 38 us: local(): lax.all_to_all(outgoing, spread, split_axis=0, concat_axis=0, tiled=True)]
    all_to_all x2 -> x0, waiting for transfers between devices: 45.6 us -> none  [the longest x1 27.6 us: local(): lax.all_to_all(summed, spread, split_axis=0, concat_axis=0, tiled=True)]
    all_to_all x2 -> x0, starting transfers between devices: 15.4 us -> none  [the longest x1 8.66 us: local(): lax.all_to_all(outgoing, spread, split_axis=0, concat_axis=0, tiled=True)]
    pallas_call x4 -> x5, Pallas kernels: 35.2 us -> 22.2 us  [the longest x2 9.74 us: attend(): pl.pallas_call(functools.partial(attn_kernel, first), grid_spec=pltpu.Pre...]
    all_to_all x1, waiting for transfers between devices: 23.7 us -> 11.7 us  [local(): lax.all_to_all(partial.reshape(32, tok, width), MP, split_axis=0, concat_...]
    unnamed x31 -> x29, local copies, waits for them, and re-layouts: 6.9 us -> 11.4 us
    ppermute x8, waiting for transfers between devices: 14.4 us -> 10.1 us  [swap(): return lax.ppermute(v, axes, [(i, i ^ bit) for i in range(count)])]
    convert_element_type x1, other arithmetic: 3.89 us -> 1.13 us  [local(): summed = (kept.astype(F32) + got.astype(F32)).astype(BF)]
  transfers between devices with their start and end apart: 11 -> 9, of which waited for: 7 -> 6; matrix products, arithmetic and copies ran while one was open for 11% -> 10% of each run, Pallas kernels for 5% -> 9%
where the time goes in v3:
time: 168 us; the launch traced here: 167 us
  blocking collectives  74.6 us (44%)
  local copies, waits for them, and re-layouts  25.2 us (15%)
  Pallas kernels  24.1 us (14%)
  waiting for transfers between devices  21.7 us (13%)
  starting transfers between devices  16.6 us (10%)
  other arithmetic  4.06 us (2%)
    all_to_all x1, blocking collectives, local(): lax.all_to_all(outgoing, spread, split_axis=0, concat_axis=0, tiled=True)  38 us
    all_to_all x1, blocking collectives, local(): lax.all_to_all(summed, spread, split_axis=0, concat_axis=0, tiled=True)  36.6 us
    all_to_all x1, waiting for transfers between devices, local(): lax.all_to_all(partial.reshape(32, tok, width), MP, split_axis=0, concat_...  11.7 us
    optimization_barrier x1, local copies, waits for them, and re-layouts, local(): lax.optimization_barrier((partial, routes, gate_weights, w_in))  11.6 us
    unnamed x29, local copies, waits for them, and re-layouts  11.4 us
    ppermute x8, waiting for transfers between devices, swap(): return lax.ppermute(v, axes, [(i, i ^ bit) for i in range(count)])  10.1 us
    pallas_call x2, Pallas kernels, attend(): pl.pallas_call(functools.partial(attn_kernel, first), grid_spec=pltpu.Pre...  9.74 us
    pallas_call x2, Pallas kernels, experts(): pl.pallas_call(expert_kernel, in_specs=[pl.BlockSpec(memory_space=pltpu.V...  9.59 us
  transfers between devices with their start and end apart: 9, of which 6 were waited for; matrix products, arithmetic and copies ran while one was open for 10% of the time, Pallas kernels for 9%

profile of v3, /device:TPU:0, one launch (start us, length us, event | category | flops | bytes accessed | tf_op | source)
XLA Modules:
  0.0 167.2 jit_solution(2919447453811567006)
XLA Ops:
  0.0 3.3 %collective-permute-start.2 = (bf16[256,256]{1,0:T(8,128)(2,1)}, bf16[256,256]{1,0:T(8,128)(2,1)S(1)}, u32[]{:S(2)}, u32[]{:S(2)}) collective-permute-start(bf16[256,256]{1,0:T(8,128)(2,1)} %qa_ref.1), channel_id=1, source_target_pairs={{0,64},{32,96},{64,0},{96,32},{1,65},{33,97},{65,1},{97,33},{2,66}... | collective-permute-start | bytes 393224 | tf_op jit(solution)/shard_map/ppermute | solution.py:270
  3.3 0.0 collective-permute-start.3
  3.3 0.4 collective-permute-start
  4.3 0.8 copy.22
  5.1 0.1 reshape.52
  5.2 0.1 pad_add_fusion.info
  5.2 2.3 %collective-permute-done.2.qa_ref = bf16[256,256]{1,0:T(8,128)(2,1)S(1)} collective-permute-done((bf16[256,256]{1,0:T(8,128)(2,1)}, bf16[256,256]{1,0:T(8,128)(2,1)S(1)}, u32[]{:S(2)}, u32[]{:S(2)}) %collective-permute-start.2) | collective-permute-done | bytes 131104 | tf_op jit(solution)/shard_map/ppermute | solution.py:270
  7.5 3.0 %collective-permute-done.3.qb_ref = bf16[256,256]{1,0:T(8,128)(2,1)S(1)} collective-permute-done((bf16[256,256]{1,0:T(8,128)(2,1)}, bf16[256,256]{1,0:T(8,128)(2,1)S(1)}, u32[]{:S(2)}, u32[]{:S(2)}) %collective-permute-start.3) | collective-permute-done | bytes 131104 | tf_op jit(solution)/shard_map/ppermute | solution.py:270
  10.5 0.0 copy-start.2
  10.5 2.2 %copy-done.2 = bf16[2,2048,512]{2,1,0:T(8,128)(2,1)S(1)} copy-done((bf16[2,2048,512]{2,1,0:T(8,128)(2,1)S(1)}, bf16[2,2048,512]{2,1,0:T(8,128)(2,1)}, u32[]{:S(2)}) %copy-start.2) | copy-done | bytes 4194328
  12.7 0.0 copy-start.5
  12.7 1.0 copy-done.5
  13.8 0.0 copy-start.3
  13.8 4.9 %attend.3 = (bf16[272,256]{1,0:T(8,128)(2,1)S(1)}, bf16[272,256]{1,0:T(8,128)(2,1)S(1)}) custom-call(s32[9]{0:T(128)S(1)} %pad_add_fusion.info, bf16[256,256]{1,0:T(8,128)(2,1)S(1)} %collective-permute-done.2.qa_ref, bf16[256,256]{1,0:T(8,128)(2,1)S(1)} %collective-permute-done.3.qb_ref, bf16[2,2048,512]{2,1,0:T(8,128)(2,1)S(1)} %copy-done.2, ...), custom_call_target="tpu_custom_call" | custom-call | flops 2415919104 | bytes 1179648 | tf_op jit(solution)/shard_map/attend/pallas_call | solution.py:79
  18.6 1.4 collective-permute-start.4
  20.1 1.3 collective-permute-start.5
  21.4 0.0 collective-permute-done.qb_ref
  21.4 0.0 copy-done.3
  21.4 0.0 copy-done.9
  21.4 4.9 %attend.2 = (bf16[272,256]{1,0:T(8,128)(2,1)S(1)}, bf16[272,256]{1,0:T(8,128)(2,1)S(1)}) custom-call(s32[9]{0:T(128)S(1)} %pad_add_fusion.info, bf16[256,256]{1,0:T(8,128)(2,1)S(1)} %copy-done.9, bf16[256,256]{1,0:T(8,128)(2,1)S(1)} %collective-permute-done.qb_ref, bf16[2,2048,512]{2,1,0:T(8,128)(2,1)S(1)} %copy-done.3, bf16[2,2048,512]{2,1,0:T(8,128)(2,1)S(1)} %copy-done.3, ...), custom_call_target="tpu_custom_call" | custom-call | flops 2415919104 | bytes 1179648 | tf_op jit(solution)/shard_map/attend/pallas_call | solution.py:79
  26.3 1.0 collective-permute-start.1
  27.3 0.0 collective-permute-done.4.c_ref
  27.3 0.2 collective-permute-done.5.d_ref
  27.5 0.8 collective-permute-done.1.b_ref
  28.3 0.0 copy-done.6
  28.3 2.9 %project.1 = bf16[256,4096]{1,0:T(8,128)(2,1)} custom-call(bf16[272,256]{1,0:T(8,128)(2,1)S(1)} %get-tuple-element.21.a_ref, bf16[272,256]{1,0:T(8,128)(2,1)S(1)} %collective-permute-done.1.b_ref, bf16[272,256]{1,0:T(8,128)(2,1)S(1)} %collective-permute-done.4.c_ref, bf16[272,256]{1,0:T(8,128)(2,1)S(1)} %collective-permute-done.5.d_ref, ...), custom_call_target="tpu_custom_call" | custom-call | flops 536870912 | bytes 4194304 | tf_op jit(solution)/shard_map/project/pallas_call | solution.py:135
  31.2 8.6 %all-to-all-start = ((bf16[32,8,4096]{2,1,0:T(8,128)(2,1)}), bf16[32,8,4096]{2,1,0:T(8,128)(2,1)S(1)}, u32[]{:S(2)}, u32[]{:S(2)}) async-start(bf16[32,8,4096]{2,1,0:T(8,128)(2,1)} %bitcast.4), calls=%async_computation | async-start | bytes 4194304 | tf_op jit(solution)/shard_map/all_to_all | solution.py:311
  39.8 0.0 copy-done.13
  39.8 0.1 reduce_sum.38
  39.9 0.0 copy-done.12
  39.9 1.3 convert_reduce_fusion
  41.2 0.1 broadcast_divide_fusion
  41.3 0.1 select_reduce_fusion
  41.4 0.1 copy.23
  41.5 0.1 copy.24
  41.6 1.2 broadcast_multiply_fusion
  42.9 0.5 mul.59
  43.3 0.1 copy.25
  43.4 1.4 convert_element_type.43
  44.8 0.0 copy-start.10
  44.8 0.0 copy-start.11
  44.8 11.6 %copy.29 = bf16[2,4096,2,384]{3,1,2,0:T(8,128)(2,1)} copy(bf16[2,4096,2,384]{3,2,1,0:T(2,128)(2,1)} %param.24) | data formatting | bytes 25165824 | tf_op jit(solution)/shard_map/optimization_barrier | solution.py:308
  56.5 11.7 %all-to-all-done.arrived_ref = bf16[32,8,4096]{2,1,0:T(8,128)(2,1)S(1)} async-done(((bf16[32,8,4096]{2,1,0:T(8,128)(2,1)}), bf16[32,8,4096]{2,1,0:T(8,128)(2,1)S(1)}, u32[]{:S(2)}, u32[]{:S(2)}) %all-to-all-start) | async-done | bytes 2097184 | tf_op jit(solution)/shard_map/all_to_all | solution.py:311
  68.1 0.0 copy-done.10
  68.1 0.0 copy-done.11
  68.1 0.8 settle.1
  68.9 0.0 copy-start.7
  68.9 0.0 copy-start.8
  69.0 38.0 %all_to_all.15.rows_ref = bf16[64,16,1024]{2,1,0:T(8,128)(2,1)S(1)} all-to-all(bf16[64,16,1024]{2,1,0:T(8,128)(2,1)S(1)} %get-tuple-element.32), channel_id=1, replica_groups=mesh['yh'=2,'core'=2,'x'=4,'yl'=2,'z'=4] {'yh','x','yl','z'}, dimensions={0} | all-to-all | bytes 4194304 | tf_op jit(solution)/shard_map/all_to_all | solution.py:345
  107.0 0.0 collective-permute-start.6
  107.0 0.0 copy-done.7
  107.0 0.0 copy-done.8
  107.0 0.0 copy-start
  107.0 4.6 %copy-done = bf16[2,4096,2,384]{3,1,2,0:T(8,128)(2,1)S(1)} copy-done((bf16[2,4096,2,384]{3,1,2,0:T(8,128)(2,1)S(1)}, bf16[2,4096,2,384]{3,1,2,0:T(8,128)(2,1)}, u32[]{:S(2)}) %copy-start) | copy-done | bytes 12582936
  111.5 2.8 %copy-done.4 = bf16[2,384,4096]{2,1,0:T(8,128)(2,1)S(1)} copy-done((bf16[2,384,4096]{2,1,0:T(8,128)(2,1)S(1)}, bf16[2,384,4096]{2,1,0:T(8,128)(2,1)}, u32[]{:S(2)}) %copy-start.4) | copy-done | bytes 6291480
  114.3 4.8 %experts.2 = bf16[64,16,1024]{2,1,0:T(8,128)(2,1)S(1)} custom-call(bf16[64,16,1024]{2,1,0:T(8,128)(2,1)S(1)} %all_to_all.15.rows_ref, bf16[256,256]{1,0:T(8,128)(2,1)S(1)} %copy-done.7, bf16[256,256]{1,0:T(8,128)(2,1)S(1)} %copy-done.8, bf16[2,2,4096,384]{3,2,1,0:T(8,128)(2,1)S(1)} %bitcast.18, bf16[2,384,4096]{2,1,0:T(8,128)(2,1)S(1)} %copy-done.4), custom_call_target="tpu_custom_call" | custom-call | flops 2415919104 | bytes 18874368 | tf_op jit(solution)/shard_map/experts/pallas_call | solution.py:227
  119.1 0.0 collective-permute-done.6.rows_ref
  119.1 0.0 copy-done.1
  119.2 4.8 %experts.3 = bf16[64,16,1024]{2,1,0:T(8,128)(2,1)S(1)} custom-call(bf16[64,16,1024]{2,1,0:T(8,128)(2,1)S(1)} %collective-permute-done.6.rows_ref, bf16[256,256]{1,0:T(8,128)(2,1)S(1)} %copy-done.7, bf16[256,256]{1,0:T(8,128)(2,1)S(1)} %copy-done.8, bf16[2,2,4096,384]{3,2,1,0:T(8,128)(2,1)S(1)} %bitcast.19, bf16[2,384,4096]{2,1,0:T(8,128)(2,1)S(1)} %copy-done.4), custom_call_target="tpu_custom_call" | custom-call | flops 2415919104 | bytes 18874368 | tf_op jit(solution)/shard_map/experts/pallas_call | solution.py:227
  124.0 0.6 collective-permute-start.7
  124.5 3.8 %collective-permute-done.7 = bf16[64,16,1024]{2,1,0:T(8,128)(2,1)S(1)} collective-permute-done((bf16[64,16,1024]{2,1,0:T(8,128)(2,1)S(1)}, bf16[64,16,1024]{2,1,0:T(8,128)(2,1)S(1)}, u32[]{:S(2)}, u32[]{:S(2)}) %collective-permute-start.7) | collective-permute-done | bytes 2097184 | tf_op jit(solution)/shard_map/ppermute | solution.py:270
  128.3 1.1 add_convert_fusion
  129.5 36.6 %all_to_all.16 = bf16[64,16,1024]{2,1,0:T(8,128)(2,1)S(1)} all-to-all(bf16[64,16,1024]{2,1,0:T(8,128)(2,1)S(1)} %add_convert_fusion), channel_id=1, replica_groups=mesh['yh'=2,'core'=2,'x'=4,'yl'=2,'z'=4] {'yh','x','yl','z'}, dimensions={0} | all-to-all | bytes 4194304 | tf_op jit(solution)/shard_map/all_to_all | solution.py:352
  166.1 1.1 combine.1
  (11 shorter events, 0.0 us)
Async XLA Ops:
  0.0 7.5 %collective-permute-start.2 = (bf16[256,256]{1,0:T(8,128)(2,1)}, bf16[256,256]{1,0:T(8,128)(2,1)S(1)}, u32[]{:S(2)}, u32[]{:S(2)}) collective-permute-start(bf16[256,256]{1,0:T(8,128)(2,1)} %qa_ref.1), channel_id=1, source_target_pairs={{0,64},{32,96},{64,0},{96,32},{1,65},{33,97},{65,1},{97,33},{2,66}... | collective-permute-start | bytes 393224 | tf_op jit(solution)/shard_map/ppermute | solution.py:270
  3.3 7.2 %collective-permute-start.3 = (bf16[256,256]{1,0:T(8,128)(2,1)}, bf16[256,256]{1,0:T(8,128)(2,1)S(1)}, u32[]{:S(2)}, u32[]{:S(2)}) collective-permute-start(bf16[256,256]{1,0:T(8,128)(2,1)} %qa_ref.1), channel_id=1, source_target_pairs={{0,96},{32,64},{64,32},{96,0},{1,97},{33,65},{65,33},{97,1},{2,98}... | collective-permute-start | bytes 393224 | tf_op jit(solution)/shard_map/ppermute | solution.py:270
  3.3 18.1 %collective-permute-start = (bf16[256,256]{1,0:T(8,128)(2,1)}, bf16[256,256]{1,0:T(8,128)(2,1)S(1)}, u32[]{:S(2)}, u32[]{:S(2)}) collective-permute-start(bf16[256,256]{1,0:T(8,128)(2,1)} %qa_ref.1), channel_id=1, source_target_pairs={{0,32},{32,0},{64,96},{96,64},{1,33},{33,1},{65,97},{97,65},{2,34}... | collective-permute-start | bytes 393224 | tf_op jit(solution)/shard_map/ppermute | solution.py:270
  10.5 2.2 %copy-start.2 = (bf16[2,2048,512]{2,1,0:T(8,128)(2,1)S(1)}, bf16[2,2048,512]{2,1,0:T(8,128)(2,1)}, u32[]{:S(2)}) copy-start(bf16[2,2048,512]{2,1,0:T(8,128)(2,1)} %vc_ref.3) | copy-start | bytes 12582916
  12.7 1.0 copy-start.5
  13.8 7.7 %copy-start.3 = (bf16[2,2048,512]{2,1,0:T(8,128)(2,1)S(1)}, bf16[2,2048,512]{2,1,0:T(8,128)(2,1)}, u32[]{:S(2)}) copy-start(bf16[2,2048,512]{2,1,0:T(8,128)(2,1)} %vc_ref.3) | copy-start | bytes 12582916
  13.8 7.7 %copy-start.9 = (bf16[256,256]{1,0:T(8,128)(2,1)S(1)}, bf16[256,256]{1,0:T(8,128)(2,1)}, u32[]{:S(2)}) copy-start(bf16[256,256]{1,0:T(8,128)(2,1)} %qa_ref.1) | copy-start | bytes 393220
  18.6 8.7 %collective-permute-start.4 = (bf16[272,256]{1,0:T(8,128)(2,1)S(1)}, bf16[272,256]{1,0:T(8,128)(2,1)S(1)}, u32[]{:S(2)}, u32[]{:S(2)}) collective-permute-start(bf16[272,256]{1,0:T(8,128)(2,1)S(1)} %get-tuple-element.23), channel_id=1, source_target_pairs={{0,64},{32,96},{64,0},{96,32},{1,65},{33,97},{65,1},{97,33},{2,66}... | collective-permute-start | bytes 417800 | tf_op jit(solution)/shard_map/ppermute | solution.py:270
  20.1 8.3 %copy-start.6 = (bf16[256,4096]{1,0:T(8,128)(2,1)S(1)}, bf16[256,4096]{1,0:T(8,128)(2,1)}, u32[]{:S(2)}) copy-start(bf16[256,4096]{1,0:T(8,128)(2,1)} %w_ref.1) | copy-start | bytes 6291460
  20.1 7.4 %collective-permute-start.5 = (bf16[272,256]{1,0:T(8,128)(2,1)S(1)}, bf16[272,256]{1,0:T(8,128)(2,1)S(1)}, u32[]{:S(2)}, u32[]{:S(2)}) collective-permute-start(bf16[272,256]{1,0:T(8,128)(2,1)S(1)} %get-tuple-element.24), channel_id=1, source_target_pairs={{0,96},{32,64},{64,32},{96,0},{1,97},{33,65},{65,33},{97,1},{2,98}... | collective-permute-start | bytes 417800 | tf_op jit(solution)/shard_map/ppermute | solution.py:270
  26.3 2.0 %collective-permute-start.1 = (bf16[272,256]{1,0:T(8,128)(2,1)S(1)}, bf16[272,256]{1,0:T(8,128)(2,1)S(1)}, u32[]{:S(2)}, u32[]{:S(2)}) collective-permute-start(bf16[272,256]{1,0:T(8,128)(2,1)S(1)} %get-tuple-element.22), channel_id=1, source_target_pairs={{0,32},{32,0},{64,96},{96,64},{1,33},{33,1},{65,97},{97,65},{2,34}... | collective-permute-start | bytes 417800 | tf_op jit(solution)/shard_map/ppermute | solution.py:270
  31.2 8.6 %copy-start.13 = (f32[8,8]{1,0:T(8,128)S(1)}, f32[8,8]{1,0:T(8,128)}, u32[]{:S(2)}) copy-start(f32[8,8]{1,0:T(8,128)} %param.23) | copy-start | bytes 772
  31.2 8.7 %copy-start.12 = (s32[8,8]{1,0:T(8,128)S(1)}, s32[8,8]{1,0:T(8,128)}, u32[]{:S(2)}) copy-start(s32[8,8]{1,0:T(8,128)} %param.22) | copy-start | bytes 772
  31.2 36.9 %all-to-all-start = ((bf16[32,8,4096]{2,1,0:T(8,128)(2,1)}), bf16[32,8,4096]{2,1,0:T(8,128)(2,1)S(1)}, u32[]{:S(2)}, u32[]{:S(2)}) async-start(bf16[32,8,4096]{2,1,0:T(8,128)(2,1)} %bitcast.4), calls=%async_computation | async-start | bytes 4194304 | tf_op jit(solution)/shard_map/all_to_all | solution.py:311
  44.8 23.3 %copy-start.10 = (bf16[8,4096]{1,0:T(8,128)(2,1)S(1)}, bf16[8,4096]{1,0:T(8,128)(2,1)}, u32[]{:S(2)}) copy-start(bf16[8,4096]{1,0:T(8,128)(2,1)} %residual_ref.1) | copy-start | bytes 196612
  44.8 23.3 %copy-start.11 = (f32[4096]{0:T(1024)S(1)}, f32[4096]{0:T(1024)}, u32[]{:S(2)}) copy-start(f32[4096]{0:T(1024)} %param.21) | copy-start | bytes 49156
  68.9 38.0 %copy-start.7 = (bf16[256,256]{1,0:T(8,128)(2,1)S(1)}, bf16[256,256]{1,0:T(8,128)(2,1)}, u32[]{:S(2)}) copy-start(bf16[256,256]{1,0:T(8,128)(2,1)} %constant.28.clone.perm_ref) | copy-start | bytes 393220
  68.9 38.0 %copy-start.8 = (bf16[256,256]{1,0:T(8,128)(2,1)S(1)}, bf16[256,256]{1,0:T(8,128)(2,1)}, u32[]{:S(2)}) copy-start(bf16[256,256]{1,0:T(8,128)(2,1)} %constant.29.clone.back_ref) | copy-start | bytes 393220
  107.0 12.2 %collective-permute-start.6 = (bf16[64,16,1024]{2,1,0:T(8,128)(2,1)S(1)}, bf16[64,16,1024]{2,1,0:T(8,128)(2,1)S(1)}, u32[]{:S(2)}, u32[]{:S(2)}) collective-permute-start(bf16[64,16,1024]{2,1,0:T(8,128)(2,1)S(1)} %all_to_all.15.rows_ref), channel_id=1, source_target_pairs={{0,32},{32,0},{1,33},{33,1},{2,34},{34,2},{3,35},{35,3},{4,36},{36... | collective-permute-start | bytes 6291464 | tf_op jit(solution)/shard_map/ppermute | solution.py:270
  107.0 4.6 %copy-start = (bf16[2,4096,2,384]{3,1,2,0:T(8,128)(2,1)S(1)}, bf16[2,4096,2,384]{3,1,2,0:T(8,128)(2,1)}, u32[]{:S(2)}) copy-start(bf16[2,4096,2,384]{3,1,2,0:T(8,128)(2,1)} %copy.29) | copy-start | bytes 37748740
  111.5 2.8 %copy-start.4 = (bf16[2,384,4096]{2,1,0:T(8,128)(2,1)S(1)}, bf16[2,384,4096]{2,1,0:T(8,128)(2,1)}, u32[]{:S(2)}) copy-start(bf16[2,384,4096]{2,1,0:T(8,128)(2,1)} %wout_ref.3) | copy-start | bytes 18874372
  114.3 4.8 %copy-start.1 = (bf16[2,4096,2,384]{3,1,2,0:T(8,128)(2,1)S(1)}, bf16[2,4096,2,384]{3,1,2,0:T(8,128)(2,1)}, u32[]{:S(2)}) copy-start(bf16[2,4096,2,384]{3,1,2,0:T(8,128)(2,1)} %copy.29) | copy-start | bytes 37748740
  124.0 4.4 %collective-permute-start.7 = (bf16[64,16,1024]{2,1,0:T(8,128)(2,1)S(1)}, bf16[64,16,1024]{2,1,0:T(8,128)(2,1)S(1)}, u32[]{:S(2)}, u32[]{:S(2)}) collective-permute-start(bf16[64,16,1024]{2,1,0:T(8,128)(2,1)S(1)} %experts.3), channel_id=1, source_target_pairs={{0,32},{32,0},{1,33},{33,1},{2,34},{34,2},{3,35},{35,3},{4,36},{36... | collective-permute-start | bytes 6291464 | tf_op jit(solution)/shard_map/ppermute | solution.py:270

commit v4 on v3

--- a/solution.py
+++ b/solution.py
@@ -18,11 +18,12 @@
 ANY_LAST = (((1,), (1,)), ((), ()))
 
 
-def attn_kernel(first, info, qa_ref, qb_ref, kc_ref, vc_ref, kn_ref, vn_ref, oa_ref, ob_ref, s_ref):
+def attn_kernel(
+    first, info, spans, qa_ref, qb_ref, kc_ref, vc_ref, kn_ref, vn_ref, oa_ref, ob_ref, s_ref
+):
     rows = qa_ref.shape[0]
-    cache_rows = kc_ref.shape[1]
     chunk = kn_ref.shape[1]
-    chunks = cache_rows // chunk
+    chunks = kc_ref.shape[1] // chunk
     coef = math.log2(math.e) / math.sqrt(HEAD_DIM)
     valid = info[1]
     key_pos = info[2] * rows + lax.broadcasted_iota(jnp.int32, (1, chunk), 1)
@@ -32,7 +33,7 @@
         pos = (info[2] ^ (first + b)) * rows + lax.broadcasted_iota(jnp.int32, (rows, 1), 0)
         limit = pos
         for a in range(3):
-            start, end = info[3 + 2 * a], info[4 + 2 * a]
+            start, end = spans[0, a], spans[1, a]
             limit = jnp.where((pos >= start) & (pos < end), jnp.maximum(limit, end - 1), limit)
         tract_ok = key_pos <= limit
         stats = jnp.zeros((rows, 128), F32)
@@ -41,12 +42,11 @@
             q = q_ref[:, h * HEAD_DIM : (h + 1) * HEAD_DIM]
             top = None
             for c in range(chunks + 1):
+                k = kc_ref[0, c * chunk : (c + 1) * chunk, :] if c < chunks else kn_ref[0]
+                s = lax.dot_general(q, k, ANY_LAST, preferred_element_type=F32)
                 if c < chunks:
-                    k = kc_ref[0, c * chunk : (c + 1) * chunk, :]
-                    s = lax.dot_general(q, k, ANY_LAST, preferred_element_type=F32)
                     s = s + jnp.where(column < valid - c * chunk, 0.0, NEG)
                 else:
-                    s = lax.dot_general(q, kn_ref[0], ANY_LAST, preferred_element_type=F32)
                     s = jnp.where(tract_ok, s, NEG)
                 s_ref[at, :, c * chunk : (c + 1) * chunk] = s
                 top = s if top is None else jnp.maximum(top, s)
@@ -69,38 +69,38 @@
         out_ref[rows : rows + 16, :] = stats.T[0:16, :].astype(BF)
 
 
-def attend(first, info, qa, qb, cache_kv, new_kv):
+def attend(first, info, spans, qa, qb, cache_kv, new_kv):
     rows = qa.shape[0]
     cache_rows, new_rows = cache_kv.shape[1], new_kv.shape[1]
     keys = cache_rows + new_rows
-    whole = pl.BlockSpec((rows, 2 * HEAD_DIM), lambda i, t: (0, 0))
-    result = pl.BlockSpec((rows + 16, 2 * HEAD_DIM), lambda i, t: (0, 0))
+    whole = pl.BlockSpec((rows, 2 * HEAD_DIM), lambda i, t, u: (0, 0))
+    result = pl.BlockSpec((rows + 16, 2 * HEAD_DIM), lambda i, t, u: (0, 0))
     shape = jax.ShapeDtypeStruct((rows + 16, 2 * HEAD_DIM), BF)
     return pl.pallas_call(
         functools.partial(attn_kernel, first),
         grid_spec=pltpu.PrefetchScalarGridSpec(
-            num_scalar_prefetch=1,
+            num_scalar_prefetch=2,
             grid=(1,),
             in_specs=[
                 whole,
                 whole,
-                pl.BlockSpec((1, cache_rows, HEAD_DIM), lambda i, t: (0, 0, t[0])),
-                pl.BlockSpec((1, cache_rows, HEAD_DIM), lambda i, t: (1, 0, t[0])),
-                pl.BlockSpec((1, new_rows, HEAD_DIM), lambda i, t: (0, 0, t[0])),
-                pl.BlockSpec((1, new_rows, HEAD_DIM), lambda i, t: (1, 0, t[0])),
+                pl.BlockSpec((1, cache_rows, HEAD_DIM), lambda i, t, u: (0, 0, t[0])),
+                pl.BlockSpec((1, cache_rows, HEAD_DIM), lambda i, t, u: (1, 0, t[0])),
+                pl.BlockSpec((1, new_rows, HEAD_DIM), lambda i, t, u: (0, 0, t[0])),
+                pl.BlockSpec((1, new_rows, HEAD_DIM), lambda i, t, u: (1, 0, t[0])),
             ],
             out_specs=[result, result],
             scratch_shapes=[pltpu.VMEM((4, rows, keys), F32)],
         ),
         out_shape=[shape, shape],
-        compiler_params=pltpu.CompilerParams(vmem_limit_bytes=20 << 20),
+        compiler_params=pltpu.CompilerParams(vmem_limit_bytes=50 << 20),
         cost_estimate=pl.CostEstimate(
             flops=32 * rows * keys * HEAD_DIM,
             bytes_accessed=4 * keys * HEAD_DIM,
             transcendentals=4 * rows * keys,
         ),
         name="attend",
-    )(info, qa, qb, cache_kv, cache_kv, new_kv, new_kv)
+    )(info, spans, qa, qb, cache_kv, cache_kv, new_kv, new_kv)
 
 
 def project_kernel(a_ref, b_ref, c_ref, d_ref, w_ref, out_ref, att_ref):
@@ -146,7 +146,27 @@
     )(*parts, out_proj)
 
 
-def settle_kernel(arrived_ref, residual_ref, gain_ref, pick_ref, stream_ref, out_ref):
+def slot_table(flat, routes_ref, values, columns):
+    tok, top = routes_ref.shape
+    named = jnp.concatenate([routes_ref[...]] * 4, axis=0)
+    row = lax.broadcasted_iota(jnp.int32, named.shape, 0)
+    token = row & (tok - 1)
+    rank = jnp.zeros(named.shape, jnp.int32)
+    for t in range(tok):
+        for k in range(top):
+            rank = rank + jnp.where((named == flat[t, k]) & (token > t), 1, 0)
+    slot = named * 2 + rank
+    column = lax.broadcasted_iota(jnp.int32, (1, columns), 1)
+    here = (column >> 4) * 4 + (column & 3)
+    table = jnp.zeros((4 * tok, columns), F32)
+    for k in range(top):
+        value = values[:, k : k + 1] if values is not None else 1.0
+        table = table + jnp.where(slot[:, k : k + 1] == here, value, 0.0)
+    chunk = lax.broadcasted_iota(jnp.int32, (4 * tok, 1), 0) // tok
+    return jnp.where(chunk == ((column >> 2) & 3), table, 0.0)
+
+
+def settle_kernel(flat, arrived_ref, residual_ref, gain_ref, routes_ref, stream_ref, out_ref):
     tok, width = residual_ref.shape
     groups = arrived_ref.shape[0]
     chunk = out_ref.shape[2]
@@ -169,28 +189,34 @@
         p * scale * gain_ref[:, c * chunk : (c + 1) * chunk] for c, p in enumerate(pieces)
     ]
     stacked = jnp.concatenate(normed, axis=0).astype(BF)
-    rows = jnp.dot(pick_ref[...], stacked, preferred_element_type=F32).astype(BF)
     half = out_ref.shape[0] // 2
+    pick = slot_table(flat, routes_ref, None, half * 16).astype(BF)
+    rows = lax.dot_general(
+        pick, stacked, (((0,), (0,)), ((), ())), preferred_element_type=F32
+    ).astype(BF)
     rows = rows.reshape(half, 16, chunk)
     out_ref[0:half] = rows
     out_ref[half : 2 * half] = rows
 
 
-def settle(arrived, residual, gain, pick):
+def settle(arrived, residual, gain, routes, devices):
     tok, width = residual.shape
     chunk = width // 4
     return pl.pallas_call(
         settle_kernel,
+        in_specs=[pl.BlockSpec(memory_space=pltpu.SMEM)]
+        + [pl.BlockSpec(memory_space=pltpu.VMEM)] * 4,
+        out_specs=[pl.BlockSpec(memory_space=pltpu.VMEM)] * 2,
         out_shape=[
             jax.ShapeDtypeStruct((tok, width), BF),
-            jax.ShapeDtypeStruct((pick.shape[0] // 8, 16, chunk), BF),
+            jax.ShapeDtypeStruct((devices, 16, chunk), BF),
         ],
-        compiler_params=pltpu.CompilerParams(vmem_limit_bytes=20 << 20),
+        compiler_params=pltpu.CompilerParams(vmem_limit_bytes=10 << 20),
         cost_estimate=pl.CostEstimate(
             flops=1 << 26, bytes_accessed=4 << 20, transcendentals=0
         ),
         name="settle",
-    )(arrived, residual, gain.reshape(1, width), pick)
+    )(routes, arrived, residual, gain.reshape(1, width), routes)
 
 
 def expert_kernel(rows_ref, perm_ref, back_ref, win_ref, wout_ref, out_ref, x_ref, z_ref):
@@ -233,7 +259,7 @@
             pltpu.VMEM((2, count, width), BF),
             pltpu.VMEM((2, count, width), BF),
         ],
-        compiler_params=pltpu.CompilerParams(vmem_limit_bytes=16 << 20),
+        compiler_params=pltpu.CompilerParams(vmem_limit_bytes=10 << 20),
         cost_estimate=pl.CostEstimate(
             flops=12 * count * width * ff,
             bytes_accessed=12 * width * ff,
@@ -243,10 +269,18 @@
     )(rows, perm, back, w_in, w_out)
 
 
-def combine_kernel(share_ref, returned_ref, stream_ref, out_ref):
+def combine_kernel(flat, routes_ref, gates_ref, returned_ref, stream_ref, out_ref):
     tok = stream_ref.shape[0]
     chunk = returned_ref.shape[1]
-    both = jnp.dot(share_ref[...], returned_ref[...], preferred_element_type=F32)
+    gates = gates_ref[...]
+    gates = gates / jnp.sum(gates, axis=1, keepdims=True)
+    share = slot_table(
+        flat, routes_ref, jnp.concatenate([gates] * 4, axis=0), returned_ref.shape[0] // 2
+    )
+    coarse = share.astype(BF).astype(F32)
+    pieces = jnp.concatenate([coarse, share - coarse], axis=0).astype(BF)
+    pieces = jnp.concatenate([pieces, pieces], axis=1)
+    both = jnp.dot(pieces, returned_ref[...], preferred_element_type=F32)
     half = both.shape[0] // 2
     total = both[:half] + both[half:]
     for c in range(half // tok):
@@ -256,13 +290,16 @@
         ).astype(BF)
 
 
-def combine(share, returned, stream):
+def combine(routes, gates, returned, stream):
     return pl.pallas_call(
         combine_kernel,
+        in_specs=[pl.BlockSpec(memory_space=pltpu.SMEM)]
+        + [pl.BlockSpec(memory_space=pltpu.VMEM)] * 4,
+        out_specs=pl.BlockSpec(memory_space=pltpu.VMEM),
         out_shape=jax.ShapeDtypeStruct(stream.shape, BF),
-        compiler_params=pltpu.CompilerParams(vmem_limit_bytes=20 << 20),
+        compiler_params=pltpu.CompilerParams(vmem_limit_bytes=10 << 20),
         name="combine",
-    )(share, returned, stream)
+    )(routes, routes, gates, returned, stream)
 
 
 def swap(v, axes, bit):
@@ -295,52 +332,30 @@
     query_parts = [queries] + [swap(queries, SEQ, d) for d in (1, 2, 3)]
     valid = jnp.clip(cached_len[0] - seq * cache, 0, cache)
 
-    place = jnp.stack([lax.axis_index("x"), valid, seq]).astype(jnp.int32)
-    info = jnp.concatenate([place, image_spans.reshape(-1)])
+    info = jnp.stack([lax.axis_index("x"), valid, seq]).astype(jnp.int32)
+    spans = image_spans.T
 
     def attend_pair(d):
-        return attend(d, info, query_parts[d], query_parts[d + 1], cache_kv, new_kv)
+        return attend(d, info, spans, query_parts[d], query_parts[d + 1], cache_kv, new_kv)
 
     mine, beside = attend_pair(0)
+    mine, query_parts[2], query_parts[3] = lax.optimization_barrier(
+        (mine, query_parts[2], query_parts[3])
+    )
     across, diagonal = attend_pair(2)
+    across, diagonal, w_in = lax.optimization_barrier((across, diagonal, w_in))
+    turned = w_in.transpose(0, 2, 1, 3)
     parts = [mine, swap(beside, SEQ, 1), swap(across, SEQ, 2), swap(diagonal, SEQ, 3)]
+    parts, turned = lax.optimization_barrier((parts, turned))
     partial = project(parts, out_proj)
-    partial, routes, gate_weights, w_in = lax.optimization_barrier(
-        (partial, routes, gate_weights, w_in)
-    )
     arrived = lax.all_to_all(
         partial.reshape(32, tok, width), MP, split_axis=0, concat_axis=0, tiled=True
     )
-    turned = w_in.transpose(0, 2, 1, 3)
-
-    gate_share = gate_weights / jnp.sum(gate_weights, axis=1, keepdims=True)
-    top = routes.shape[1]
-    same = routes[:, :, None, None] == routes[None, None, :, :]
-    earlier = jnp.arange(tok)[:, None] > jnp.arange(tok)[None, :]
-    rank = jnp.sum((same & earlier[:, None, :, None]).astype(jnp.int32), axis=(2, 3))
-    slot = routes * 2 + rank
-    pairs = 32
-    placement = slot[:, :, None] == jnp.arange(pairs * 4, dtype=jnp.int32)[None, None, :]
-    chosen = jnp.sum(placement.astype(F32), axis=1)
-    weighed = jnp.sum(jnp.where(placement, gate_share[:, :, None], 0.0), axis=1)
-    eye = jnp.eye(4, dtype=F32)
-
-    def spread_rows(v):
-        wide = v.reshape(1, tok, pairs, 1, 4) * eye.reshape(4, 1, 1, 4, 1)
-        return wide.reshape(4 * tok, pairs * 16)
-
-    pick = spread_rows(chosen).astype(BF).T
-    share = spread_rows(weighed)
-    coarse = share.astype(BF)
-    fine = (share - coarse.astype(F32)).astype(BF)
-    share = jnp.concatenate([coarse, fine], axis=0)
-    share = jnp.concatenate([share, share], axis=1)
 
     perm = np.eye(256).reshape(16, 4, 2, 2, 256).transpose(2, 1, 0, 3, 4).reshape(256, 256)
     perm, back = jnp.asarray(perm, BF), jnp.asarray(perm.T, BF)
 
-    arrived, pick, share, turned = lax.optimization_barrier((arrived, pick, share, turned))
-    stream, outgoing = settle(arrived, residual, norm_gain, pick)
+    stream, outgoing = settle(arrived, residual, norm_gain, routes, 64)
 
     own = lax.all_to_all(outgoing, spread, split_axis=0, concat_axis=0, tiled=True)
     other = swap(own, ("core",), 1)
@@ -350,7 +365,7 @@
     got = swap(sent, ("core",), 1)
     summed = (kept.astype(F32) + got.astype(F32)).astype(BF)
     returned = lax.all_to_all(summed, spread, split_axis=0, concat_axis=0, tiled=True)
-    return combine(share, returned.reshape(-1, quarter), stream)
+    return combine(routes, gate_weights, returned.reshape(-1, quarter), stream)
 
 
 def solution(mesh):

time: 168 us -> 160 us (0.952)
  blocking collectives: 74.6 us -> 109 us
  waiting for transfers between devices: 21.7 us -> 3.8 us
  local copies, waits for them, and re-layouts: 25.2 us -> 10.3 us
  starting transfers between devices: 16.6 us -> 7.71 us
  other arithmetic: 4.06 us -> 1.1 us
  Pallas kernels: 24.1 us -> 26.7 us
    all_to_all x0 -> x1, blocking collectives: none -> 37 us  [local(): lax.all_to_all(partial.reshape(32, tok, width), MP, split_axis=0, concat_...]
    all_to_all x1 -> x0, waiting for transfers between devices: 11.7 us -> none  [local(): lax.all_to_all(partial.reshape(32, tok, width), MP, split_axis=0, concat_...]
    unnamed x29 -> x26, local copies, waits for them, and re-layouts: 11.4 us -> 2.69 us
    all_to_all x1 -> x0, starting transfers between devices: 8.58 us -> none  [local(): lax.all_to_all(partial.reshape(32, tok, width), MP, split_axis=0, concat_...]
    ppermute x8, waiting for transfers between devices: 10.1 us -> 3.8 us  [swap(): return lax.ppermute(v, axes, [(i, i ^ bit) for i in range(count)])]
    optimization_barrier x1, local copies, waits for them, and re-layouts: 11.6 us -> 7.57 us  [local(): across, diagonal, w_in = lax.optimization_barrier((across, diagonal, w_in))]
    pallas_call x2, Pallas kernels: 9.74 us -> 12 us  [attend(): pl.pallas_call(functools.partial(attn_kernel, first), grid_spec=pltpu.Pre...]
    all_to_all x1, blocking collectives: 38 us -> 35.8 us  [local(): lax.all_to_all(outgoing, spread, split_axis=0, concat_axis=0, tiled=True)]
  transfers between devices with their start and end apart: 9 -> 8, of which waited for: 6 -> 1; matrix products, arithmetic and copies ran while one was open for 10% -> 5% of each run, Pallas kernels for 9% -> 7%
where the time goes in v4:
time: 160 us
  blocking collectives  109 us (68%)
  Pallas kernels  26.7 us (17%)
  local copies, waits for them, and re-layouts  10.3 us (6%)
  starting transfers between devices  7.71 us (5%)
  waiting for transfers between devices  3.8 us (2%)
    all_to_all x1, blocking collectives, local(): lax.all_to_all(partial.reshape(32, tok, width), MP, split_axis=0, concat_...  37 us
    all_to_all x1, blocking collectives, local(): lax.all_to_all(summed, spread, split_axis=0, concat_axis=0, tiled=True)  36.3 us
    all_to_all x1, blocking collectives, local(): lax.all_to_all(outgoing, spread, split_axis=0, concat_axis=0, tiled=True)  35.8 us
    pallas_call x2, Pallas kernels, attend(): pl.pallas_call(functools.partial(attn_kernel, first), grid_spec=pltpu.Pre...  12 us
    pallas_call x2, Pallas kernels, experts(): pl.pallas_call(expert_kernel, in_specs=[pl.BlockSpec(memory_space=pltpu.V...  9.75 us
    ppermute x8, starting transfers between devices, swap(): return lax.ppermute(v, axes, [(i, i ^ bit) for i in range(count)])  7.71 us
    optimization_barrier x1, local copies, waits for them, and re-layouts, local(): across, diagonal, w_in = lax.optimization_barrier((across, diagonal, w_in))  7.57 us
    ppermute x8, waiting for transfers between devices, swap(): return lax.ppermute(v, axes, [(i, i ^ bit) for i in range(count)])  3.8 us
  transfers between devices with their start and end apart: 8, of which 1 were waited for; matrix products, arithmetic and copies ran while one was open for 5% of the time, Pallas kernels for 7%

profile of v4, /device:TPU:0, one launch (start us, length us, event | category | flops | bytes accessed | tf_op | source)
XLA Modules:
  0.0 159.5 jit_solution(7764577241856226495)
XLA Ops:
  0.0 0.0 collective-permute-start
  0.0 3.3 %collective-permute-start.1 = (bf16[256,256]{1,0:T(8,128)(2,1)}, bf16[256,256]{1,0:T(8,128)(2,1)S(1)}, u32[]{:S(2)}, u32[]{:S(2)}) collective-permute-start(bf16[256,256]{1,0:T(8,128)(2,1)} %qa_ref.1), channel_id=1, source_target_pairs={{0,64},{32,96},{64,0},{96,32},{1,65},{33,97},{65,1},{97,33},{2,66}... | collective-permute-start | bytes 393224 | tf_op jit(solution)/shard_map/ppermute | solution.py:307
  3.3 0.1 collective-permute-start.2
  4.1 0.1 pad_add_fusion.info
  4.2 0.0 collective-permute-done.qb_ref
  4.2 0.0 copy-start
  4.2 1.0 copy-done
  5.2 0.0 copy-start.5
  5.2 0.9 copy-done.5
  6.1 0.0 copy-start.10
  6.1 0.7 copy-done.10
  6.8 0.0 copy-start.1
  6.8 6.0 %attend.2 = (bf16[272,256]{1,0:T(8,128)(2,1)S(1)}, bf16[272,256]{1,0:T(8,128)(2,1)S(1)}) custom-call(s32[3]{0:T(128)S(1)} %pad_add_fusion.info, s32[2,3]{1,0:T(2,128)S(1)} %bitcast.19, bf16[256,256]{1,0:T(8,128)(2,1)S(1)} %copy-done.5, bf16[256,256]{1,0:T(8,128)(2,1)S(1)} %collective-permute-done.qb_ref, bf16[2,2048,512]{2,1,0:T(8,128)(2,1)} %vc_ref.3, ...), custom_call_target="tpu_custom_call" | custom-call | flops 2415919104 | bytes 1179648 | tf_op jit(solution)/shard_map/attend/pallas_call | solution.py:79
  12.8 0.0 collective-permute-done.1.qa_ref
  12.8 0.0 collective-permute-done.2.qb_ref
  12.8 0.0 copy-done.1
  12.8 6.0 %attend.3 = (bf16[272,256]{1,0:T(8,128)(2,1)S(1)}, bf16[272,256]{1,0:T(8,128)(2,1)S(1)}) custom-call(s32[3]{0:T(128)S(1)} %pad_add_fusion.info, s32[2,3]{1,0:T(2,128)S(1)} %bitcast.20, bf16[256,256]{1,0:T(8,128)(2,1)S(1)} %collective-permute-done.1.qa_ref, bf16[256,256]{1,0:T(8,128)(2,1)S(1)} %collective-permute-done.2.qb_ref, bf16[2,2048,512]{2,1,0:T(8,128)(2,1)} %vc_ref.3, ...), custom_call_target="tpu_custom_call" | custom-call | flops 2415919104 | bytes 1179648 | tf_op jit(solution)/shard_map/attend/pallas_call | solution.py:79
  18.8 3.3 %collective-permute-start.4 = (bf16[272,256]{1,0:T(8,128)(2,1)S(1)}, bf16[272,256]{1,0:T(8,128)(2,1)S(1)}, u32[]{:S(2)}, u32[]{:S(2)}) collective-permute-start(bf16[272,256]{1,0:T(8,128)(2,1)S(1)} %get-tuple-element.31), channel_id=1, source_target_pairs={{0,64},{32,96},{64,0},{96,32},{1,65},{33,97},{65,1},{97,33},{2,66}... | collective-permute-start | bytes 417800 | tf_op jit(solution)/shard_map/ppermute | solution.py:307
  22.1 0.0 collective-permute-start.5
  22.1 0.0 copy-start.2
  22.1 0.4 collective-permute-start.3
  22.6 7.6 %copy.17 = bf16[2,4096,2,384]{3,1,2,0:T(8,128)(2,1)S(1)} copy(bf16[2,4096,2,384]{3,2,1,0:T(2,128)(2,1)} %param.24) | data formatting | bytes 25165824 | tf_op jit(solution)/shard_map/optimization_barrier | solution.py:346
  30.1 0.0 collective-permute-done.4.c_ref
  30.1 0.0 collective-permute-done.5.d_ref
  30.2 0.0 collective-permute-done.3.b_ref
  30.2 0.0 copy-done.2
  30.2 0.0 copy-start.6
  30.2 0.0 copy-start.7
  30.2 0.0 copy-start.8
  30.2 0.0 slice-start
  30.2 1.5 project.1
  31.7 0.0 slice-start.1
  31.8 37.0 %all_to_all.15.arrived_ref = bf16[32,8,4096]{2,1,0:T(8,128)(2,1)S(1)} all-to-all(bf16[32,8,4096]{2,1,0:T(8,128)(2,1)S(1)} %bitcast.16), channel_id=1, replica_groups=mesh['yh'=2,'core'=2,'x'=4,'yl'=2,'z'=4] {'x','yl','z'}, dimensions={0} | all-to-all | bytes 4194304 | tf_op jit(solution)/shard_map/all_to_all | solution.py:351
  68.8 0.0 copy-done.6
  68.8 0.0 copy-done.7
  68.8 0.0 copy-done.8
  68.8 1.5 settle.1
  70.3 0.0 copy-start.3
  70.3 0.0 copy-start.4
  70.3 35.8 %all_to_all.16.rows_ref = bf16[64,16,1024]{2,1,0:T(8,128)(2,1)S(1)} all-to-all(bf16[64,16,1024]{2,1,0:T(8,128)(2,1)S(1)} %get-tuple-element.38), channel_id=1, replica_groups=mesh['yh'=2,'core'=2,'x'=4,'yl'=2,'z'=4] {'yh','x','yl','z'}, dimensions={0} | all-to-all | bytes 4194304 | tf_op jit(solution)/shard_map/all_to_all | solution.py:360
  106.1 0.0 collective-permute-start.6
  106.1 0.0 slice-done
  106.1 0.0 slice-done.1
  106.1 0.0 copy-done.3
  106.1 0.0 copy-done.4
  106.2 4.9 %experts.2 = bf16[64,16,1024]{2,1,0:T(8,128)(2,1)S(1)} custom-call(bf16[64,16,1024]{2,1,0:T(8,128)(2,1)S(1)} %all_to_all.16.rows_ref, bf16[256,256]{1,0:T(8,128)(2,1)S(1)} %copy-done.3, bf16[256,256]{1,0:T(8,128)(2,1)S(1)} %copy-done.4, bf16[2,2,4096,384]{3,2,1,0:T(8,128)(2,1)S(1)} %bitcast.12, bf16[2,384,4096]{2,1,0:T(8,128)(2,1)S(1)} %bitcast.15), custom_call_target="tpu_custom_call" | custom-call | flops 2415919104 | bytes 18874368 | tf_op jit(solution)/shard_map/experts/pallas_call | solution.py:253
  111.0 0.0 collective-permute-done.6.rows_ref
  111.0 4.9 %experts.3 = bf16[64,16,1024]{2,1,0:T(8,128)(2,1)S(1)} custom-call(bf16[64,16,1024]{2,1,0:T(8,128)(2,1)S(1)} %collective-permute-done.6.rows_ref, bf16[256,256]{1,0:T(8,128)(2,1)S(1)} %copy-done.3, bf16[256,256]{1,0:T(8,128)(2,1)S(1)} %copy-done.4, bf16[2,2,4096,384]{3,2,1,0:T(8,128)(2,1)S(1)} %bitcast.13, bf16[2,384,4096]{2,1,0:T(8,128)(2,1)S(1)} %bitcast.15), custom_call_target="tpu_custom_call" | custom-call | flops 2415919104 | bytes 18874368 | tf_op jit(solution)/shard_map/experts/pallas_call | solution.py:253
  115.9 0.6 collective-permute-start.7
  116.5 3.8 %collective-permute-done.7 = bf16[64,16,1024]{2,1,0:T(8,128)(2,1)S(1)} collective-permute-done((bf16[64,16,1024]{2,1,0:T(8,128)(2,1)S(1)}, bf16[64,16,1024]{2,1,0:T(8,128)(2,1)S(1)}, u32[]{:S(2)}, u32[]{:S(2)}) %collective-permute-start.7) | collective-permute-done | bytes 2097184 | tf_op jit(solution)/shard_map/ppermute | solution.py:307
  120.3 1.0 add_convert_fusion
  121.3 0.0 copy-start.9
  121.3 36.3 %all_to_all.17 = bf16[64,16,1024]{2,1,0:T(8,128)(2,1)S(1)} all-to-all(bf16[64,16,1024]{2,1,0:T(8,128)(2,1)S(1)} %add_convert_fusion), channel_id=1, replica_groups=mesh['yh'=2,'core'=2,'x'=4,'yl'=2,'z'=4] {'yh','x','yl','z'}, dimensions={0} | all-to-all | bytes 4194304 | tf_op jit(solution)/shard_map/all_to_all | solution.py:367
  157.6 0.0 copy-done.9
  157.6 1.9 %combine.1 = bf16[8,4096]{1,0:T(8,128)(2,1)} custom-call(s32[8,8]{1,0:T(8,128)S(1)} %copy-done.6, s32[8,8]{1,0:T(8,128)S(1)} %copy-done.6, f32[8,8]{1,0:T(8,128)S(1)} %copy-done.9, bf16[1024,1024]{1,0:T(8,128)(2,1)S(1)} %bitcast.17, bf16[8,4096]{1,0:T(8,128)(2,1)S(1)} %get-tuple-element.42.stream_ref), custom_call_target="tpu_custom_call" | custom-call | tf_op jit(solution)/shard_map/combine/pallas_call | solution.py:294
  (1 shorter events, 0.0 us)
Async XLA Ops:
  0.0 4.2 %collective-permute-start = (bf16[256,256]{1,0:T(8,128)(2,1)}, bf16[256,256]{1,0:T(8,128)(2,1)S(1)}, u32[]{:S(2)}, u32[]{:S(2)}) collective-permute-start(bf16[256,256]{1,0:T(8,128)(2,1)} %qa_ref.1), channel_id=1, source_target_pairs={{0,32},{32,0},{64,96},{96,64},{1,33},{33,1},{65,97},{97,65},{2,34}... | collective-permute-start | bytes 393224 | tf_op jit(solution)/shard_map/ppermute | solution.py:307
  0.0 12.8 %collective-permute-start.1 = (bf16[256,256]{1,0:T(8,128)(2,1)}, bf16[256,256]{1,0:T(8,128)(2,1)S(1)}, u32[]{:S(2)}, u32[]{:S(2)}) collective-permute-start(bf16[256,256]{1,0:T(8,128)(2,1)} %qa_ref.1), channel_id=1, source_target_pairs={{0,64},{32,96},{64,0},{96,32},{1,65},{33,97},{65,1},{97,33},{2,66}... | collective-permute-start | bytes 393224 | tf_op jit(solution)/shard_map/ppermute | solution.py:307
  3.3 9.5 %collective-permute-start.2 = (bf16[256,256]{1,0:T(8,128)(2,1)}, bf16[256,256]{1,0:T(8,128)(2,1)S(1)}, u32[]{:S(2)}, u32[]{:S(2)}) collective-permute-start(bf16[256,256]{1,0:T(8,128)(2,1)} %qa_ref.1), channel_id=1, source_target_pairs={{0,96},{32,64},{64,32},{96,0},{1,97},{33,65},{65,33},{97,1},{2,98}... | collective-permute-start | bytes 393224 | tf_op jit(solution)/shard_map/ppermute | solution.py:307
  4.2 1.0 copy-start
  5.2 0.9 copy-start.5
  6.1 0.7 copy-start.10
  6.8 6.0 %copy-start.1 = (bf16[2,256,512]{2,1,0:T(8,128)(2,1)S(1)}, bf16[2,256,512]{2,1,0:T(8,128)(2,1)}, u32[]{:S(2)}) copy-start(bf16[2,256,512]{2,1,0:T(8,128)(2,1)} %vn_ref.3) | copy-start | bytes 1572868
  18.8 11.3 %collective-permute-start.4 = (bf16[272,256]{1,0:T(8,128)(2,1)S(1)}, bf16[272,256]{1,0:T(8,128)(2,1)S(1)}, u32[]{:S(2)}, u32[]{:S(2)}) collective-permute-start(bf16[272,256]{1,0:T(8,128)(2,1)S(1)} %get-tuple-element.31), channel_id=1, source_target_pairs={{0,64},{32,96},{64,0},{96,32},{1,65},{33,97},{65,1},{97,33},{2,66}... | collective-permute-start | bytes 417800 | tf_op jit(solution)/shard_map/ppermute | solution.py:307
  22.1 8.0 %collective-permute-start.5 = (bf16[272,256]{1,0:T(8,128)(2,1)S(1)}, bf16[272,256]{1,0:T(8,128)(2,1)S(1)}, u32[]{:S(2)}, u32[]{:S(2)}) collective-permute-start(bf16[272,256]{1,0:T(8,128)(2,1)S(1)} %get-tuple-element.32), channel_id=1, source_target_pairs={{0,96},{32,64},{64,32},{96,0},{1,97},{33,65},{65,33},{97,1},{2,98}... | collective-permute-start | bytes 417800 | tf_op jit(solution)/shard_map/ppermute | solution.py:307
  22.1 8.0 %copy-start.2 = (bf16[256,4096]{1,0:T(8,128)(2,1)S(1)}, bf16[256,4096]{1,0:T(8,128)(2,1)}, u32[]{:S(2)}) copy-start(bf16[256,4096]{1,0:T(8,128)(2,1)} %w_ref.1) | copy-start | bytes 6291460
  22.1 8.0 %collective-permute-start.3 = (bf16[272,256]{1,0:T(8,128)(2,1)S(1)}, bf16[272,256]{1,0:T(8,128)(2,1)S(1)}, u32[]{:S(2)}, u32[]{:S(2)}) collective-permute-start(bf16[272,256]{1,0:T(8,128)(2,1)S(1)} %get-tuple-element.26), channel_id=1, source_target_pairs={{0,32},{32,0},{64,96},{96,64},{1,33},{33,1},{65,97},{97,65},{2,34}... | collective-permute-start | bytes 417800 | tf_op jit(solution)/shard_map/ppermute | solution.py:307
  30.2 38.6 %copy-start.6 = (s32[8,8]{1,0:T(8,128)S(1)}, s32[8,8]{1,0:T(8,128)}, u32[]{:S(2)}) copy-start(s32[8,8]{1,0:T(8,128)} %routes_ref.3) | copy-start | bytes 772
  30.2 38.6 %copy-start.7 = (bf16[8,4096]{1,0:T(8,128)(2,1)S(1)}, bf16[8,4096]{1,0:T(8,128)(2,1)}, u32[]{:S(2)}) copy-start(bf16[8,4096]{1,0:T(8,128)(2,1)} %residual_ref.1) | copy-start | bytes 196612
  30.2 38.6 %copy-start.8 = (f32[4096]{0:T(1024)S(1)}, f32[4096]{0:T(1024)}, u32[]{:S(2)}) copy-start(f32[4096]{0:T(1024)} %param.21) | copy-start | bytes 49156
  30.2 75.9 %slice-start = ((s8[6291456]{0:T(1024)(128)(4,1)}), s8[2097152]{0:T(1024)(128)(4,1)S(1)}, s32[]{:S(2)}) async-start(s8[6291456]{0:T(1024)(128)(4,1)} %bitcast.14), calls=%async_computation.3 | async-start | bytes 4194304
  31.7 74.4 %slice-start.1 = ((s8[6291456]{0:T(1024)(128)(4,1)}), s8[4194304]{0:T(1024)(128)(4,1)S(1)}, s32[]{:S(2)}) async-start(s8[6291456]{0:T(1024)(128)(4,1)} %bitcast.14), calls=%async_computation.4 | async-start | bytes 8388608
  70.3 35.8 %copy-start.3 = (bf16[256,256]{1,0:T(8,128)(2,1)S(1)}, bf16[256,256]{1,0:T(8,128)(2,1)}, u32[]{:S(2)}) copy-start(bf16[256,256]{1,0:T(8,128)(2,1)} %constant.25.clone.perm_ref) | copy-start | bytes 393220
  70.3 35.8 %copy-start.4 = (bf16[256,256]{1,0:T(8,128)(2,1)S(1)}, bf16[256,256]{1,0:T(8,128)(2,1)}, u32[]{:S(2)}) copy-start(bf16[256,256]{1,0:T(8,128)(2,1)} %constant.26.clone.back_ref) | copy-start | bytes 393220
  106.1 4.9 %collective-permute-start.6 = (bf16[64,16,1024]{2,1,0:T(8,128)(2,1)S(1)}, bf16[64,16,1024]{2,1,0:T(8,128)(2,1)S(1)}, u32[]{:S(2)}, u32[]{:S(2)}) collective-permute-start(bf16[64,16,1024]{2,1,0:T(8,128)(2,1)S(1)} %all_to_all.16.rows_ref), channel_id=1, source_target_pairs={{0,32},{32,0},{1,33},{33,1},{2,34},{34,2},{3,35},{35,3},{4,36},{36... | collective-permute-start | bytes 6291464 | tf_op jit(solution)/shard_map/ppermute | solution.py:307
  115.9 4.3 %collective-permute-start.7 = (bf16[64,16,1024]{2,1,0:T(8,128)(2,1)S(1)}, bf16[64,16,1024]{2,1,0:T(8,128)(2,1)S(1)}, u32[]{:S(2)}, u32[]{:S(2)}) collective-permute-start(bf16[64,16,1024]{2,1,0:T(8,128)(2,1)S(1)} %experts.3), channel_id=1, source_target_pairs={{0,32},{32,0},{1,33},{33,1},{2,34},{34,2},{3,35},{35,3},{4,36},{36... | collective-permute-start | bytes 6291464 | tf_op jit(solution)/shard_map/ppermute | solution.py:307
  121.3 36.3 %copy-start.9 = (f32[8,8]{1,0:T(8,128)S(1)}, f32[8,8]{1,0:T(8,128)}, u32[]{:S(2)}) copy-start(f32[8,8]{1,0:T(8,128)} %gates_ref.1) | copy-start | bytes 772

commit v5 on v4

--- a/solution.py
+++ b/solution.py
@@ -11,7 +11,7 @@
 
 HEAD_DIM = 128
 SEQ = ("yh", "core")
-MP = ("x", "yl", "z")
+MP = ("x", "yl", "zh", "zl")
 NEG = -1e30
 BF = jnp.bfloat16
 F32 = jnp.float32
@@ -22,31 +22,38 @@
     first, info, spans, qa_ref, qb_ref, kc_ref, vc_ref, kn_ref, vn_ref, oa_ref, ob_ref, s_ref
 ):
     rows = qa_ref.shape[0]
+    heads = qa_ref.shape[1] // HEAD_DIM
+    cache_rows = kc_ref.shape[1]
     chunk = kn_ref.shape[1]
-    chunks = kc_ref.shape[1] // chunk
+    chunks = cache_rows // chunk
     coef = math.log2(math.e) / math.sqrt(HEAD_DIM)
     valid = info[1]
-    key_pos = info[2] * rows + lax.broadcasted_iota(jnp.int32, (1, chunk), 1)
+    key_pos = info[2] * chunk + lax.broadcasted_iota(jnp.int32, (1, chunk), 1)
     lane = lax.broadcasted_iota(jnp.int32, (rows, 128), 1)
     column = lax.broadcasted_iota(jnp.int32, (1, chunk), 1)
+    row = lax.broadcasted_iota(jnp.int32, (2 * rows, 1), 0) & (rows - 1)
     for b, (q_ref, out_ref) in enumerate(((qa_ref, oa_ref), (qb_ref, ob_ref))):
-        pos = (info[2] ^ (first + b)) * rows + lax.broadcasted_iota(jnp.int32, (rows, 1), 0)
+        pos = (info[2] ^ (first + b)) * chunk + row + (row & ~7) + info[3] * 8
         limit = pos
         for a in range(3):
             start, end = spans[0, a], spans[1, a]
             limit = jnp.where((pos >= start) & (pos < end), jnp.maximum(limit, end - 1), limit)
         tract_ok = key_pos <= limit
         stats = jnp.zeros((rows, 128), F32)
-        for h in range(2):
-            at = 2 * b + h
-            q = q_ref[:, h * HEAD_DIM : (h + 1) * HEAD_DIM]
+        for pair in range(heads // 2):
+            at = heads // 2 * b + pair
+            cols = [
+                slice((2 * pair + j) * HEAD_DIM, (2 * pair + j + 1) * HEAD_DIM) for j in range(2)
+            ]
+            q = jnp.concatenate([q_ref[:, cols[0]], q_ref[:, cols[1]]], axis=0)
             top = None
             for c in range(chunks + 1):
-                k = kc_ref[0, c * chunk : (c + 1) * chunk, :] if c < chunks else kn_ref[0]
-                s = lax.dot_general(q, k, ANY_LAST, preferred_element_type=F32)
                 if c < chunks:
+                    k = kc_ref[0, c * chunk : (c + 1) * chunk, :]
+                    s = lax.dot_general(q, k, ANY_LAST, preferred_element_type=F32)
                     s = s + jnp.where(column < valid - c * chunk, 0.0, NEG)
                 else:
+                    s = lax.dot_general(q, kn_ref[0], ANY_LAST, preferred_element_type=F32)
                     s = jnp.where(tract_ok, s, NEG)
                 s_ref[at, :, c * chunk : (c + 1) * chunk] = s
                 top = s if top is None else jnp.maximum(top, s)
@@ -60,22 +67,28 @@
                 part = jnp.dot(p.astype(BF), v, preferred_element_type=F32)
                 acc = part if acc is None else acc + part
             total = jnp.sum(total, axis=1, keepdims=True)
-            out_ref[0:rows, h * HEAD_DIM : (h + 1) * HEAD_DIM] = (acc / total).astype(BF)
+            result = (acc / total).astype(BF)
             level = m + jnp.log2(total)
-            for part in range(3):
-                piece = level.astype(BF).astype(F32)
-                level = level - piece
-                stats = jnp.where(lane == 3 * h + part, piece, stats)
-        out_ref[rows : rows + 16, :] = stats.T[0:16, :].astype(BF)
+            for j in range(2):
+                out_ref[0:rows, cols[j]] = result[j * rows : (j + 1) * rows]
+                rest = level[j * rows : (j + 1) * rows]
+                for part in range(3):
+                    piece = rest.astype(BF).astype(F32)
+                    rest = rest - piece
+                    stats = jnp.where(lane == 3 * (2 * pair + j) + part, piece, stats)
+        turned = stats.T[0:16, :].astype(BF)
+        out_ref[rows : rows + 16, 0:rows] = turned
+        out_ref[rows : rows + 16, rows:] = jnp.zeros((16, out_ref.shape[1] - rows), BF)
 
 
 def attend(first, info, spans, qa, qb, cache_kv, new_kv):
-    rows = qa.shape[0]
+    rows, width = qa.shape
     cache_rows, new_rows = cache_kv.shape[1], new_kv.shape[1]
     keys = cache_rows + new_rows
-    whole = pl.BlockSpec((rows, 2 * HEAD_DIM), lambda i, t, u: (0, 0))
-    result = pl.BlockSpec((rows + 16, 2 * HEAD_DIM), lambda i, t, u: (0, 0))
-    shape = jax.ShapeDtypeStruct((rows + 16, 2 * HEAD_DIM), BF)
+    whole = pl.BlockSpec((rows, width), lambda i, t, u: (0, 0))
+    result = pl.BlockSpec((rows + 16, width), lambda i, t, u: (0, 0))
+    shape = jax.ShapeDtypeStruct((rows + 16, width), BF)
+    heads = width // HEAD_DIM
     return pl.pallas_call(
         functools.partial(attn_kernel, first),
         grid_spec=pltpu.PrefetchScalarGridSpec(
@@ -90,60 +103,82 @@
                 pl.BlockSpec((1, new_rows, HEAD_DIM), lambda i, t, u: (1, 0, t[0])),
             ],
             out_specs=[result, result],
-            scratch_shapes=[pltpu.VMEM((4, rows, keys), F32)],
+            scratch_shapes=[pltpu.VMEM((heads, 2 * rows, keys), F32)],
         ),
         out_shape=[shape, shape],
-        compiler_params=pltpu.CompilerParams(vmem_limit_bytes=50 << 20),
+        compiler_params=pltpu.CompilerParams(vmem_limit_bytes=48 << 20),
         cost_estimate=pl.CostEstimate(
-            flops=32 * rows * keys * HEAD_DIM,
+            flops=8 * heads * rows * keys * HEAD_DIM,
             bytes_accessed=4 * keys * HEAD_DIM,
-            transcendentals=4 * rows * keys,
+            transcendentals=2 * heads * rows * keys,
         ),
         name="attend",
     )(info, spans, qa, qb, cache_kv, cache_kv, new_kv, new_kv)
 
 
-def project_kernel(a_ref, b_ref, c_ref, d_ref, w_ref, out_ref, att_ref):
+def merge_kernel(a_ref, b_ref, c_ref, d_ref, out_ref):
     parts = (a_ref, b_ref, c_ref, d_ref)
-    rows = out_ref.shape[0]
+    rows, heads = out_ref.shape[0], a_ref.shape[1] // HEAD_DIM
     pad = jnp.zeros((112, rows), F32)
     stats = [
-        jnp.concatenate([p[rows : rows + 16, :].astype(F32), pad], axis=0).T for p in parts
+        jnp.concatenate([p[rows : rows + 16, 0:rows].astype(F32), pad], axis=0).T for p in parts
     ]
-    for h in range(2):
+    for h in range(heads):
         cols = slice(h * HEAD_DIM, (h + 1) * HEAD_DIM)
         at = 3 * h
         levels = [
             t[:, at : at + 1] + t[:, at + 1 : at + 2] + t[:, at + 2 : at + 3] for t in stats
         ]
-        best = jnp.maximum(
-            jnp.maximum(levels[0], levels[1]), jnp.maximum(levels[2], levels[3])
-        )
+        best = jnp.maximum(jnp.maximum(levels[0], levels[1]), jnp.maximum(levels[2], levels[3]))
         weights = [jnp.exp2(v - best) for v in levels]
         total = weights[0] + weights[1] + weights[2] + weights[3]
         acc = None
         for w, p in zip(weights, parts):
             term = p[0:rows, cols].astype(F32) * w
             acc = term if acc is None else acc + term
-        att_ref[:, cols] = (acc / total).astype(BF)
-    out_ref[...] = jnp.dot(att_ref[...], w_ref[...], preferred_element_type=F32).astype(BF)
-
-
-def project(parts, out_proj):
+        out_ref[:, cols] = (acc / total).astype(BF)
+
+
+def merge(parts):
     rows, depth = parts[0].shape[0] - 16, parts[0].shape[1]
-    width = out_proj.shape[1]
+    return pl.pallas_call(
+        merge_kernel,
+        in_specs=[pl.BlockSpec(memory_space=pltpu.VMEM)] * 4,
+        out_specs=pl.BlockSpec(memory_space=pltpu.VMEM),
+        out_shape=jax.ShapeDtypeStruct((rows, depth), BF),
+        compiler_params=pltpu.CompilerParams(vmem_limit_bytes=10 << 20),
+        cost_estimate=pl.CostEstimate(flops=1 << 20, bytes_accessed=5 << 17, transcendentals=0),
+        name="merge",
+    )(*parts)
+
+
+def project_kernel(core_ref, mine_ref, other_ref, own_ref, near_ref, out_ref):
+    rows = mine_ref.shape[0]
+    half = own_ref.shape[0]
+    core = core_ref[0]
+    for att, side in ((mine_ref, core), (other_ref, 1 - core)):
+        at = pl.multiple_of(side * rows, rows)
+        out_ref[pl.ds(at, rows), :] = (
+            jnp.dot(att[:, :half], own_ref[...], preferred_element_type=F32)
+            + jnp.dot(att[:, half:], near_ref[...], preferred_element_type=F32)
+        ).astype(BF)
+
+
+def project(core, mine, other, own, near):
+    rows, depth = mine.shape
+    width = own.shape[1]
     return pl.pallas_call(
         project_kernel,
-        in_specs=[pl.BlockSpec(memory_space=pltpu.VMEM)] * 5,
+        in_specs=[pl.BlockSpec(memory_space=pltpu.SMEM)]
+        + [pl.BlockSpec(memory_space=pltpu.VMEM)] * 4,
         out_specs=pl.BlockSpec(memory_space=pltpu.VMEM),
-        out_shape=jax.ShapeDtypeStruct((rows, width), BF),
-        scratch_shapes=[pltpu.VMEM((rows, depth), BF)],
-        compiler_params=pltpu.CompilerParams(vmem_limit_bytes=16 << 20),
+        out_shape=jax.ShapeDtypeStruct((2 * rows, width), BF),
+        compiler_params=pltpu.CompilerParams(vmem_limit_bytes=10 << 20),
         cost_estimate=pl.CostEstimate(
-            flops=2 * rows * depth * width, bytes_accessed=4 * depth * width, transcendentals=0
+            flops=4 * rows * depth * width, bytes_accessed=2 * depth * width, transcendentals=0
         ),
         name="project",
-    )(*parts, out_proj)
+    )(core.reshape(1), mine, other, own, near)
 
 
 def slot_table(flat, routes_ref, values, columns):
@@ -166,7 +201,35 @@
     return jnp.where(chunk == ((column >> 2) & 3), table, 0.0)
 
 
-def settle_kernel(flat, arrived_ref, residual_ref, gain_ref, routes_ref, stream_ref, out_ref):
+def tables_kernel(flat, routes_ref, gates_ref, pick_ref, share_ref):
+    gates = gates_ref[...]
+    gates = gates / jnp.sum(gates, axis=1, keepdims=True)
+    columns = pick_ref.shape[1]
+    pick_ref[...] = slot_table(flat, routes_ref, None, columns).astype(BF)
+    share = slot_table(flat, routes_ref, jnp.concatenate([gates] * 4, axis=0), columns)
+    coarse = share.astype(BF).astype(F32)
+    pieces = jnp.concatenate([coarse, share - coarse], axis=0).astype(BF)
+    share_ref[:, :columns] = pieces
+    share_ref[:, columns:] = pieces
+
+
+def tables(routes, gates, columns):
+    rows = 4 * routes.shape[0]
+    return pl.pallas_call(
+        tables_kernel,
+        in_specs=[pl.BlockSpec(memory_space=pltpu.SMEM)]
+        + [pl.BlockSpec(memory_space=pltpu.VMEM)] * 2,
+        out_specs=[pl.BlockSpec(memory_space=pltpu.VMEM)] * 2,
+        out_shape=[
+            jax.ShapeDtypeStruct((rows, columns), BF),
+            jax.ShapeDtypeStruct((2 * rows, 2 * columns), BF),
+        ],
+        compiler_params=pltpu.CompilerParams(vmem_limit_bytes=10 << 20),
+        name="tables",
+    )(routes, routes, gates)
+
+
+def settle_kernel(arrived_ref, residual_ref, gain_ref, pick_ref, stream_ref, out_ref):
     tok, width = residual_ref.shape
     groups = arrived_ref.shape[0]
     chunk = out_ref.shape[2]
@@ -175,9 +238,11 @@
     square = None
     for c in range(chunks):
         cols = slice(c * chunk, (c + 1) * chunk)
-        acc = arrived_ref[0, :, cols].astype(F32)
-        for g in range(1, groups):
-            acc = acc + arrived_ref[g, :, cols].astype(F32)
+        first = 0 if c < chunks // 2 else groups // 2
+        part = slice(c % 2 * chunk, (c % 2 + 1) * chunk)
+        acc = arrived_ref[first, :, part].astype(F32)
+        for g in range(first + 1, first + groups // 2):
+            acc = acc + arrived_ref[g, :, part].astype(F32)
         stream = (residual_ref[:, cols].astype(F32) + acc).astype(BF)
         stream_ref[:, cols] = stream
         piece = stream.astype(F32)
@@ -190,33 +255,31 @@
     ]
     stacked = jnp.concatenate(normed, axis=0).astype(BF)
     half = out_ref.shape[0] // 2
-    pick = slot_table(flat, routes_ref, None, half * 16).astype(BF)
     rows = lax.dot_general(
-        pick, stacked, (((0,), (0,)), ((), ())), preferred_element_type=F32
+        pick_ref[...], stacked, (((0,), (0,)), ((), ())), preferred_element_type=F32
     ).astype(BF)
     rows = rows.reshape(half, 16, chunk)
     out_ref[0:half] = rows
     out_ref[half : 2 * half] = rows
 
 
-def settle(arrived, residual, gain, routes, devices):
+def settle(arrived, residual, gain, pick):
     tok, width = residual.shape
     chunk = width // 4
     return pl.pallas_call(
         settle_kernel,
-        in_specs=[pl.BlockSpec(memory_space=pltpu.SMEM)]
-        + [pl.BlockSpec(memory_space=pltpu.VMEM)] * 4,
+        in_specs=[pl.BlockSpec(memory_space=pltpu.VMEM)] * 4,
         out_specs=[pl.BlockSpec(memory_space=pltpu.VMEM)] * 2,
         out_shape=[
             jax.ShapeDtypeStruct((tok, width), BF),
-            jax.ShapeDtypeStruct((devices, 16, chunk), BF),
+            jax.ShapeDtypeStruct((pick.shape[1] // 8, 16, chunk), BF),
         ],
         compiler_params=pltpu.CompilerParams(vmem_limit_bytes=10 << 20),
         cost_estimate=pl.CostEstimate(
             flops=1 << 26, bytes_accessed=4 << 20, transcendentals=0
         ),
         name="settle",
-    )(routes, arrived, residual, gain.reshape(1, width), routes)
+    )(arrived, residual, gain.reshape(1, width), pick)
 
 
 def expert_kernel(rows_ref, perm_ref, back_ref, win_ref, wout_ref, out_ref, x_ref, z_ref):
@@ -269,18 +332,10 @@
     )(rows, perm, back, w_in, w_out)
 
 
-def combine_kernel(flat, routes_ref, gates_ref, returned_ref, stream_ref, out_ref):
+def combine_kernel(share_ref, returned_ref, stream_ref, out_ref):
     tok = stream_ref.shape[0]
     chunk = returned_ref.shape[1]
-    gates = gates_ref[...]
-    gates = gates / jnp.sum(gates, axis=1, keepdims=True)
-    share = slot_table(
-        flat, routes_ref, jnp.concatenate([gates] * 4, axis=0), returned_ref.shape[0] // 2
-    )
-    coarse = share.astype(BF).astype(F32)
-    pieces = jnp.concatenate([coarse, share - coarse], axis=0).astype(BF)
-    pieces = jnp.concatenate([pieces, pieces], axis=1)
-    both = jnp.dot(pieces, returned_ref[...], preferred_element_type=F32)
+    both = jnp.dot(share_ref[...], returned_ref[...], preferred_element_type=F32)
     half = both.shape[0] // 2
     total = both[:half] + both[half:]
     for c in range(half // tok):
@@ -290,16 +345,15 @@
         ).astype(BF)
 
 
-def combine(routes, gates, returned, stream):
+def combine(share, returned, stream):
     return pl.pallas_call(
         combine_kernel,
-        in_specs=[pl.BlockSpec(memory_space=pltpu.SMEM)]
-        + [pl.BlockSpec(memory_space=pltpu.VMEM)] * 4,
+        in_specs=[pl.BlockSpec(memory_space=pltpu.VMEM)] * 3,
         out_specs=pl.BlockSpec(memory_space=pltpu.VMEM),
         out_shape=jax.ShapeDtypeStruct(stream.shape, BF),
         compiler_params=pltpu.CompilerParams(vmem_limit_bytes=10 << 20),
         name="combine",
-    )(routes, routes, gates, returned, stream)
+    )(share, returned, stream)
 
 
 def swap(v, axes, bit):
@@ -329,10 +383,21 @@
     quarter = width // 4
     spread = ("yh",) + MP
 
-    query_parts = [queries] + [swap(queries, SEQ, d) for d in (1, 2, 3)]
+    core, parity = lax.axis_index("core"), lax.axis_index("zl")
+    blocks = queries.reshape(tract // (2 * tok), 2, tok, queries.shape[1])
+    stay = lax.dynamic_index_in_dim(blocks, parity, 1, keepdims=False)
+    leave = lax.dynamic_index_in_dim(blocks, 1 - parity, 1, keepdims=False)
+    rows = tract // 2
+    came = swap(leave.reshape(rows, -1), ("zl",), 1)
+    mine_q = jnp.concatenate([stay.reshape(rows, -1), came], axis=1)
+    columns = lax.dynamic_slice_in_dim(out_proj, core * (width // 2), width // 2, 1)
+    columns, mine_q = lax.optimization_barrier((columns, mine_q))
+    near = swap(columns, ("zl",), 1)
+
+    query_parts = [mine_q] + [swap(mine_q, SEQ, d) for d in (1, 2, 3)]
     valid = jnp.clip(cached_len[0] - seq * cache, 0, cache)
 
-    info = jnp.stack([lax.axis_index("x"), valid, seq]).astype(jnp.int32)
+    info = jnp.stack([lax.axis_index("x"), valid, seq, parity]).astype(jnp.int32)
     spans = image_spans.T
 
     def attend_pair(d):
@@ -343,19 +408,27 @@
         (mine, query_parts[2], query_parts[3])
     )
     across, diagonal = attend_pair(2)
-    across, diagonal, w_in = lax.optimization_barrier((across, diagonal, w_in))
+    across, diagonal, w_in, routes, gate_weights = lax.optimization_barrier(
+        (across, diagonal, w_in, routes, gate_weights)
+    )
     turned = w_in.transpose(0, 2, 1, 3)
+    pick, share = tables(routes, gate_weights, 512)
     parts = [mine, swap(beside, SEQ, 1), swap(across, SEQ, 2), swap(diagonal, SEQ, 3)]
-    parts, turned = lax.optimization_barrier((parts, turned))
-    partial = project(parts, out_proj)
+    parts, turned, pick, share = lax.optimization_barrier((parts, turned, pick, share))
+    merged = merge(parts)
+    partial = project(core, merged, swap(merged, ("core",), 1), columns, near)
     arrived = lax.all_to_all(
-        partial.reshape(32, tok, width), MP, split_axis=0, concat_axis=0, tiled=True
+        partial.reshape(32, tok, width // 2),
+        ("core", "x", "yl", "zh"),
+        split_axis=0,
+        concat_axis=0,
+        tiled=True,
     )
 
     perm = np.eye(256).reshape(16, 4, 2, 2, 256).transpose(2, 1, 0, 3, 4).reshape(256, 256)
     perm, back = jnp.asarray(perm, BF), jnp.asarray(perm.T, BF)
 
-    stream, outgoing = settle(arrived, residual, norm_gain, routes, 64)
+    stream, outgoing = settle(arrived, residual, norm_gain, pick)
 
     own = lax.all_to_all(outgoing, spread, split_axis=0, concat_axis=0, tiled=True)
     other = swap(own, ("core",), 1)
@@ -365,11 +438,11 @@
     got = swap(sent, ("core",), 1)
     summed = (kept.astype(F32) + got.astype(F32)).astype(BF)
     returned = lax.all_to_all(summed, spread, split_axis=0, concat_axis=0, tiled=True)
-    return combine(routes, gate_weights, returned.reshape(-1, quarter), stream)
+    return combine(share, returned.reshape(-1, quarter), stream)
 
 
 def solution(mesh):
-    fine = Mesh(mesh.devices.reshape(2, 2, 4, 2, 4), SEQ + MP)
+    fine = Mesh(mesh.devices.reshape(2, 2, 4, 2, 2, 2), SEQ + MP)
     in_specs = (
         P(SEQ, MP),
         P(None, SEQ, None),

time: 160 us -> 158 us (0.988)
  blocking collectives: 109 us -> 99.7 us
  starting transfers between devices: 7.71 us -> 12.3 us
  waiting for transfers between devices: 3.8 us -> 6.06 us
    all_to_all x1, blocking collectives: 37 us -> 27.2 us  [local(): lax.all_to_all(partial.reshape(32, tok, width // 2), ('core', 'x', 'yl',...]
    ppermute x8 -> x11, starting transfers between devices: 7.71 us -> 12.3 us  [swap(): return lax.ppermute(v, axes, [(i, i ^ bit) for i in range(count)])]
    ppermute x8 -> x11, waiting for transfers between devices: 3.8 us -> 6.06 us  [swap(): return lax.ppermute(v, axes, [(i, i ^ bit) for i in range(count)])]
    pallas_call x2, Pallas kernels: 12 us -> 9.89 us  [attend(): pl.pallas_call(functools.partial(attn_kernel, first), grid_spec=pltpu.Pre...]
  transfers between devices with their start and end apart: 8 -> 11, of which waited for: 1 -> 3; matrix products, arithmetic and copies ran while one was open for 5% -> 6% of each run, Pallas kernels for 7% -> 10%
where the time goes in v5:
time: 158 us; the launch traced here: 157 us
  blocking collectives  99.7 us (63%)
  Pallas kernels  25.1 us (16%)
  starting transfers between devices  12.3 us (8%)
  local copies, waits for them, and re-layouts  11.9 us (8%)
  waiting for transfers between devices  6.06 us (4%)
    all_to_all x1, blocking collectives, local(): lax.all_to_all(summed, spread, split_axis=0, concat_axis=0, tiled=True)  36.9 us
    all_to_all x1, blocking collectives, local(): lax.all_to_all(outgoing, spread, split_axis=0, concat_axis=0, tiled=True)  35.6 us
    all_to_all x1, blocking collectives, local(): lax.all_to_all(partial.reshape(32, tok, width // 2), ('core', 'x', 'yl',...  27.2 us
    ppermute x11, starting transfers between devices, swap(): return lax.ppermute(v, axes, [(i, i ^ bit) for i in range(count)])  12.3 us
    pallas_call x2, Pallas kernels, attend(): pl.pallas_call(functools.partial(attn_kernel, first), grid_spec=pltpu.Pre...  9.89 us
    pallas_call x2, Pallas kernels, experts(): pl.pallas_call(expert_kernel, in_specs=[pl.BlockSpec(memory_space=pltpu.V...  9.6 us
    optimization_barrier x1, local copies, waits for them, and re-layouts, local(): lax.optimization_barrier((across, diagonal, w_in, routes, gate_weights))  7.58 us
    ppermute x11, waiting for transfers between devices, swap(): return lax.ppermute(v, axes, [(i, i ^ bit) for i in range(count)])  6.06 us
  transfers between devices with their start and end apart: 11, of which 3 were waited for; matrix products, arithmetic and copies ran while one was open for 6% of the time, Pallas kernels for 10%

profile of v5, /device:TPU:0, one launch (start us, length us, event | category | flops | bytes accessed | tf_op | source)
XLA Modules:
  0.0 157.2 jit_solution(7123625668110236131)
XLA Ops:
  0.0 0.0 copy-start
  0.0 0.0 copy-start.9
  0.0 0.0 copy-start.3
  0.0 1.0 dynamic-slice_bitcast_fusion.1
  1.0 2.1 %collective-permute-start = (bf16[128,256]{1,0:T(8,128)(2,1)S(1)}, bf16[128,256]{1,0:T(8,128)(2,1)S(1)}, u32[]{:S(2)}, u32[]{:S(2)}) collective-permute-start(bf16[128,256]{1,0:T(8,128)(2,1)S(1)} %get-tuple-element.60), channel_id=1, source_target_pairs={{0,1},{1,0},{2,3},{3,2},{4,5},{5,4},{6,7},{7,6},{8,9},{9,8},{10,11... | collective-permute-start | bytes 196616 | tf_op jit(solution)/shard_map/ppermute | solution.py:361
  3.1 0.0 copy-done
  3.1 1.1 constant_dynamic-slice_fusion.own_ref
  4.2 1.1 collective-permute-done
  5.4 2.1 %collective-permute-start.8 = (bf16[256,2048]{1,0:T(8,128)(2,1)}, bf16[256,2048]{1,0:T(8,128)(2,1)}, u32[]{:S(2)}, u32[]{:S(2)}) collective-permute-start(bf16[256,2048]{1,0:T(8,128)(2,1)} %constant_dynamic-slice_fusion.own_ref), channel_id=1, source_target_pairs={{0,1},{1,0},{2,3},{3,2},{4,5},{5,4},{6,7},{7,6},{8,9},{9,8},{10,11... | collective-permute-start | bytes 3145736 | tf_op jit(solution)/shard_map/ppermute | solution.py:361
  7.5 0.0 collective-permute-start.1
  8.2 3.3 %collective-permute-start.2 = (bf16[128,512]{1,0:T(8,128)(2,1)S(1)}, bf16[128,512]{1,0:T(8,128)(2,1)S(1)}, u32[]{:S(2)}, u32[]{:S(2)}) collective-permute-start(bf16[128,512]{1,0:T(8,128)(2,1)S(1)} %pad_maximum_fusion.qa_ref), channel_id=1, source_target_pairs={{0,64},{32,96},{64,0},{96,32},{1,65},{33,97},{65,1},{97,33},{2,66}... | collective-permute-start | bytes 393224 | tf_op jit(solution)/shard_map/ppermute | solution.py:361
  11.4 0.2 collective-permute-start.3
  11.6 0.1 pad_add_fusion.info
  11.7 0.0 collective-permute-done.1.qb_ref
  11.7 0.0 copy-done.9
  11.7 0.0 copy-done.3
  11.7 0.0 copy-start.1
  11.7 2.2 %copy-done.1 = bf16[2,2048,512]{2,1,0:T(8,128)(2,1)S(1)} copy-done((bf16[2,2048,512]{2,1,0:T(8,128)(2,1)S(1)}, bf16[2,2048,512]{2,1,0:T(8,128)(2,1)}, u32[]{:S(2)}) %copy-start.1) | copy-done | bytes 4194328
  13.9 0.0 copy-start.2
  13.9 4.9 %attend.2 = (bf16[144,512]{1,0:T(8,128)(2,1)S(1)}, bf16[144,512]{1,0:T(8,128)(2,1)S(1)}) custom-call(s32[4]{0:T(128)S(1)} %pad_add_fusion.info, s32[2,3]{1,0:T(2,128)S(1)} %bitcast.30, bf16[128,512]{1,0:T(8,128)(2,1)S(1)} %pad_maximum_fusion.qa_ref, bf16[128,512]{1,0:T(8,128)(2,1)S(1)} %collective-permute-done.1.qb_ref, bf16[2,2048,512]{2,1,0:T(8,128)(2,1)S(1)} %copy-done.1, ...), custom_call_target="tpu_custom_call" | custom-call | flops 1207959552 | bytes 1179648 | tf_op jit(solution)/shard_map/attend/pallas_call | solution.py:92
  18.9 0.0 collective-permute-done.2.qa_ref
  18.9 0.0 collective-permute-done.3.qb_ref
  18.9 0.0 copy-done.2
  18.9 0.0 slice-start
  18.9 4.9 %attend.3 = (bf16[144,512]{1,0:T(8,128)(2,1)S(1)}, bf16[144,512]{1,0:T(8,128)(2,1)S(1)}) custom-call(s32[4]{0:T(128)S(1)} %pad_add_fusion.info, s32[2,3]{1,0:T(2,128)S(1)} %bitcast.31, bf16[128,512]{1,0:T(8,128)(2,1)S(1)} %collective-permute-done.2.qa_ref, bf16[128,512]{1,0:T(8,128)(2,1)S(1)} %collective-permute-done.3.qb_ref, ...), custom_call_target="tpu_custom_call" | custom-call | flops 1207959552 | bytes 1179648 | tf_op jit(solution)/shard_map/attend/pallas_call | solution.py:92
  23.9 3.3 %collective-permute-start.5 = (bf16[144,512]{1,0:T(8,128)(2,1)S(1)}, bf16[144,512]{1,0:T(8,128)(2,1)S(1)}, u32[]{:S(2)}, u32[]{:S(2)}) collective-permute-start(bf16[144,512]{1,0:T(8,128)(2,1)S(1)} %get-tuple-element.40), channel_id=1, source_target_pairs={{0,64},{32,96},{64,0},{96,32},{1,65},{33,97},{65,1},{97,33},{2,66}... | collective-permute-start | bytes 442376 | tf_op jit(solution)/shard_map/ppermute | solution.py:361
  27.1 0.0 collective-permute-start.6
  27.1 0.0 copy-start.8
  27.1 0.0 copy-start.10
  27.1 0.0 slice-start.1
  27.1 0.5 collective-permute-start.4
  27.6 7.6 %copy.21 = bf16[2,4096,2,384]{3,1,2,0:T(8,128)(2,1)S(1)} copy(bf16[2,4096,2,384]{3,2,1,0:T(2,128)(2,1)} %param.24) | data formatting | bytes 25165824 | tf_op jit(solution)/shard_map/optimization_barrier | solution.py:411
  35.2 0.0 copy-done.8
  35.2 0.0 copy-done.10
  35.2 0.9 tables.1
  36.1 0.0 collective-permute-done.5.c_ref
  36.2 0.0 collective-permute-done.6.d_ref
  36.2 0.0 collective-permute-done.4.b_ref
  36.2 0.6 merge.1.mine_ref
  36.8 0.3 collective-permute-start.7
  37.2 1.1 collective-permute-done.7.other_ref
  38.3 0.0 collective-permute-done.8.near_ref
  38.3 0.0 copy-start.6
  38.3 2.3 %project.1 = bf16[256,2048]{1,0:T(8,128)(2,1)S(1)} custom-call(s32[1]{0:T(128)} %bitcast.10.core_ref, bf16[128,512]{1,0:T(8,128)(2,1)S(1)} %merge.1.mine_ref, bf16[128,512]{1,0:T(8,128)(2,1)S(1)} %collective-permute-done.7.other_ref, bf16[256,2048]{1,0:T(8,128)(2,1)} %constant_dynamic-slice_fusion.own_ref, bf16[256,2048]{1,0:T(8,128)(2,1)} %collective-permute-done.8.near_ref), custom_call_target="tpu_custom_call" | custom-call | flops 536870912 | bytes 2097152 | tf_op jit(solution)/shard_map/project/pallas_call | solution.py:170
  40.6 27.2 %all_to_all.15.arrived_ref = bf16[32,8,2048]{2,1,0:T(8,128)(2,1)S(1)} all-to-all(bf16[32,8,2048]{2,1,0:T(8,128)(2,1)S(1)} %bitcast.28), channel_id=1, replica_groups=mesh['yh'=2,'core'=2,'x'=4,'yl'=2,'zh'=2,'zl'=2] {'core','x','yl','zh'}, dimensions={0} | all-to-all | bytes 2097152 | tf_op jit(solution)/shard_map/all_to_all | solution.py:420
  67.8 0.0 copy-done.6
  67.8 0.0 copy-done.7
  67.8 0.7 settle.1
  68.4 0.0 copy-start.4
  68.4 0.0 copy-start.5
  68.5 35.6 %all_to_all.16.rows_ref = bf16[64,16,1024]{2,1,0:T(8,128)(2,1)S(1)} all-to-all(bf16[64,16,1024]{2,1,0:T(8,128)(2,1)S(1)} %get-tuple-element.54), channel_id=1, replica_groups=mesh['yh'=2,'core'=2,'x'=4,'yl'=2,'zh'=2,'zl'=2] {'yh','x','yl','zh','zl'}, dimensions={0} | all-to-all | bytes 4194304 | tf_op jit(solution)/shard_map/all_to_all | solution.py:433
  104.1 0.0 collective-permute-start.9
  104.1 0.0 slice-done
  104.1 0.0 slice-done.1
  104.1 0.0 copy-done.4
  104.1 0.0 copy-done.5
  104.1 4.8 %experts.2 = bf16[64,16,1024]{2,1,0:T(8,128)(2,1)S(1)} custom-call(bf16[64,16,1024]{2,1,0:T(8,128)(2,1)S(1)} %all_to_all.16.rows_ref, bf16[256,256]{1,0:T(8,128)(2,1)S(1)} %copy-done.4, bf16[256,256]{1,0:T(8,128)(2,1)S(1)} %copy-done.5, bf16[2,2,4096,384]{3,2,1,0:T(8,128)(2,1)S(1)} %bitcast.23, bf16[2,384,4096]{2,1,0:T(8,128)(2,1)S(1)} %bitcast.26), custom_call_target="tpu_custom_call" | custom-call | flops 2415919104 | bytes 18874368 | tf_op jit(solution)/shard_map/experts/pallas_call | solution.py:316
  108.9 0.0 collective-permute-done.9.rows_ref
  108.9 4.8 %experts.3 = bf16[64,16,1024]{2,1,0:T(8,128)(2,1)S(1)} custom-call(bf16[64,16,1024]{2,1,0:T(8,128)(2,1)S(1)} %collective-permute-done.9.rows_ref, bf16[256,256]{1,0:T(8,128)(2,1)S(1)} %copy-done.4, bf16[256,256]{1,0:T(8,128)(2,1)S(1)} %copy-done.5, bf16[2,2,4096,384]{3,2,1,0:T(8,128)(2,1)S(1)} %bitcast.24, bf16[2,384,4096]{2,1,0:T(8,128)(2,1)S(1)} %bitcast.26), custom_call_target="tpu_custom_call" | custom-call | flops 2415919104 | bytes 18874368 | tf_op jit(solution)/shard_map/experts/pallas_call | solution.py:316
  113.7 0.6 collective-permute-start.10
  114.3 3.8 %collective-permute-done.10 = bf16[64,16,1024]{2,1,0:T(8,128)(2,1)S(1)} collective-permute-done((bf16[64,16,1024]{2,1,0:T(8,128)(2,1)S(1)}, bf16[64,16,1024]{2,1,0:T(8,128)(2,1)S(1)}, u32[]{:S(2)}, u32[]{:S(2)}) %collective-permute-start.10) | collective-permute-done | bytes 2097184 | tf_op jit(solution)/shard_map/ppermute | solution.py:361
  118.1 1.1 add_convert_fusion
  119.2 36.9 %all_to_all.17 = bf16[64,16,1024]{2,1,0:T(8,128)(2,1)S(1)} all-to-all(bf16[64,16,1024]{2,1,0:T(8,128)(2,1)S(1)} %add_convert_fusion), channel_id=1, replica_groups=mesh['yh'=2,'core'=2,'x'=4,'yl'=2,'zh'=2,'zl'=2] {'yh','x','yl','zh','zl'}, dimensions={0} | all-to-all | bytes 4194304 | tf_op jit(solution)/shard_map/all_to_all | solution.py:440
  156.1 1.1 combine.1
  (3 shorter events, 0.0 us)
Async XLA Ops:
  0.0 3.1 %copy-start = (bf16[256,4096]{1,0:T(8,128)(2,1)S(1)}, bf16[256,4096]{1,0:T(8,128)(2,1)}, u32[]{:S(2)}) copy-start(bf16[256,4096]{1,0:T(8,128)(2,1)} %param.20) | copy-start | bytes 6291460
  0.0 11.7 %copy-start.9 = (s32[3,2]{0,1:T(2,128)S(1)}, s32[3,2]{0,1:T(2,128)}, u32[]{:S(2)}) copy-start(s32[3,2]{0,1:T(2,128)} %param.18) | copy-start | bytes 76
  0.0 11.7 %copy-start.3 = (bf16[2,256,512]{2,1,0:T(8,128)(2,1)S(1)}, bf16[2,256,512]{2,1,0:T(8,128)(2,1)}, u32[]{:S(2)}) copy-start(bf16[2,256,512]{2,1,0:T(8,128)(2,1)} %vn_ref.3) | copy-start | bytes 1572868
  1.0 4.3 %collective-permute-start = (bf16[128,256]{1,0:T(8,128)(2,1)S(1)}, bf16[128,256]{1,0:T(8,128)(2,1)S(1)}, u32[]{:S(2)}, u32[]{:S(2)}) collective-permute-start(bf16[128,256]{1,0:T(8,128)(2,1)S(1)} %get-tuple-element.60), channel_id=1, source_target_pairs={{0,1},{1,0},{2,3},{3,2},{4,5},{5,4},{6,7},{7,6},{8,9},{9,8},{10,11... | collective-permute-start | bytes 196616 | tf_op jit(solution)/shard_map/ppermute | solution.py:361
  5.4 32.9 %collective-permute-start.8 = (bf16[256,2048]{1,0:T(8,128)(2,1)}, bf16[256,2048]{1,0:T(8,128)(2,1)}, u32[]{:S(2)}, u32[]{:S(2)}) collective-permute-start(bf16[256,2048]{1,0:T(8,128)(2,1)} %constant_dynamic-slice_fusion.own_ref), channel_id=1, source_target_pairs={{0,1},{1,0},{2,3},{3,2},{4,5},{5,4},{6,7},{7,6},{8,9},{9,8},{10,11... | collective-permute-start | bytes 3145736 | tf_op jit(solution)/shard_map/ppermute | solution.py:361
  7.5 4.2 %collective-permute-start.1 = (bf16[128,512]{1,0:T(8,128)(2,1)S(1)}, bf16[128,512]{1,0:T(8,128)(2,1)S(1)}, u32[]{:S(2)}, u32[]{:S(2)}) collective-permute-start(bf16[128,512]{1,0:T(8,128)(2,1)S(1)} %pad_maximum_fusion.qa_ref), channel_id=1, source_target_pairs={{0,32},{32,0},{64,96},{96,64},{1,33},{33,1},{65,97},{97,65},{2,34}... | collective-permute-start | bytes 393224 | tf_op jit(solution)/shard_map/ppermute | solution.py:361
  8.2 10.7 %collective-permute-start.2 = (bf16[128,512]{1,0:T(8,128)(2,1)S(1)}, bf16[128,512]{1,0:T(8,128)(2,1)S(1)}, u32[]{:S(2)}, u32[]{:S(2)}) collective-permute-start(bf16[128,512]{1,0:T(8,128)(2,1)S(1)} %pad_maximum_fusion.qa_ref), channel_id=1, source_target_pairs={{0,64},{32,96},{64,0},{96,32},{1,65},{33,97},{65,1},{97,33},{2,66}... | collective-permute-start | bytes 393224 | tf_op jit(solution)/shard_map/ppermute | solution.py:361
  11.4 7.5 %collective-permute-start.3 = (bf16[128,512]{1,0:T(8,128)(2,1)S(1)}, bf16[128,512]{1,0:T(8,128)(2,1)S(1)}, u32[]{:S(2)}, u32[]{:S(2)}) collective-permute-start(bf16[128,512]{1,0:T(8,128)(2,1)S(1)} %pad_maximum_fusion.qa_ref), channel_id=1, source_target_pairs={{0,96},{32,64},{64,32},{96,0},{1,97},{33,65},{65,33},{97,1},{2,98}... | collective-permute-start | bytes 393224 | tf_op jit(solution)/shard_map/ppermute | solution.py:361
  11.7 2.2 %copy-start.1 = (bf16[2,2048,512]{2,1,0:T(8,128)(2,1)S(1)}, bf16[2,2048,512]{2,1,0:T(8,128)(2,1)}, u32[]{:S(2)}) copy-start(bf16[2,2048,512]{2,1,0:T(8,128)(2,1)} %vc_ref.3) | copy-start | bytes 12582916
  13.9 5.0 %copy-start.2 = (bf16[2,2048,512]{2,1,0:T(8,128)(2,1)S(1)}, bf16[2,2048,512]{2,1,0:T(8,128)(2,1)}, u32[]{:S(2)}) copy-start(bf16[2,2048,512]{2,1,0:T(8,128)(2,1)} %vc_ref.3) | copy-start | bytes 12582916
  18.9 85.2 %slice-start = ((s8[6291456]{0:T(1024)(128)(4,1)}), s8[2097152]{0:T(1024)(128)(4,1)S(1)}, s32[]{:S(2)}) async-start(s8[6291456]{0:T(1024)(128)(4,1)} %bitcast.25), calls=%async_computation.3 | async-start | bytes 4194304
  23.9 12.3 %collective-permute-start.5 = (bf16[144,512]{1,0:T(8,128)(2,1)S(1)}, bf16[144,512]{1,0:T(8,128)(2,1)S(1)}, u32[]{:S(2)}, u32[]{:S(2)}) collective-permute-start(bf16[144,512]{1,0:T(8,128)(2,1)S(1)} %get-tuple-element.40), channel_id=1, source_target_pairs={{0,64},{32,96},{64,0},{96,32},{1,65},{33,97},{65,1},{97,33},{2,66}... | collective-permute-start | bytes 442376 | tf_op jit(solution)/shard_map/ppermute | solution.py:361
  27.1 9.1 %collective-permute-start.6 = (bf16[144,512]{1,0:T(8,128)(2,1)S(1)}, bf16[144,512]{1,0:T(8,128)(2,1)S(1)}, u32[]{:S(2)}, u32[]{:S(2)}) collective-permute-start(bf16[144,512]{1,0:T(8,128)(2,1)S(1)} %get-tuple-element.41), channel_id=1, source_target_pairs={{0,96},{32,64},{64,32},{96,0},{1,97},{33,65},{65,33},{97,1},{2,98}... | collective-permute-start | bytes 442376 | tf_op jit(solution)/shard_map/ppermute | solution.py:361
  27.1 8.1 %copy-start.8 = (s32[8,8]{1,0:T(8,128)S(1)}, s32[8,8]{1,0:T(8,128)}, u32[]{:S(2)}) copy-start(s32[8,8]{1,0:T(8,128)} %routes_ref) | copy-start | bytes 772
  27.1 8.1 %copy-start.10 = (f32[8,8]{1,0:T(8,128)S(1)}, f32[8,8]{1,0:T(8,128)}, u32[]{:S(2)}) copy-start(f32[8,8]{1,0:T(8,128)} %gates_ref) | copy-start | bytes 772
  27.1 76.9 %slice-start.1 = ((s8[6291456]{0:T(1024)(128)(4,1)}), s8[4194304]{0:T(1024)(128)(4,1)S(1)}, s32[]{:S(2)}) async-start(s8[6291456]{0:T(1024)(128)(4,1)} %bitcast.25), calls=%async_computation.4 | async-start | bytes 8388608
  27.1 9.0 %collective-permute-start.4 = (bf16[144,512]{1,0:T(8,128)(2,1)S(1)}, bf16[144,512]{1,0:T(8,128)(2,1)S(1)}, u32[]{:S(2)}, u32[]{:S(2)}) collective-permute-start(bf16[144,512]{1,0:T(8,128)(2,1)S(1)} %get-tuple-element.35), channel_id=1, source_target_pairs={{0,32},{32,0},{64,96},{96,64},{1,33},{33,1},{65,97},{97,65},{2,34}... | collective-permute-start | bytes 442376 | tf_op jit(solution)/shard_map/ppermute | solution.py:361
  36.8 1.4 collective-permute-start.7
  38.3 29.5 %copy-start.6 = (bf16[8,4096]{1,0:T(8,128)(2,1)S(1)}, bf16[8,4096]{1,0:T(8,128)(2,1)}, u32[]{:S(2)}) copy-start(bf16[8,4096]{1,0:T(8,128)(2,1)} %residual_ref.1) | copy-start | bytes 196612
  38.3 29.5 %copy-start.7 = (f32[4096]{0:T(1024)S(1)}, f32[4096]{0:T(1024)}, u32[]{:S(2)}) copy-start(f32[4096]{0:T(1024)} %param.21) | copy-start | bytes 49156
  68.4 35.6 %copy-start.4 = (bf16[256,256]{1,0:T(8,128)(2,1)S(1)}, bf16[256,256]{1,0:T(8,128)(2,1)}, u32[]{:S(2)}) copy-start(bf16[256,256]{1,0:T(8,128)(2,1)} %constant.39.clone.perm_ref) | copy-start | bytes 393220
  68.4 35.6 %copy-start.5 = (bf16[256,256]{1,0:T(8,128)(2,1)S(1)}, bf16[256,256]{1,0:T(8,128)(2,1)}, u32[]{:S(2)}) copy-start(bf16[256,256]{1,0:T(8,128)(2,1)} %constant.40.clone.back_ref) | copy-start | bytes 393220
  104.1 4.9 %collective-permute-start.9 = (bf16[64,16,1024]{2,1,0:T(8,128)(2,1)S(1)}, bf16[64,16,1024]{2,1,0:T(8,128)(2,1)S(1)}, u32[]{:S(2)}, u32[]{:S(2)}) collective-permute-start(bf16[64,16,1024]{2,1,0:T(8,128)(2,1)S(1)} %all_to_all.16.rows_ref), channel_id=1, source_target_pairs={{0,32},{32,0},{1,33},{33,1},{2,34},{34,2},{3,35},{35,3},{4,36},{36... | collective-permute-start | bytes 6291464 | tf_op jit(solution)/shard_map/ppermute | solution.py:361
  113.7 4.4 %collective-permute-start.10 = (bf16[64,16,1024]{2,1,0:T(8,128)(2,1)S(1)}, bf16[64,16,1024]{2,1,0:T(8,128)(2,1)S(1)}, u32[]{:S(2)}, u32[]{:S(2)}) collective-permute-start(bf16[64,16,1024]{2,1,0:T(8,128)(2,1)S(1)} %experts.3), channel_id=1, source_target_pairs={{0,32},{32,0},{1,33},{33,1},{2,34},{34,2},{3,35},{35,3},{4,36},{36... | collective-permute-start | bytes 6291464 | tf_op jit(solution)/shard_map/ppermute | solution.py:361

commit v6 on v5

--- a/solution.py
+++ b/solution.py
@@ -408,15 +408,17 @@
         (mine, query_parts[2], query_parts[3])
     )
     across, diagonal = attend_pair(2)
-    across, diagonal, w_in, routes, gate_weights = lax.optimization_barrier(
-        (across, diagonal, w_in, routes, gate_weights)
+    across, diagonal, w_in = lax.optimization_barrier((across, diagonal, w_in))
+    turned = w_in.transpose(0, 2, 1, 3)
+    parts = [mine, swap(beside, SEQ, 1), swap(across, SEQ, 2), swap(diagonal, SEQ, 3)]
+    parts, turned = lax.optimization_barrier((parts, turned))
+    merged, routes, gate_weights = lax.optimization_barrier(
+        (merge(parts), routes, gate_weights)
     )
-    turned = w_in.transpose(0, 2, 1, 3)
+    beside_merged = swap(merged, ("core",), 1)
     pick, share = tables(routes, gate_weights, 512)
-    parts = [mine, swap(beside, SEQ, 1), swap(across, SEQ, 2), swap(diagonal, SEQ, 3)]
-    parts, turned, pick, share = lax.optimization_barrier((parts, turned, pick, share))
-    merged = merge(parts)
-    partial = project(core, merged, swap(merged, ("core",), 1), columns, near)
+    beside_merged, pick, share = lax.optimization_barrier((beside_merged, pick, share))
+    partial = project(core, merged, beside_merged, columns, near)
     arrived = lax.all_to_all(
         partial.reshape(32, tok, width // 2),
         ("core", "x", "yl", "zh"),

time: 158 us -> 157 us (level)
  no operation moved by 1% of the time
where the time goes in v6:
time: 157 us; the launch traced here: 156 us
  blocking collectives  99.7 us (64%)
  Pallas kernels  25.3 us (16%)
  starting transfers between devices  12.3 us (8%)
  local copies, waits for them, and re-layouts  11.9 us (8%)
  waiting for transfers between devices  5.11 us (3%)
    all_to_all x1, blocking collectives, local(): lax.all_to_all(summed, spread, split_axis=0, concat_axis=0, tiled=True)  36.9 us
    all_to_all x1, blocking collectives, local(): lax.all_to_all(outgoing, spread, split_axis=0, concat_axis=0, tiled=True)  35.6 us
    all_to_all x1, blocking collectives, local(): lax.all_to_all(partial.reshape(32, tok, width // 2), ('core', 'x', 'yl',...  27.2 us
    ppermute x11, starting transfers between devices, swap(): return lax.ppermute(v, axes, [(i, i ^ bit) for i in range(count)])  12.3 us
    pallas_call x2, Pallas kernels, attend(): pl.pallas_call(functools.partial(attn_kernel, first), grid_spec=pltpu.Pre...  9.89 us
    pallas_call x2, Pallas kernels, experts(): pl.pallas_call(expert_kernel, in_specs=[pl.BlockSpec(memory_space=pltpu.V...  9.74 us
    optimization_barrier x1, local copies, waits for them, and re-layouts, local(): across, diagonal, w_in = lax.optimization_barrier((across, diagonal, w_in))  7.58 us
    ppermute x11, waiting for transfers between devices, swap(): return lax.ppermute(v, axes, [(i, i ^ bit) for i in range(count)])  5.11 us
  transfers between devices with their start and end apart: 11, of which 3 were waited for; matrix products, arithmetic and copies ran while one was open for 6% of the time, Pallas kernels for 10%

profile of v6, /device:TPU:0, one launch (start us, length us, event | category | flops | bytes accessed | tf_op | source)
XLA Modules:
  0.0 156.2 jit_solution(16472940168766950934)
XLA Ops:
  0.0 0.0 copy-start
  0.0 0.0 copy-start.9
  0.0 0.0 copy-start.3
  0.0 1.0 dynamic-slice_bitcast_fusion.1
  1.0 2.1 %collective-permute-start = (bf16[128,256]{1,0:T(8,128)(2,1)S(1)}, bf16[128,256]{1,0:T(8,128)(2,1)S(1)}, u32[]{:S(2)}, u32[]{:S(2)}) collective-permute-start(bf16[128,256]{1,0:T(8,128)(2,1)S(1)} %get-tuple-element.64), channel_id=1, source_target_pairs={{0,1},{1,0},{2,3},{3,2},{4,5},{5,4},{6,7},{7,6},{8,9},{9,8},{10,11... | collective-permute-start | bytes 196616 | tf_op jit(solution)/shard_map/ppermute | solution.py:361
  3.1 0.0 copy-done
  3.1 1.1 constant_dynamic-slice_fusion.own_ref
  4.2 1.1 collective-permute-done
  5.4 2.1 %collective-permute-start.8 = (bf16[256,2048]{1,0:T(8,128)(2,1)}, bf16[256,2048]{1,0:T(8,128)(2,1)}, u32[]{:S(2)}, u32[]{:S(2)}) collective-permute-start(bf16[256,2048]{1,0:T(8,128)(2,1)} %constant_dynamic-slice_fusion.own_ref), channel_id=1, source_target_pairs={{0,1},{1,0},{2,3},{3,2},{4,5},{5,4},{6,7},{7,6},{8,9},{9,8},{10,11... | collective-permute-start | bytes 3145736 | tf_op jit(solution)/shard_map/ppermute | solution.py:361
  7.5 0.0 collective-permute-start.1
  8.2 3.3 %collective-permute-start.2 = (bf16[128,512]{1,0:T(8,128)(2,1)S(1)}, bf16[128,512]{1,0:T(8,128)(2,1)S(1)}, u32[]{:S(2)}, u32[]{:S(2)}) collective-permute-start(bf16[128,512]{1,0:T(8,128)(2,1)S(1)} %pad_maximum_fusion.qa_ref), channel_id=1, source_target_pairs={{0,64},{32,96},{64,0},{96,32},{1,65},{33,97},{65,1},{97,33},{2,66}... | collective-permute-start | bytes 393224 | tf_op jit(solution)/shard_map/ppermute | solution.py:361
  11.4 0.2 collective-permute-start.3
  11.6 0.1 pad_add_fusion.info
  11.7 0.0 collective-permute-done.1.qb_ref
  11.7 0.0 copy-done.9
  11.7 0.0 copy-done.3
  11.7 0.0 copy-start.1
  11.7 2.2 %copy-done.1 = bf16[2,2048,512]{2,1,0:T(8,128)(2,1)S(1)} copy-done((bf16[2,2048,512]{2,1,0:T(8,128)(2,1)S(1)}, bf16[2,2048,512]{2,1,0:T(8,128)(2,1)}, u32[]{:S(2)}) %copy-start.1) | copy-done | bytes 4194328
  13.9 0.0 copy-start.2
  13.9 4.9 %attend.2 = (bf16[144,512]{1,0:T(8,128)(2,1)S(1)}, bf16[144,512]{1,0:T(8,128)(2,1)S(1)}) custom-call(s32[4]{0:T(128)S(1)} %pad_add_fusion.info, s32[2,3]{1,0:T(2,128)S(1)} %bitcast.30, bf16[128,512]{1,0:T(8,128)(2,1)S(1)} %pad_maximum_fusion.qa_ref, bf16[128,512]{1,0:T(8,128)(2,1)S(1)} %collective-permute-done.1.qb_ref, bf16[2,2048,512]{2,1,0:T(8,128)(2,1)S(1)} %copy-done.1, ...), custom_call_target="tpu_custom_call" | custom-call | flops 1207959552 | bytes 1179648 | tf_op jit(solution)/shard_map/attend/pallas_call | solution.py:92
  18.9 0.0 collective-permute-done.2.qa_ref
  18.9 0.0 collective-permute-done.3.qb_ref
  18.9 0.0 copy-done.2
  18.9 0.0 slice-start
  18.9 4.9 %attend.3 = (bf16[144,512]{1,0:T(8,128)(2,1)S(1)}, bf16[144,512]{1,0:T(8,128)(2,1)S(1)}) custom-call(s32[4]{0:T(128)S(1)} %pad_add_fusion.info, s32[2,3]{1,0:T(2,128)S(1)} %bitcast.31, bf16[128,512]{1,0:T(8,128)(2,1)S(1)} %collective-permute-done.2.qa_ref, bf16[128,512]{1,0:T(8,128)(2,1)S(1)} %collective-permute-done.3.qb_ref, ...), custom_call_target="tpu_custom_call" | custom-call | flops 1207959552 | bytes 1179648 | tf_op jit(solution)/shard_map/attend/pallas_call | solution.py:92
  23.9 3.3 %collective-permute-start.5 = (bf16[144,512]{1,0:T(8,128)(2,1)S(1)}, bf16[144,512]{1,0:T(8,128)(2,1)S(1)}, u32[]{:S(2)}, u32[]{:S(2)}) collective-permute-start(bf16[144,512]{1,0:T(8,128)(2,1)S(1)} %get-tuple-element.42), channel_id=1, source_target_pairs={{0,64},{32,96},{64,0},{96,32},{1,65},{33,97},{65,1},{97,33},{2,66}... | collective-permute-start | bytes 442376 | tf_op jit(solution)/shard_map/ppermute | solution.py:361
  27.1 0.0 collective-permute-start.6
  27.1 0.0 copy-start.8
  27.1 0.0 copy-start.10
  27.1 0.0 slice-start.1
  27.1 0.5 collective-permute-start.4
  27.6 7.6 %copy.21 = bf16[2,4096,2,384]{3,1,2,0:T(8,128)(2,1)S(1)} copy(bf16[2,4096,2,384]{3,2,1,0:T(2,128)(2,1)} %param.24) | data formatting | bytes 25165824 | tf_op jit(solution)/shard_map/optimization_barrier | solution.py:411
  35.2 0.0 collective-permute-done.5.c_ref
  35.2 0.0 collective-permute-done.6.d_ref
  35.2 0.0 collective-permute-done.4.b_ref
  35.2 0.6 merge.1.mine_ref
  35.9 0.3 collective-permute-start.7
  36.2 0.0 copy-done.8
  36.2 0.0 copy-done.10
  36.2 0.9 tables.1
  37.1 0.1 collective-permute-done.7.other_ref
  37.3 0.0 collective-permute-done.8.near_ref
  37.3 0.0 copy-start.6
  37.3 2.3 %project.1 = bf16[256,2048]{1,0:T(8,128)(2,1)S(1)} custom-call(s32[1]{0:T(128)} %bitcast.10.core_ref, bf16[128,512]{1,0:T(8,128)(2,1)S(1)} %merge.1.mine_ref, bf16[128,512]{1,0:T(8,128)(2,1)S(1)} %collective-permute-done.7.other_ref, bf16[256,2048]{1,0:T(8,128)(2,1)} %constant_dynamic-slice_fusion.own_ref, bf16[256,2048]{1,0:T(8,128)(2,1)} %collective-permute-done.8.near_ref), custom_call_target="tpu_custom_call" | custom-call | flops 536870912 | bytes 2097152 | tf_op jit(solution)/shard_map/project/pallas_call | solution.py:170
  39.6 27.2 %all_to_all.15.arrived_ref = bf16[32,8,2048]{2,1,0:T(8,128)(2,1)S(1)} all-to-all(bf16[32,8,2048]{2,1,0:T(8,128)(2,1)S(1)} %bitcast.28), channel_id=1, replica_groups=mesh['yh'=2,'core'=2,'x'=4,'yl'=2,'zh'=2,'zl'=2] {'core','x','yl','zh'}, dimensions={0} | all-to-all | bytes 2097152 | tf_op jit(solution)/shard_map/all_to_all | solution.py:422
  66.8 0.0 copy-done.6
  66.8 0.0 copy-done.7
  66.8 0.7 settle.1
  67.5 0.0 copy-start.4
  67.5 0.0 copy-start.5
  67.5 35.6 %all_to_all.16.rows_ref = bf16[64,16,1024]{2,1,0:T(8,128)(2,1)S(1)} all-to-all(bf16[64,16,1024]{2,1,0:T(8,128)(2,1)S(1)} %get-tuple-element.58), channel_id=1, replica_groups=mesh['yh'=2,'core'=2,'x'=4,'yl'=2,'zh'=2,'zl'=2] {'yh','x','yl','zh','zl'}, dimensions={0} | all-to-all | bytes 4194304 | tf_op jit(solution)/shard_map/all_to_all | solution.py:435
  103.1 0.0 collective-permute-start.9
  103.1 0.0 slice-done
  103.1 0.0 slice-done.1
  103.1 0.0 copy-done.4
  103.1 0.0 copy-done.5
  103.1 4.9 %experts.2 = bf16[64,16,1024]{2,1,0:T(8,128)(2,1)S(1)} custom-call(bf16[64,16,1024]{2,1,0:T(8,128)(2,1)S(1)} %all_to_all.16.rows_ref, bf16[256,256]{1,0:T(8,128)(2,1)S(1)} %copy-done.4, bf16[256,256]{1,0:T(8,128)(2,1)S(1)} %copy-done.5, bf16[2,2,4096,384]{3,2,1,0:T(8,128)(2,1)S(1)} %bitcast.23, bf16[2,384,4096]{2,1,0:T(8,128)(2,1)S(1)} %bitcast.26), custom_call_target="tpu_custom_call" | custom-call | flops 2415919104 | bytes 18874368 | tf_op jit(solution)/shard_map/experts/pallas_call | solution.py:316
  108.0 0.0 collective-permute-done.9.rows_ref
  108.0 4.9 %experts.3 = bf16[64,16,1024]{2,1,0:T(8,128)(2,1)S(1)} custom-call(bf16[64,16,1024]{2,1,0:T(8,128)(2,1)S(1)} %collective-permute-done.9.rows_ref, bf16[256,256]{1,0:T(8,128)(2,1)S(1)} %copy-done.4, bf16[256,256]{1,0:T(8,128)(2,1)S(1)} %copy-done.5, bf16[2,2,4096,384]{3,2,1,0:T(8,128)(2,1)S(1)} %bitcast.24, bf16[2,384,4096]{2,1,0:T(8,128)(2,1)S(1)} %bitcast.26), custom_call_target="tpu_custom_call" | custom-call | flops 2415919104 | bytes 18874368 | tf_op jit(solution)/shard_map/experts/pallas_call | solution.py:316
  112.9 0.6 collective-permute-start.10
  113.5 3.8 %collective-permute-done.10 = bf16[64,16,1024]{2,1,0:T(8,128)(2,1)S(1)} collective-permute-done((bf16[64,16,1024]{2,1,0:T(8,128)(2,1)S(1)}, bf16[64,16,1024]{2,1,0:T(8,128)(2,1)S(1)}, u32[]{:S(2)}, u32[]{:S(2)}) %collective-permute-start.10) | collective-permute-done | bytes 2097184 | tf_op jit(solution)/shard_map/ppermute | solution.py:361
  117.2 1.0 add_convert_fusion
  118.2 36.9 %all_to_all.17 = bf16[64,16,1024]{2,1,0:T(8,128)(2,1)S(1)} all-to-all(bf16[64,16,1024]{2,1,0:T(8,128)(2,1)S(1)} %add_convert_fusion), channel_id=1, replica_groups=mesh['yh'=2,'core'=2,'x'=4,'yl'=2,'zh'=2,'zl'=2] {'yh','x','yl','zh','zl'}, dimensions={0} | all-to-all | bytes 4194304 | tf_op jit(solution)/shard_map/all_to_all | solution.py:442
  155.1 1.1 combine.1
  (3 shorter events, 0.0 us)
Async XLA Ops:
  0.0 3.1 %copy-start = (bf16[256,4096]{1,0:T(8,128)(2,1)S(1)}, bf16[256,4096]{1,0:T(8,128)(2,1)}, u32[]{:S(2)}) copy-start(bf16[256,4096]{1,0:T(8,128)(2,1)} %param.20) | copy-start | bytes 6291460
  0.0 11.7 %copy-start.9 = (s32[3,2]{0,1:T(2,128)S(1)}, s32[3,2]{0,1:T(2,128)}, u32[]{:S(2)}) copy-start(s32[3,2]{0,1:T(2,128)} %param.18) | copy-start | bytes 76
  0.0 11.7 %copy-start.3 = (bf16[2,256,512]{2,1,0:T(8,128)(2,1)S(1)}, bf16[2,256,512]{2,1,0:T(8,128)(2,1)}, u32[]{:S(2)}) copy-start(bf16[2,256,512]{2,1,0:T(8,128)(2,1)} %vn_ref.3) | copy-start | bytes 1572868
  1.0 4.3 %collective-permute-start = (bf16[128,256]{1,0:T(8,128)(2,1)S(1)}, bf16[128,256]{1,0:T(8,128)(2,1)S(1)}, u32[]{:S(2)}, u32[]{:S(2)}) collective-permute-start(bf16[128,256]{1,0:T(8,128)(2,1)S(1)} %get-tuple-element.64), channel_id=1, source_target_pairs={{0,1},{1,0},{2,3},{3,2},{4,5},{5,4},{6,7},{7,6},{8,9},{9,8},{10,11... | collective-permute-start | bytes 196616 | tf_op jit(solution)/shard_map/ppermute | solution.py:361
  5.4 31.9 %collective-permute-start.8 = (bf16[256,2048]{1,0:T(8,128)(2,1)}, bf16[256,2048]{1,0:T(8,128)(2,1)}, u32[]{:S(2)}, u32[]{:S(2)}) collective-permute-start(bf16[256,2048]{1,0:T(8,128)(2,1)} %constant_dynamic-slice_fusion.own_ref), channel_id=1, source_target_pairs={{0,1},{1,0},{2,3},{3,2},{4,5},{5,4},{6,7},{7,6},{8,9},{9,8},{10,11... | collective-permute-start | bytes 3145736 | tf_op jit(solution)/shard_map/ppermute | solution.py:361
  7.5 4.2 %collective-permute-start.1 = (bf16[128,512]{1,0:T(8,128)(2,1)S(1)}, bf16[128,512]{1,0:T(8,128)(2,1)S(1)}, u32[]{:S(2)}, u32[]{:S(2)}) collective-permute-start(bf16[128,512]{1,0:T(8,128)(2,1)S(1)} %pad_maximum_fusion.qa_ref), channel_id=1, source_target_pairs={{0,32},{32,0},{64,96},{96,64},{1,33},{33,1},{65,97},{97,65},{2,34}... | collective-permute-start | bytes 393224 | tf_op jit(solution)/shard_map/ppermute | solution.py:361
  8.2 10.7 %collective-permute-start.2 = (bf16[128,512]{1,0:T(8,128)(2,1)S(1)}, bf16[128,512]{1,0:T(8,128)(2,1)S(1)}, u32[]{:S(2)}, u32[]{:S(2)}) collective-permute-start(bf16[128,512]{1,0:T(8,128)(2,1)S(1)} %pad_maximum_fusion.qa_ref), channel_id=1, source_target_pairs={{0,64},{32,96},{64,0},{96,32},{1,65},{33,97},{65,1},{97,33},{2,66}... | collective-permute-start | bytes 393224 | tf_op jit(solution)/shard_map/ppermute | solution.py:361
  11.4 7.5 %collective-permute-start.3 = (bf16[128,512]{1,0:T(8,128)(2,1)S(1)}, bf16[128,512]{1,0:T(8,128)(2,1)S(1)}, u32[]{:S(2)}, u32[]{:S(2)}) collective-permute-start(bf16[128,512]{1,0:T(8,128)(2,1)S(1)} %pad_maximum_fusion.qa_ref), channel_id=1, source_target_pairs={{0,96},{32,64},{64,32},{96,0},{1,97},{33,65},{65,33},{97,1},{2,98}... | collective-permute-start | bytes 393224 | tf_op jit(solution)/shard_map/ppermute | solution.py:361
  11.7 2.2 %copy-start.1 = (bf16[2,2048,512]{2,1,0:T(8,128)(2,1)S(1)}, bf16[2,2048,512]{2,1,0:T(8,128)(2,1)}, u32[]{:S(2)}) copy-start(bf16[2,2048,512]{2,1,0:T(8,128)(2,1)} %vc_ref.3) | copy-start | bytes 12582916
  13.9 5.0 %copy-start.2 = (bf16[2,2048,512]{2,1,0:T(8,128)(2,1)S(1)}, bf16[2,2048,512]{2,1,0:T(8,128)(2,1)}, u32[]{:S(2)}) copy-start(bf16[2,2048,512]{2,1,0:T(8,128)(2,1)} %vc_ref.3) | copy-start | bytes 12582916
  18.9 84.2 %slice-start = ((s8[6291456]{0:T(1024)(128)(4,1)}), s8[2097152]{0:T(1024)(128)(4,1)S(1)}, s32[]{:S(2)}) async-start(s8[6291456]{0:T(1024)(128)(4,1)} %bitcast.25), calls=%async_computation.3 | async-start | bytes 4194304
  23.9 11.3 %collective-permute-start.5 = (bf16[144,512]{1,0:T(8,128)(2,1)S(1)}, bf16[144,512]{1,0:T(8,128)(2,1)S(1)}, u32[]{:S(2)}, u32[]{:S(2)}) collective-permute-start(bf16[144,512]{1,0:T(8,128)(2,1)S(1)} %get-tuple-element.42), channel_id=1, source_target_pairs={{0,64},{32,96},{64,0},{96,32},{1,65},{33,97},{65,1},{97,33},{2,66}... | collective-permute-start | bytes 442376 | tf_op jit(solution)/shard_map/ppermute | solution.py:361
  27.1 8.1 %collective-permute-start.6 = (bf16[144,512]{1,0:T(8,128)(2,1)S(1)}, bf16[144,512]{1,0:T(8,128)(2,1)S(1)}, u32[]{:S(2)}, u32[]{:S(2)}) collective-permute-start(bf16[144,512]{1,0:T(8,128)(2,1)S(1)} %get-tuple-element.43), channel_id=1, source_target_pairs={{0,96},{32,64},{64,32},{96,0},{1,97},{33,65},{65,33},{97,1},{2,98}... | collective-permute-start | bytes 442376 | tf_op jit(solution)/shard_map/ppermute | solution.py:361
  27.1 9.1 %copy-start.8 = (s32[8,8]{1,0:T(8,128)S(1)}, s32[8,8]{1,0:T(8,128)}, u32[]{:S(2)}) copy-start(s32[8,8]{1,0:T(8,128)} %routes_ref) | copy-start | bytes 772
  27.1 9.1 %copy-start.10 = (f32[8,8]{1,0:T(8,128)S(1)}, f32[8,8]{1,0:T(8,128)}, u32[]{:S(2)}) copy-start(f32[8,8]{1,0:T(8,128)} %gates_ref) | copy-start | bytes 772
  27.1 76.0 %slice-start.1 = ((s8[6291456]{0:T(1024)(128)(4,1)}), s8[4194304]{0:T(1024)(128)(4,1)S(1)}, s32[]{:S(2)}) async-start(s8[6291456]{0:T(1024)(128)(4,1)} %bitcast.25), calls=%async_computation.4 | async-start | bytes 8388608
  27.1 8.1 %collective-permute-start.4 = (bf16[144,512]{1,0:T(8,128)(2,1)S(1)}, bf16[144,512]{1,0:T(8,128)(2,1)S(1)}, u32[]{:S(2)}, u32[]{:S(2)}) collective-permute-start(bf16[144,512]{1,0:T(8,128)(2,1)S(1)} %get-tuple-element.37), channel_id=1, source_target_pairs={{0,32},{32,0},{64,96},{96,64},{1,33},{33,1},{65,97},{97,65},{2,34}... | collective-permute-start | bytes 442376 | tf_op jit(solution)/shard_map/ppermute | solution.py:361
  35.9 1.4 collective-permute-start.7
  37.3 29.5 %copy-start.6 = (bf16[8,4096]{1,0:T(8,128)(2,1)S(1)}, bf16[8,4096]{1,0:T(8,128)(2,1)}, u32[]{:S(2)}) copy-start(bf16[8,4096]{1,0:T(8,128)(2,1)} %residual_ref.1) | copy-start | bytes 196612
  37.3 29.5 %copy-start.7 = (f32[4096]{0:T(1024)S(1)}, f32[4096]{0:T(1024)}, u32[]{:S(2)}) copy-start(f32[4096]{0:T(1024)} %param.21) | copy-start | bytes 49156
  67.5 35.6 %copy-start.4 = (bf16[256,256]{1,0:T(8,128)(2,1)S(1)}, bf16[256,256]{1,0:T(8,128)(2,1)}, u32[]{:S(2)}) copy-start(bf16[256,256]{1,0:T(8,128)(2,1)} %constant.39.clone.perm_ref) | copy-start | bytes 393220
  67.5 35.6 %copy-start.5 = (bf16[256,256]{1,0:T(8,128)(2,1)S(1)}, bf16[256,256]{1,0:T(8,128)(2,1)}, u32[]{:S(2)}) copy-start(bf16[256,256]{1,0:T(8,128)(2,1)} %constant.40.clone.back_ref) | copy-start | bytes 393220
  103.1 4.9 %collective-permute-start.9 = (bf16[64,16,1024]{2,1,0:T(8,128)(2,1)S(1)}, bf16[64,16,1024]{2,1,0:T(8,128)(2,1)S(1)}, u32[]{:S(2)}, u32[]{:S(2)}) collective-permute-start(bf16[64,16,1024]{2,1,0:T(8,128)(2,1)S(1)} %all_to_all.16.rows_ref), channel_id=1, source_target_pairs={{0,32},{32,0},{1,33},{33,1},{2,34},{34,2},{3,35},{35,3},{4,36},{36... | collective-permute-start | bytes 6291464 | tf_op jit(solution)/shard_map/ppermute | solution.py:361
  112.9 4.4 %collective-permute-start.10 = (bf16[64,16,1024]{2,1,0:T(8,128)(2,1)S(1)}, bf16[64,16,1024]{2,1,0:T(8,128)(2,1)S(1)}, u32[]{:S(2)}, u32[]{:S(2)}) collective-permute-start(bf16[64,16,1024]{2,1,0:T(8,128)(2,1)S(1)} %experts.3), channel_id=1, source_target_pairs={{0,32},{32,0},{1,33},{33,1},{2,34},{34,2},{3,35},{35,3},{4,36},{36... | collective-permute-start | bytes 6291464 | tf_op jit(solution)/shard_map/ppermute | solution.py:361

commit v7 on v6

--- a/solution.py
+++ b/solution.py
@@ -156,12 +156,13 @@
     rows = mine_ref.shape[0]
     half = own_ref.shape[0]
     core = core_ref[0]
-    for att, side in ((mine_ref, core), (other_ref, 1 - core)):
-        at = pl.multiple_of(side * rows, rows)
-        out_ref[pl.ds(at, rows), :] = (
-            jnp.dot(att[:, :half], own_ref[...], preferred_element_type=F32)
-            + jnp.dot(att[:, half:], near_ref[...], preferred_element_type=F32)
-        ).astype(BF)
+    att = jnp.concatenate([mine_ref[...], other_ref[...]], axis=0)
+    both = (
+        jnp.dot(att[:, :half], own_ref[...], preferred_element_type=F32)
+        + jnp.dot(att[:, half:], near_ref[...], preferred_element_type=F32)
+    ).astype(BF)
+    for part, side in ((both[:rows], core), (both[rows:], 1 - core)):
+        out_ref[pl.ds(pl.multiple_of(side * rows, rows), rows), :] = part
 
 
 def project(core, mine, other, own, near):

time: 157 us -> 157 us (level)
  no operation moved by 1% of the time
where the time goes in v7:
time: 157 us; the launch traced here: 156 us
  blocking collectives  99.7 us (64%)
  Pallas kernels  25.3 us (16%)
  starting transfers between devices  12.3 us (8%)
  local copies, waits for them, and re-layouts  11.9 us (8%)
  waiting for transfers between devices  5.11 us (3%)
    all_to_all x1, blocking collectives, local(): lax.all_to_all(summed, spread, split_axis=0, concat_axis=0, tiled=True)  36.9 us
    all_to_all x1, blocking collectives, local(): lax.all_to_all(outgoing, spread, split_axis=0, concat_axis=0, tiled=True)  35.6 us
    all_to_all x1, blocking collectives, local(): lax.all_to_all(partial.reshape(32, tok, width // 2), ('core', 'x', 'yl',...  27.2 us
    ppermute x11, starting transfers between devices, swap(): return lax.ppermute(v, axes, [(i, i ^ bit) for i in range(count)])  12.3 us
    pallas_call x2, Pallas kernels, attend(): pl.pallas_call(functools.partial(attn_kernel, first), grid_spec=pltpu.Pre...  9.89 us
    pallas_call x2, Pallas kernels, experts(): pl.pallas_call(expert_kernel, in_specs=[pl.BlockSpec(memory_space=pltpu.V...  9.75 us
    optimization_barrier x1, local copies, waits for them, and re-layouts, local(): across, diagonal, w_in = lax.optimization_barrier((across, diagonal, w_in))  7.58 us
    ppermute x11, waiting for transfers between devices, swap(): return lax.ppermute(v, axes, [(i, i ^ bit) for i in range(count)])  5.11 us
  transfers between devices with their start and end apart: 11, of which 3 were waited for; matrix products, arithmetic and copies ran while one was open for 6% of the time, Pallas kernels for 10%

profile of v7, /device:TPU:0, one launch (start us, length us, event | category | flops | bytes accessed | tf_op | source)
XLA Modules:
  0.0 156.2 jit_solution(5972581189290552445)
XLA Ops:
  0.0 0.0 copy-start
  0.0 0.0 copy-start.9
  0.0 0.0 copy-start.3
  0.0 1.0 dynamic-slice_bitcast_fusion.1
  1.0 2.1 %collective-permute-start = (bf16[128,256]{1,0:T(8,128)(2,1)S(1)}, bf16[128,256]{1,0:T(8,128)(2,1)S(1)}, u32[]{:S(2)}, u32[]{:S(2)}) collective-permute-start(bf16[128,256]{1,0:T(8,128)(2,1)S(1)} %get-tuple-element.64), channel_id=1, source_target_pairs={{0,1},{1,0},{2,3},{3,2},{4,5},{5,4},{6,7},{7,6},{8,9},{9,8},{10,11... | collective-permute-start | bytes 196616 | tf_op jit(solution)/shard_map/ppermute | solution.py:362
  3.1 0.0 copy-done
  3.1 1.1 constant_dynamic-slice_fusion.own_ref
  4.2 1.1 collective-permute-done
  5.4 2.1 %collective-permute-start.8 = (bf16[256,2048]{1,0:T(8,128)(2,1)}, bf16[256,2048]{1,0:T(8,128)(2,1)}, u32[]{:S(2)}, u32[]{:S(2)}) collective-permute-start(bf16[256,2048]{1,0:T(8,128)(2,1)} %constant_dynamic-slice_fusion.own_ref), channel_id=1, source_target_pairs={{0,1},{1,0},{2,3},{3,2},{4,5},{5,4},{6,7},{7,6},{8,9},{9,8},{10,11... | collective-permute-start | bytes 3145736 | tf_op jit(solution)/shard_map/ppermute | solution.py:362
  7.5 0.0 collective-permute-start.1
  8.2 3.3 %collective-permute-start.2 = (bf16[128,512]{1,0:T(8,128)(2,1)S(1)}, bf16[128,512]{1,0:T(8,128)(2,1)S(1)}, u32[]{:S(2)}, u32[]{:S(2)}) collective-permute-start(bf16[128,512]{1,0:T(8,128)(2,1)S(1)} %pad_maximum_fusion.qa_ref), channel_id=1, source_target_pairs={{0,64},{32,96},{64,0},{96,32},{1,65},{33,97},{65,1},{97,33},{2,66}... | collective-permute-start | bytes 393224 | tf_op jit(solution)/shard_map/ppermute | solution.py:362
  11.4 0.2 collective-permute-start.3
  11.6 0.1 pad_add_fusion.info
  11.7 0.0 collective-permute-done.1.qb_ref
  11.7 0.0 copy-done.9
  11.7 0.0 copy-done.3
  11.7 0.0 copy-start.1
  11.7 2.2 %copy-done.1 = bf16[2,2048,512]{2,1,0:T(8,128)(2,1)S(1)} copy-done((bf16[2,2048,512]{2,1,0:T(8,128)(2,1)S(1)}, bf16[2,2048,512]{2,1,0:T(8,128)(2,1)}, u32[]{:S(2)}) %copy-start.1) | copy-done | bytes 4194328
  13.9 0.0 copy-start.2
  13.9 4.9 %attend.2 = (bf16[144,512]{1,0:T(8,128)(2,1)S(1)}, bf16[144,512]{1,0:T(8,128)(2,1)S(1)}) custom-call(s32[4]{0:T(128)S(1)} %pad_add_fusion.info, s32[2,3]{1,0:T(2,128)S(1)} %bitcast.30, bf16[128,512]{1,0:T(8,128)(2,1)S(1)} %pad_maximum_fusion.qa_ref, bf16[128,512]{1,0:T(8,128)(2,1)S(1)} %collective-permute-done.1.qb_ref, bf16[2,2048,512]{2,1,0:T(8,128)(2,1)S(1)} %copy-done.1, ...), custom_call_target="tpu_custom_call" | custom-call | flops 1207959552 | bytes 1179648 | tf_op jit(solution)/shard_map/attend/pallas_call | solution.py:92
  18.9 0.0 collective-permute-done.2.qa_ref
  18.9 0.0 collective-permute-done.3.qb_ref
  18.9 0.0 copy-done.2
  18.9 0.0 slice-start
  18.9 4.9 %attend.3 = (bf16[144,512]{1,0:T(8,128)(2,1)S(1)}, bf16[144,512]{1,0:T(8,128)(2,1)S(1)}) custom-call(s32[4]{0:T(128)S(1)} %pad_add_fusion.info, s32[2,3]{1,0:T(2,128)S(1)} %bitcast.31, bf16[128,512]{1,0:T(8,128)(2,1)S(1)} %collective-permute-done.2.qa_ref, bf16[128,512]{1,0:T(8,128)(2,1)S(1)} %collective-permute-done.3.qb_ref, ...), custom_call_target="tpu_custom_call" | custom-call | flops 1207959552 | bytes 1179648 | tf_op jit(solution)/shard_map/attend/pallas_call | solution.py:92
  23.9 3.3 %collective-permute-start.5 = (bf16[144,512]{1,0:T(8,128)(2,1)S(1)}, bf16[144,512]{1,0:T(8,128)(2,1)S(1)}, u32[]{:S(2)}, u32[]{:S(2)}) collective-permute-start(bf16[144,512]{1,0:T(8,128)(2,1)S(1)} %get-tuple-element.42), channel_id=1, source_target_pairs={{0,64},{32,96},{64,0},{96,32},{1,65},{33,97},{65,1},{97,33},{2,66}... | collective-permute-start | bytes 442376 | tf_op jit(solution)/shard_map/ppermute | solution.py:362
  27.1 0.0 collective-permute-start.6
  27.1 0.0 copy-start.10
  27.1 0.0 slice-start.1
  27.1 0.5 collective-permute-start.4
  27.6 7.6 %copy.21 = bf16[2,4096,2,384]{3,1,2,0:T(8,128)(2,1)S(1)} copy(bf16[2,4096,2,384]{3,2,1,0:T(2,128)(2,1)} %param.24) | data formatting | bytes 25165824 | tf_op jit(solution)/shard_map/optimization_barrier | solution.py:412
  35.2 0.0 collective-permute-done.5.c_ref
  35.2 0.0 collective-permute-done.6.d_ref
  35.2 0.0 collective-permute-done.4.b_ref
  35.2 0.6 merge.1.mine_ref
  35.9 0.3 collective-permute-start.7
  36.2 0.0 copy-done.8
  36.2 0.0 copy-done.10
  36.2 0.9 tables.1
  37.1 0.1 collective-permute-done.7.other_ref
  37.3 0.0 collective-permute-done.8.near_ref
  37.3 0.0 copy-start.6
  37.3 0.0 copy-start.7
  37.3 2.3 %project.1 = bf16[256,2048]{1,0:T(8,128)(2,1)S(1)} custom-call(s32[1]{0:T(128)} %bitcast.10.core_ref, bf16[128,512]{1,0:T(8,128)(2,1)S(1)} %merge.1.mine_ref, bf16[128,512]{1,0:T(8,128)(2,1)S(1)} %collective-permute-done.7.other_ref, bf16[256,2048]{1,0:T(8,128)(2,1)} %constant_dynamic-slice_fusion.own_ref, bf16[256,2048]{1,0:T(8,128)(2,1)} %collective-permute-done.8.near_ref), custom_call_target="tpu_custom_call" | custom-call | flops 536870912 | bytes 2097152 | tf_op jit(solution)/shard_map/project/pallas_call | solution.py:171
  39.6 27.2 %all_to_all.15.arrived_ref = bf16[32,8,2048]{2,1,0:T(8,128)(2,1)S(1)} all-to-all(bf16[32,8,2048]{2,1,0:T(8,128)(2,1)S(1)} %bitcast.28), channel_id=1, replica_groups=mesh['yh'=2,'core'=2,'x'=4,'yl'=2,'zh'=2,'zl'=2] {'core','x','yl','zh'}, dimensions={0} | all-to-all | bytes 2097152 | tf_op jit(solution)/shard_map/all_to_all | solution.py:423
  66.8 0.0 copy-done.6
  66.8 0.0 copy-done.7
  66.8 0.7 settle.1
  67.4 0.0 copy-start.4
  67.5 0.0 copy-start.5
  67.5 35.6 %all_to_all.16.rows_ref = bf16[64,16,1024]{2,1,0:T(8,128)(2,1)S(1)} all-to-all(bf16[64,16,1024]{2,1,0:T(8,128)(2,1)S(1)} %get-tuple-element.58), channel_id=1, replica_groups=mesh['yh'=2,'core'=2,'x'=4,'yl'=2,'zh'=2,'zl'=2] {'yh','x','yl','zh','zl'}, dimensions={0} | all-to-all | bytes 4194304 | tf_op jit(solution)/shard_map/all_to_all | solution.py:436
  103.1 0.0 collective-permute-start.9
  103.1 0.0 slice-done
  103.1 0.0 slice-done.1
  103.1 0.0 copy-done.4
  103.1 0.0 copy-done.5
  103.1 4.9 %experts.2 = bf16[64,16,1024]{2,1,0:T(8,128)(2,1)S(1)} custom-call(bf16[64,16,1024]{2,1,0:T(8,128)(2,1)S(1)} %all_to_all.16.rows_ref, bf16[256,256]{1,0:T(8,128)(2,1)S(1)} %copy-done.4, bf16[256,256]{1,0:T(8,128)(2,1)S(1)} %copy-done.5, bf16[2,2,4096,384]{3,2,1,0:T(8,128)(2,1)S(1)} %bitcast.23, bf16[2,384,4096]{2,1,0:T(8,128)(2,1)S(1)} %bitcast.26), custom_call_target="tpu_custom_call" | custom-call | flops 2415919104 | bytes 18874368 | tf_op jit(solution)/shard_map/experts/pallas_call | solution.py:317
  108.0 0.0 collective-permute-done.9.rows_ref
  108.0 4.9 %experts.3 = bf16[64,16,1024]{2,1,0:T(8,128)(2,1)S(1)} custom-call(bf16[64,16,1024]{2,1,0:T(8,128)(2,1)S(1)} %collective-permute-done.9.rows_ref, bf16[256,256]{1,0:T(8,128)(2,1)S(1)} %copy-done.4, bf16[256,256]{1,0:T(8,128)(2,1)S(1)} %copy-done.5, bf16[2,2,4096,384]{3,2,1,0:T(8,128)(2,1)S(1)} %bitcast.24, bf16[2,384,4096]{2,1,0:T(8,128)(2,1)S(1)} %bitcast.26), custom_call_target="tpu_custom_call" | custom-call | flops 2415919104 | bytes 18874368 | tf_op jit(solution)/shard_map/experts/pallas_call | solution.py:317
  112.9 0.6 collective-permute-start.10
  113.5 3.8 %collective-permute-done.10 = bf16[64,16,1024]{2,1,0:T(8,128)(2,1)S(1)} collective-permute-done((bf16[64,16,1024]{2,1,0:T(8,128)(2,1)S(1)}, bf16[64,16,1024]{2,1,0:T(8,128)(2,1)S(1)}, u32[]{:S(2)}, u32[]{:S(2)}) %collective-permute-start.10) | collective-permute-done | bytes 2097184 | tf_op jit(solution)/shard_map/ppermute | solution.py:362
  117.2 1.0 add_convert_fusion
  118.2 36.9 %all_to_all.17 = bf16[64,16,1024]{2,1,0:T(8,128)(2,1)S(1)} all-to-all(bf16[64,16,1024]{2,1,0:T(8,128)(2,1)S(1)} %add_convert_fusion), channel_id=1, replica_groups=mesh['yh'=2,'core'=2,'x'=4,'yl'=2,'zh'=2,'zl'=2] {'yh','x','yl','zh','zl'}, dimensions={0} | all-to-all | bytes 4194304 | tf_op jit(solution)/shard_map/all_to_all | solution.py:443
  155.1 1.1 combine.1
  (3 shorter events, 0.0 us)
Async XLA Ops:
  0.0 3.1 %copy-start = (bf16[256,4096]{1,0:T(8,128)(2,1)S(1)}, bf16[256,4096]{1,0:T(8,128)(2,1)}, u32[]{:S(2)}) copy-start(bf16[256,4096]{1,0:T(8,128)(2,1)} %param.20) | copy-start | bytes 6291460
  0.0 11.7 %copy-start.9 = (s32[3,2]{0,1:T(2,128)S(1)}, s32[3,2]{0,1:T(2,128)}, u32[]{:S(2)}) copy-start(s32[3,2]{0,1:T(2,128)} %param.18) | copy-start | bytes 76
  0.0 11.7 %copy-start.3 = (bf16[2,256,512]{2,1,0:T(8,128)(2,1)S(1)}, bf16[2,256,512]{2,1,0:T(8,128)(2,1)}, u32[]{:S(2)}) copy-start(bf16[2,256,512]{2,1,0:T(8,128)(2,1)} %vn_ref.3) | copy-start | bytes 1572868
  1.0 4.3 %collective-permute-start = (bf16[128,256]{1,0:T(8,128)(2,1)S(1)}, bf16[128,256]{1,0:T(8,128)(2,1)S(1)}, u32[]{:S(2)}, u32[]{:S(2)}) collective-permute-start(bf16[128,256]{1,0:T(8,128)(2,1)S(1)} %get-tuple-element.64), channel_id=1, source_target_pairs={{0,1},{1,0},{2,3},{3,2},{4,5},{5,4},{6,7},{7,6},{8,9},{9,8},{10,11... | collective-permute-start | bytes 196616 | tf_op jit(solution)/shard_map/ppermute | solution.py:362
  5.4 31.9 %collective-permute-start.8 = (bf16[256,2048]{1,0:T(8,128)(2,1)}, bf16[256,2048]{1,0:T(8,128)(2,1)}, u32[]{:S(2)}, u32[]{:S(2)}) collective-permute-start(bf16[256,2048]{1,0:T(8,128)(2,1)} %constant_dynamic-slice_fusion.own_ref), channel_id=1, source_target_pairs={{0,1},{1,0},{2,3},{3,2},{4,5},{5,4},{6,7},{7,6},{8,9},{9,8},{10,11... | collective-permute-start | bytes 3145736 | tf_op jit(solution)/shard_map/ppermute | solution.py:362
  7.5 4.2 %collective-permute-start.1 = (bf16[128,512]{1,0:T(8,128)(2,1)S(1)}, bf16[128,512]{1,0:T(8,128)(2,1)S(1)}, u32[]{:S(2)}, u32[]{:S(2)}) collective-permute-start(bf16[128,512]{1,0:T(8,128)(2,1)S(1)} %pad_maximum_fusion.qa_ref), channel_id=1, source_target_pairs={{0,32},{32,0},{64,96},{96,64},{1,33},{33,1},{65,97},{97,65},{2,34}... | collective-permute-start | bytes 393224 | tf_op jit(solution)/shard_map/ppermute | solution.py:362
  8.2 10.7 %collective-permute-start.2 = (bf16[128,512]{1,0:T(8,128)(2,1)S(1)}, bf16[128,512]{1,0:T(8,128)(2,1)S(1)}, u32[]{:S(2)}, u32[]{:S(2)}) collective-permute-start(bf16[128,512]{1,0:T(8,128)(2,1)S(1)} %pad_maximum_fusion.qa_ref), channel_id=1, source_target_pairs={{0,64},{32,96},{64,0},{96,32},{1,65},{33,97},{65,1},{97,33},{2,66}... | collective-permute-start | bytes 393224 | tf_op jit(solution)/shard_map/ppermute | solution.py:362
  11.4 7.5 %collective-permute-start.3 = (bf16[128,512]{1,0:T(8,128)(2,1)S(1)}, bf16[128,512]{1,0:T(8,128)(2,1)S(1)}, u32[]{:S(2)}, u32[]{:S(2)}) collective-permute-start(bf16[128,512]{1,0:T(8,128)(2,1)S(1)} %pad_maximum_fusion.qa_ref), channel_id=1, source_target_pairs={{0,96},{32,64},{64,32},{96,0},{1,97},{33,65},{65,33},{97,1},{2,98}... | collective-permute-start | bytes 393224 | tf_op jit(solution)/shard_map/ppermute | solution.py:362
  11.7 2.2 %copy-start.1 = (bf16[2,2048,512]{2,1,0:T(8,128)(2,1)S(1)}, bf16[2,2048,512]{2,1,0:T(8,128)(2,1)}, u32[]{:S(2)}) copy-start(bf16[2,2048,512]{2,1,0:T(8,128)(2,1)} %vc_ref.3) | copy-start | bytes 12582916
  13.9 5.0 %copy-start.2 = (bf16[2,2048,512]{2,1,0:T(8,128)(2,1)S(1)}, bf16[2,2048,512]{2,1,0:T(8,128)(2,1)}, u32[]{:S(2)}) copy-start(bf16[2,2048,512]{2,1,0:T(8,128)(2,1)} %vc_ref.3) | copy-start | bytes 12582916
  18.9 84.2 %slice-start = ((s8[6291456]{0:T(1024)(128)(4,1)}), s8[2097152]{0:T(1024)(128)(4,1)S(1)}, s32[]{:S(2)}) async-start(s8[6291456]{0:T(1024)(128)(4,1)} %bitcast.25), calls=%async_computation.3 | async-start | bytes 4194304
  23.9 11.3 %collective-permute-start.5 = (bf16[144,512]{1,0:T(8,128)(2,1)S(1)}, bf16[144,512]{1,0:T(8,128)(2,1)S(1)}, u32[]{:S(2)}, u32[]{:S(2)}) collective-permute-start(bf16[144,512]{1,0:T(8,128)(2,1)S(1)} %get-tuple-element.42), channel_id=1, source_target_pairs={{0,64},{32,96},{64,0},{96,32},{1,65},{33,97},{65,1},{97,33},{2,66}... | collective-permute-start | bytes 442376 | tf_op jit(solution)/shard_map/ppermute | solution.py:362
  27.1 8.1 %collective-permute-start.6 = (bf16[144,512]{1,0:T(8,128)(2,1)S(1)}, bf16[144,512]{1,0:T(8,128)(2,1)S(1)}, u32[]{:S(2)}, u32[]{:S(2)}) collective-permute-start(bf16[144,512]{1,0:T(8,128)(2,1)S(1)} %get-tuple-element.43), channel_id=1, source_target_pairs={{0,96},{32,64},{64,32},{96,0},{1,97},{33,65},{65,33},{97,1},{2,98}... | collective-permute-start | bytes 442376 | tf_op jit(solution)/shard_map/ppermute | solution.py:362
  27.1 9.1 %copy-start.8 = (s32[8,8]{1,0:T(8,128)S(1)}, s32[8,8]{1,0:T(8,128)}, u32[]{:S(2)}) copy-start(s32[8,8]{1,0:T(8,128)} %routes_ref) | copy-start | bytes 772
  27.1 9.1 %copy-start.10 = (f32[8,8]{1,0:T(8,128)S(1)}, f32[8,8]{1,0:T(8,128)}, u32[]{:S(2)}) copy-start(f32[8,8]{1,0:T(8,128)} %gates_ref) | copy-start | bytes 772
  27.1 76.0 %slice-start.1 = ((s8[6291456]{0:T(1024)(128)(4,1)}), s8[4194304]{0:T(1024)(128)(4,1)S(1)}, s32[]{:S(2)}) async-start(s8[6291456]{0:T(1024)(128)(4,1)} %bitcast.25), calls=%async_computation.4 | async-start | bytes 8388608
  27.1 8.1 %collective-permute-start.4 = (bf16[144,512]{1,0:T(8,128)(2,1)S(1)}, bf16[144,512]{1,0:T(8,128)(2,1)S(1)}, u32[]{:S(2)}, u32[]{:S(2)}) collective-permute-start(bf16[144,512]{1,0:T(8,128)(2,1)S(1)} %get-tuple-element.37), channel_id=1, source_target_pairs={{0,32},{32,0},{64,96},{96,64},{1,33},{33,1},{65,97},{97,65},{2,34}... | collective-permute-start | bytes 442376 | tf_op jit(solution)/shard_map/ppermute | solution.py:362
  35.9 1.4 collective-permute-start.7
  37.3 29.5 %copy-start.6 = (bf16[8,4096]{1,0:T(8,128)(2,1)S(1)}, bf16[8,4096]{1,0:T(8,128)(2,1)}, u32[]{:S(2)}) copy-start(bf16[8,4096]{1,0:T(8,128)(2,1)} %residual_ref.1) | copy-start | bytes 196612
  37.3 29.5 %copy-start.7 = (f32[4096]{0:T(1024)S(1)}, f32[4096]{0:T(1024)}, u32[]{:S(2)}) copy-start(f32[4096]{0:T(1024)} %param.21) | copy-start | bytes 49156
  67.4 35.6 %copy-start.4 = (bf16[256,256]{1,0:T(8,128)(2,1)S(1)}, bf16[256,256]{1,0:T(8,128)(2,1)}, u32[]{:S(2)}) copy-start(bf16[256,256]{1,0:T(8,128)(2,1)} %constant.39.clone.perm_ref) | copy-start | bytes 393220
  67.5 35.6 %copy-start.5 = (bf16[256,256]{1,0:T(8,128)(2,1)S(1)}, bf16[256,256]{1,0:T(8,128)(2,1)}, u32[]{:S(2)}) copy-start(bf16[256,256]{1,0:T(8,128)(2,1)} %constant.40.clone.back_ref) | copy-start | bytes 393220
  103.1 4.9 %collective-permute-start.9 = (bf16[64,16,1024]{2,1,0:T(8,128)(2,1)S(1)}, bf16[64,16,1024]{2,1,0:T(8,128)(2,1)S(1)}, u32[]{:S(2)}, u32[]{:S(2)}) collective-permute-start(bf16[64,16,1024]{2,1,0:T(8,128)(2,1)S(1)} %all_to_all.16.rows_ref), channel_id=1, source_target_pairs={{0,32},{32,0},{1,33},{33,1},{2,34},{34,2},{3,35},{35,3},{4,36},{36... | collective-permute-start | bytes 6291464 | tf_op jit(solution)/shard_map/ppermute | solution.py:362
  112.9 4.4 %collective-permute-start.10 = (bf16[64,16,1024]{2,1,0:T(8,128)(2,1)S(1)}, bf16[64,16,1024]{2,1,0:T(8,128)(2,1)S(1)}, u32[]{:S(2)}, u32[]{:S(2)}) collective-permute-start(bf16[64,16,1024]{2,1,0:T(8,128)(2,1)S(1)} %experts.3), channel_id=1, source_target_pairs={{0,32},{32,0},{1,33},{33,1},{2,34},{34,2},{3,35},{35,3},{4,36},{36... | collective-permute-start | bytes 6291464 | tf_op jit(solution)/shard_map/ppermute | solution.py:362
